TPU v7x, 128 devices: a whole 4x4x4 slice. The times are simulated.
128 devices in a mesh: node: 4 (over y), wide: 32 (over x, z, core).
Axes of the slice: x: 4, y: 4, z: 4, core: 2. Of those that a mesh axis runs over, the one named last changes fastest.
Arguments:
- features: bfloat16 [128, 128, 9216], P(('node', 'wide')), may hold values from -6 to 6
- cotangent: bfloat16 [128, 128, 9216], P(('node', 'wide')), may hold values from -6 to 6
- wet_fraction: float32 [128, 9216], P(('node', 'wide')), may hold values from 0 to 1, as said below
- slot_tile: int32 [128], replicated, may hold values from -1 to 255, as said below
- neighbours: int32 [256, 8], replicated, may hold values from -1 to 511, as said below
- kernel: float32 [49, 128], replicated, may hold values from -0.875 to 0.875
- norm_gain: float32 [128], replicated, may hold values from 0.5 to 1.5
- weight_in: bfloat16 [128, 512], replicated, may hold values from -0.5 to 0.5
- bias_in: float32 [512], replicated, may hold values from -3 to 3
- weight_out: bfloat16 [512, 128], replicated, may hold values from -0.25 to 0.25
- layer_scale: float32 [128], replicated, may hold values from 0.5 to 1.5
Outputs:
- updated: bfloat16 [128, 128, 9216], P(('node', 'wide'))
- grad_features: bfloat16 [128, 128, 9216], P(('node', 'wide'))
- grad_weight_in: float32 [128, 512], replicated
- grad_weight_out: float32 [512, 128], replicated
- grad_kernel: float32 [49, 128], replicated
Inputs may be any that keep to these rules, and one draw needn't show every extreme that they name: `slot_tile`: slot (n * 32 + w) + j is slot j of node index n and wide index w; -1 marks an empty slot. Tile id = grid row 32 + grid column; a tile of grid column w is held only by slots of wide index w; every ocean tile is held by exactly one slot and land tiles by none; in some grid column every slot holds a tile. Row t lists the neighbours of tile t in the order N, S, W, E, NW, NE, SW, SE as 2 id + flip, or -1 where there is no ocean tile (all -1 for land tiles). Columns wrap, so neighbours lie in grid columns c - 1, c, c + 1 mod 32; the N neighbour of a tile in the top grid row is the top-row tile of grid column 31 - c with flip 1, the only entries with flip 1. The table is symmetric: B is the S (W, E, NW, NE, SW, SE) neighbour of A exactly when A is the N (E, W, SE, SW, NE, NW) neighbour of B, and flipped N neighbours are mutual. `wet_fraction`: zero in every cell of an empty slot.
All inputs are finite; a program needn't handle non-finite values.
Results may differ from a plain program's by a relative error of at most 0.0077.
Values may be sent and summed in bfloat16 or wider, within the bound.
A program may use at most 192 MiB of HBM per device.

v0:
```python
import math

import jax
import jax.numpy as jnp
from jax import lax
from jax.sharding import PartitionSpec as P

TS = 96
TPD = 1
CELLS = 9216


EPS = 1e-06
GELU_COEF = 0.7978845608028654


def swapped(value, axis, distance):
    mask = 2**distance
    pairs = [(source, source ^ mask) for source in range(lax.axis_size(axis))]
    return lax.ppermute(value, axis, pairs)


def shifted(block, axis, distance):
    devices = range(lax.axis_size(axis))
    route = [((i - distance) % len(devices), i) for i in devices]
    return lax.ppermute(block, axis, route)


def gelu_tanh(values):
    return (
        0.5 * values * (1.0 + jnp.tanh(GELU_COEF * (values + 0.044715 * values * values * values)))
    )


def tile_metric(tile_ids, tile_side, tile_rows, tile_cols):
    grid_row = jnp.maximum(tile_ids, 0) // tile_cols
    cell_row = jnp.arange(tile_side * tile_side, dtype=jnp.int32) // tile_side
    global_row = grid_row[:, None] * tile_side + cell_row[None, :]
    latitude = -80.0 + 160.0 * (global_row.astype(jnp.float32) + 0.5) / float(tile_rows * tile_side)
    return jnp.cos(latitude * (math.pi / 180.0))


def rim_pack(tile_data):
    channels, tile_side = (tile_data.shape[0], tile_data.shape[1])
    return jnp.concatenate(
        [
            tile_data[:, tile_side - 3 :, :].reshape(channels, 3 * tile_side),
            tile_data[:, :3, :].reshape(channels, 3 * tile_side),
            tile_data[:, :, :3].reshape(channels, 3 * tile_side),
            tile_data[:, :, tile_side - 3 :].reshape(channels, 3 * tile_side),
        ],
        axis=1,
    )


def flip_both(strip):
    return strip[:, ::-1, ::-1]


def assemble(tile_data, packs, mirrored, flip_north):
    channels, tile_side = (tile_data.shape[0], tile_data.shape[1])
    strip_len = 3 * tile_side
    north_rims = packs[:, :, 0:strip_len].reshape(8, channels, 3, tile_side)
    south_rims = packs[:, :, strip_len : 2 * strip_len].reshape(8, channels, 3, tile_side)
    west_rims = packs[:, :, 2 * strip_len : 3 * strip_len].reshape(8, channels, tile_side, 3)
    east_rims = packs[:, :, 3 * strip_len :].reshape(8, channels, tile_side, 3)
    north_piece = jnp.where(
        flip_north > 0, flip_both(mirrored.reshape(channels, 3, tile_side)), south_rims[0]
    )
    bottom = jnp.concatenate(
        [north_rims[6][:, :, tile_side - 3 :], north_rims[1], north_rims[7][:, :, :3]], axis=2
    )
    middle = jnp.concatenate([east_rims[2], tile_data, west_rims[3]], axis=2)
    upper_band = jnp.concatenate(
        [south_rims[4][:, :, tile_side - 3 :], north_piece, south_rims[5][:, :, :3]], axis=2
    )
    return jnp.concatenate([bottom, middle, upper_band], axis=1)


def frame_pack(spread):
    channels, wide_side = (spread.shape[0], spread.shape[1])
    tile_side = wide_side - 6
    return jnp.concatenate(
        [
            spread[:, tile_side + 3 :, :].reshape(channels, 3 * wide_side),
            spread[:, :3, :].reshape(channels, 3 * wide_side),
            spread[:, 3 : tile_side + 3, :3].reshape(channels, 3 * tile_side),
            spread[:, 3 : tile_side + 3, tile_side + 3 :].reshape(channels, 3 * tile_side),
        ],
        axis=1,
    ).astype(jnp.bfloat16)


def receive(interior, packs, mirrored, flip_north):
    channels, tile_side = (interior.shape[0], interior.shape[1])
    wide_side = tile_side + 6
    band_len = 3 * wide_side
    strip_len = 3 * tile_side
    rest = tile_side - 3
    upper_bands = packs[:, :, :band_len].reshape(8, channels, 3, wide_side).astype(jnp.float32)
    lower_bands = (
        packs[:, :, band_len : 2 * band_len].reshape(8, channels, 3, wide_side).astype(jnp.float32)
    )
    left_bands = (
        packs[:, :, 2 * band_len : 2 * band_len + strip_len]
        .reshape(8, channels, tile_side, 3)
        .astype(jnp.float32)
    )
    right_bands = (
        packs[:, :, 2 * band_len + strip_len :]
        .reshape(8, channels, tile_side, 3)
        .astype(jnp.float32)
    )
    from_north = jnp.where(
        flip_north > 0,
        flip_both(mirrored.reshape(channels, 3, tile_side).astype(jnp.float32)),
        lower_bands[0][:, :, 3 : tile_side + 3],
    )
    top_rows = (
        from_north
        + jnp.pad(lower_bands[4][:, :, tile_side + 3 :], ((0, 0), (0, 0), (0, rest)))
        + jnp.pad(lower_bands[5][:, :, :3], ((0, 0), (0, 0), (rest, 0)))
    )
    bottom_rows = (
        upper_bands[1][:, :, 3 : tile_side + 3]
        + jnp.pad(upper_bands[6][:, :, tile_side + 3 :], ((0, 0), (0, 0), (0, rest)))
        + jnp.pad(upper_bands[7][:, :, :3], ((0, 0), (0, 0), (rest, 0)))
    )
    return (
        interior
        + jnp.pad(bottom_rows, ((0, 0), (0, rest), (0, 0)))
        + jnp.pad(top_rows, ((0, 0), (rest, 0), (0, 0)))
        + jnp.pad(right_bands[2], ((0, 0), (0, 0), (0, rest)))
        + jnp.pad(left_bands[3], ((0, 0), (0, 0), (rest, 0)))
    )


def flat_padded(padded):
    channels, wide_side = (padded.shape[0], padded.shape[1])
    return jnp.pad(padded.reshape(channels, wide_side * wide_side), ((0, 0), (0, 8)))


def depthwise(padded, kernel):
    channels, wide_side = (padded.shape[0], padded.shape[1])
    tile_side = wide_side - 6
    length = tile_side * wide_side
    flat = flat_padded(padded)
    total = jnp.zeros((channels, length), jnp.float32)
    for row_off in range(7):
        for col_off in range(7):
            start = row_off * wide_side + col_off
            total = total + kernel[7 * row_off + col_off][:, None] * flat[
                :, start : start + length
            ].astype(jnp.float32)
    return total.reshape(channels, tile_side, wide_side)[:, :, :tile_side].reshape(
        channels, tile_side * tile_side
    )


def kernel_grad(padded, grad_source):
    channels, wide_side = (padded.shape[0], padded.shape[1])
    tile_side = wide_side - 6
    length = tile_side * wide_side
    flat = flat_padded(padded)
    grad_wide = jnp.pad(
        grad_source.reshape(channels, tile_side, tile_side), ((0, 0), (0, 0), (0, 6))
    ).reshape(channels, length)
    rows_out = []
    for row_off in range(7):
        for col_off in range(7):
            start = row_off * wide_side + col_off
            rows_out.append(
                jnp.sum(grad_wide * flat[:, start : start + length].astype(jnp.float32), axis=1)
            )
    return jnp.stack(rows_out, axis=0)


def spread_back(grad_bf, kernel):
    channels = grad_bf.shape[0]
    wide_side = TS + 6
    grad_wide = jnp.pad(grad_bf.reshape(channels, TS, TS), ((0, 0), (0, 0), (0, 6))).reshape(
        channels, TS * wide_side
    )
    front = 6 * wide_side + 6
    long_flat = jnp.pad(grad_wide, ((0, 0), (front, 6 * wide_side)))
    total = jnp.zeros((channels, wide_side * wide_side), jnp.float32)
    for row_off in range(7):
        for col_off in range(7):
            start = front - row_off * wide_side - col_off
            total = total + kernel[7 * row_off + col_off][:, None] * long_flat[
                :, start : start + wide_side * wide_side
            ].astype(jnp.float32)
    return total.reshape(channels, wide_side, wide_side)


def block_tile(
    padded,
    tile_x,
    tile_grad,
    wet_row,
    metric_row,
    kernel,
    norm_gain,
    weight_in,
    bias_in,
    weight_out,
    layer_scale,
):
    conv_out = depthwise(padded, kernel) / metric_row[None, :]
    centred = conv_out - jnp.mean(conv_out, axis=0, keepdims=True)
    inv_std = lax.rsqrt(jnp.mean(centred * centred, axis=0, keepdims=True) + EPS)
    normed = centred * inv_std
    normed_bf = (normed * norm_gain[:, None]).astype(jnp.bfloat16)
    hidden = jnp.dot(weight_in.T, normed_bf, preferred_element_type=jnp.float32) + bias_in[:, None]
    active, gelu_back = jax.vjp(gelu_tanh, hidden)
    active_bf = active.astype(jnp.bfloat16)
    mixed = jnp.dot(weight_out.T, active_bf, preferred_element_type=jnp.float32)
    mask_scale = wet_row[None, :] * layer_scale[:, None]
    updated = (tile_x.astype(jnp.float32) + mask_scale * mixed).astype(jnp.bfloat16)
    grad_mixed = (mask_scale * tile_grad.astype(jnp.float32)).astype(jnp.bfloat16)
    grad_w_out = jnp.dot(active_bf, grad_mixed.T, preferred_element_type=jnp.float32)
    grad_active = jnp.dot(weight_out, grad_mixed, preferred_element_type=jnp.float32)
    grad_hidden = gelu_back(grad_active)[0].astype(jnp.bfloat16)
    grad_w_in = jnp.dot(normed_bf, grad_hidden.T, preferred_element_type=jnp.float32)
    grad_normed = (
        jnp.dot(weight_in, grad_hidden, preferred_element_type=jnp.float32) * norm_gain[:, None]
    )
    grad_conv = inv_std * (
        grad_normed
        - jnp.mean(grad_normed, axis=0, keepdims=True)
        - normed * jnp.mean(grad_normed * normed, axis=0, keepdims=True)
    )
    grad_source = grad_conv / metric_row[None, :]
    grad_kern = kernel_grad(padded, grad_source)
    return (updated, grad_source.astype(jnp.bfloat16), grad_w_in, grad_w_out, grad_kern)


def neighbour_packs(main_packs, north_packs):
    bit_count = lax.axis_size("wide").bit_length() - 1
    column_main, column_north = (
        lax.all_gather(main_packs, "node", axis=0, tiled=True),
        lax.all_gather(north_packs, "node", axis=0, tiled=True),
    )
    mirrored = column_north
    for bit_pos in range(bit_count):
        mirrored = swapped(mirrored, "wide", bit_pos)
    from_west = shifted(column_main, "wide", 1)
    from_east = shifted(column_main, "wide", -1)
    return (jnp.concatenate([column_main, from_west, from_east], axis=0), mirrored)


def local(
    features,
    cotangent,
    wet_fraction,
    slot_tile,
    neighbours,
    kernel,
    norm_gain,
    weight_in,
    bias_in,
    weight_out,
    layer_scale,
):
    node_count = lax.axis_size("node")
    wide_count = lax.axis_size("wide")
    slot_count = node_count * wide_count * TPD
    node_index = lax.axis_index("node")
    wide_index = lax.axis_index("wide")
    channels = features.shape[1]
    local_slots = (node_index * wide_count + wide_index) * TPD + jnp.arange(TPD, dtype=jnp.int32)
    my_tiles = jnp.take(slot_tile, local_slots)
    metric = tile_metric(my_tiles, TS, node_count * TPD + 4, wide_count)
    near_table = jnp.where(
        my_tiles[:, None] >= 0, jnp.take(neighbours, jnp.maximum(my_tiles, 0), axis=0), -1
    )
    present = near_table >= 0
    flipped = jnp.where(present, near_table % 2, 0)
    target = jnp.maximum(near_table, 0) // 2
    slot_ids = jnp.arange(slot_count, dtype=jnp.int32)
    owner_slot = jnp.sum(
        jnp.where(slot_tile[None, None, :] == target[:, :, None], slot_ids[None, None, :], 0),
        axis=-1,
    )
    owner_node = owner_slot // (wide_count * TPD)
    owner_wide = owner_slot // TPD % wide_count
    owner_place = owner_slot % TPD
    column_side = jnp.where(
        owner_wide == wide_index,
        0,
        jnp.where(owner_wide == (wide_index + wide_count - 1) % wide_count, 1, 2),
    )
    main_index = column_side * (node_count * TPD) + owner_node * TPD + owner_place
    mirror_index = owner_node[:, 0] * TPD + owner_place[:, 0]
    weight_cells = wet_fraction * metric
    cell_field = (features.astype(jnp.float32) * weight_cells[:, None, :]).astype(jnp.bfloat16)
    tile_fields = cell_field.reshape(TPD, channels, TS, TS)
    main_packs = jax.vmap(rim_pack)(tile_fields)
    north_strips = tile_fields[:, :, TS - 3 :, :].reshape(TPD, channels, 3 * TS)
    candidates, mirrors = neighbour_packs(main_packs, north_strips)
    chosen = jnp.where(
        present[:, :, None, None], candidates[main_index], jnp.zeros((), jnp.bfloat16)
    )
    padded = jax.vmap(assemble)(tile_fields, chosen, mirrors[mirror_index], flipped[:, 0])

    def one_tile(items):
        return block_tile(
            items[0],
            items[1],
            items[2],
            items[3],
            items[4],
            kernel,
            norm_gain,
            weight_in,
            bias_in,
            weight_out,
            layer_scale,
        )

    updated, grad_source_bf, grad_w_in, grad_w_out, grad_kern = lax.map(
        one_tile, (padded, features, cotangent, wet_fraction, metric)
    )

    def spread_one(grad_bf):
        return spread_back(grad_bf, kernel)

    spreads = lax.map(spread_one, grad_source_bf)
    frames = jax.vmap(frame_pack)(spreads)
    mirror_frames = (
        spreads[:, :, TS + 3 :, 3 : TS + 3].reshape(TPD, channels, 3 * TS).astype(jnp.bfloat16)
    )
    back_candidates, back_mirrors = neighbour_packs(frames, mirror_frames)
    back_chosen = jnp.where(
        present[:, :, None, None], back_candidates[main_index], jnp.zeros((), jnp.bfloat16)
    )
    grad_field = jax.vmap(receive)(
        spreads[:, :, 3 : TS + 3, 3 : TS + 3],
        back_chosen,
        back_mirrors[mirror_index],
        flipped[:, 0],
    )
    grad_features = (
        cotangent.astype(jnp.float32)
        + weight_cells[:, None, :] * grad_field.reshape(TPD, channels, CELLS)
    ).astype(jnp.bfloat16)
    totals = lax.psum(
        (jnp.sum(grad_w_in, axis=0), jnp.sum(grad_w_out, axis=0), jnp.sum(grad_kern, axis=0)),
        ("node", "wide"),
    )
    grad_scale = 1.0 / math.sqrt(slot_count * CELLS)
    return (
        updated,
        grad_features,
        totals[0] * grad_scale,
        totals[1] * grad_scale,
        totals[2] * grad_scale,
    )


def solution(mesh):
    in_specs = (
        P(("node", "wide"), None, None),
        P(("node", "wide"), None, None),
        P(("node", "wide"), None),
        P(),
        P(),
        P(),
        P(),
        P(),
        P(),
        P(),
        P(),
    )
    out_specs = (P(("node", "wide"), None, None), P(("node", "wide"), None, None), P(), P(), P())
    return jax.shard_map(local, mesh=mesh, in_specs=in_specs, out_specs=out_specs, check_vma=False)
```

profile of v0, /device:TPU:1, one launch (start us, length us, event | category | flops | bytes accessed | tf_op | source)
XLA Modules:
  0.0 598.3 jit_solution(10572996266494016105)
XLA Ops:
  9.1 4.3 copy.185
  15.3 3.3 fusion.112
  19.8 11.6 %all_gather.13 = bf16[4,128,288]{1,2,0:T(8,128)(2,1)S(1)} all-gather(bf16[1,128,288]{1,2,0:T(8,128)(2,1)S(1)} %bitcast.388), channel_id=1, replica_groups=mesh['node'=4,'wide'=32] {'node'}, dimensions={0}, use_global_device_ids=true | all-gather | bytes 368640 | tf_op jit(solution)/shard_map/all_gather | solution.py:242
  31.4 2.8 collective-permute-start.2
  37.6 6.4 %collective-permute-done.3 = bf16[4,128,288]{1,2,0:T(8,128)(2,1)S(1)} collective-permute-done((bf16[4,128,288]{1,2,0:T(8,128)(2,1)S(1)}, bf16[4,128,288]{1,2,0:T(8,128)(2,1)S(1)}, u32[]{:S(2)}, u32[]{:S(2)}) %collective-permute-start.3) | collective-permute-done | bytes 294944 | tf_op jit(solution)/shard_map/ppermute | solution.py:20
  44.0 3.2 collective-permute-start.4
  49.4 4.3 copy.196
  56.6 7.4 %collective-permute-done.5 = bf16[4,128,288]{1,2,0:T(8,128)(2,1)S(1)} collective-permute-done((bf16[4,128,288]{1,2,0:T(8,128)(2,1)}, bf16[4,128,288]{1,2,0:T(8,128)(2,1)S(1)}, u32[]{:S(2)}, u32[]{:S(2)}) %collective-permute-start.5) | collective-permute-done | bytes 294944 | tf_op jit(solution)/shard_map/ppermute | solution.py:20
  64.0 2.9 collective-permute-start.6
  67.0 4.2 collective-permute-done.6
  71.4 3.5 pad_maximum_fusion.1
  74.8 4.2 gather_fusion
  81.0 2.7 fusion.168
  98.2 7.4 %maximum_maximum_fusion = bf16[1,128,102,102]{1,3,2,0:T(8,128)(2,1)} fusion(bf16[1,128,3,3]{1,3,2,0:T(4,128)(2,1)S(1)} %slice.1177, bf16[1,128,3,96]{1,3,2,0:T(8,128)(2,1)S(1)} %fusion.129, bf16[1,128,3,3]{1,3,2,0:T(4,128)(2,1)S(1)} %slice.1174, bf16[1,128,96,3]{1,3,2,0:T(4,128)(2,1)S(1)} %copy.194, bf16[1,128,96,96]{1,3,2,0:T(8,128)(2,1)S(1)} %bitcast.376, ...), kind=kLoop, calls=%fused_computation.249 | loop fusion | flops 23970816 | bytes 5326848 | tf_op jit(solution)/shard_map/vmap()/concatenate | solution.py:77
  105.5 3.6 reshape.905
  109.6 37.2 %fusion.87 = f32[128,9792]{0,1:T(8,128)} fusion(f32[128]{0:T(128)S(1)} %copy-done.25, f32[128]{0:T(128)S(1)} %copy-done.26, f32[128]{0:T(128)S(1)} %copy-done.28, f32[128]{0:T(128)S(1)} %copy-done.29, f32[128]{0:T(128)S(1)} %copy-done.30, f32[128]{0:T(128)S(1)} %copy-done.31, f32[128]{0:T(128)S(1)} %copy-done.32, f32[128]{0:T(128)S(1)} %copy-done.33, ...), kind=kLoop, calls=%fused_computation.205 | loop fusion | flops 182992896 | bytes 115493376 | tf_op jit(solution)/shard_map/while/body/eval_jaxpr/add | solution.py:152
  146.7 6.2 %reshape.906 = f32[128,96,102]{0,2,1:T(8,128)} reshape(f32[128,9792]{0,1:T(8,128)} %fusion.87) | data formatting | bytes 10027008 | tf_op jit(solution)/shard_map/while/body/eval_jaxpr/reshape | solution.py:155
  153.0 4.9 fusion.122
  157.9 8.0 %multiply_reduce_fusion = (f32[96,96]{1,0:T(8,128)S(1)}, f32[128,96,96]{0,2,1:T(8,128)}) fusion(f32[96,96]{1,0:T(8,128)S(1)} %broadcast_multiply_fusion.2, f32[96,96]{1,0:T(8,128)S(1)} %fusion.136, f32[128,96,102]{0,2,1:T(8,128)} %reshape.906), kind=kLoop, calls=%fused_computation.246 | loop fusion | flops 4709376 | bytes 9547776 | tf_op jit(solution)/shard_map/while/body/eval_jaxpr/reduce_sum | solution.py:211
  166.1 6.9 %fusion.121 = f32[128,9216]{0,1:T(8,128)S(1)} fusion(f32[128,96,96]{0,2,1:T(8,128)} %get-tuple-element.208, f32[9216]{0:T(1024)S(1)} %div.135, f32[9216]{0:T(1024)S(1)} %fusion.144), kind=kLoop, calls=%fused_computation.244 | loop fusion | flops 2359296 | bytes 9510912 | tf_op jit(solution)/shard_map/while/body/eval_jaxpr/sub | solution.py:210
  173.1 12.2 %multiply_convert_fusion = (bf16[512,9216]{0,1:T(8,128)(2,1)}, f32[9216,512]{1,0:T(8,128)}) fusion(f32[512]{0:T(512)S(1)} %copy-done.70, bf16[128,512]{1,0:T(8,128)(2,1)S(1)} %copy-done, f32[128,9216]{0,1:T(8,128)S(1)} %fusion.121, f32[128]{0:T(128)S(1)} %copy-done.15, f32[9216]{0:T(1024)S(1)} %rsqrt.13), kind=kOutput, calls=%fused_computation.21 | convolution fusion | flops 1258684416 | bytes 33200640 | tf_op jit(solution)/shard_map/while/body/eval_jaxpr/dot_general | solution.py:214
  185.3 19.7 %fusion.3 = bf16[512,9216]{0,1:T(8,128)(2,1)S(1)} fusion(f32[9216,512]{1,0:T(8,128)} %get-tuple-element.286, f32[512]{0:T(512)S(1)} %copy-done.70, bf16[512,128]{1,0:T(8,128)(2,1)S(1)} %copy-done.68, bf16[1,128,9216]{1,2,0:T(8,128)(2,1)S(1)} %copy-done.7, f32[128]{0:T(128)S(1)} %copy-done.72, f32[9216]{0:T(1024)S(1)} %bitcast.405), kind=kOutput, calls=%fused_computation.9 | convolution fusion | flops 1330642944 | bytes 30841344 | tf_op jit(solution)/shard_map/while/body/eval_jaxpr/dot_general | solution.py:222
  205.1 7.2 %fusion.120 = (f32[9216]{0:T(1024)S(1)}, f32[9216,128]{1,0:T(8,128)}) fusion(f32[128,9216]{0,1:T(8,128)S(1)} %fusion.121, f32[9216]{0:T(1024)S(1)} %rsqrt.13, f32[128]{0:T(128)S(1)} %copy-done.15, bf16[512,9216]{0,1:T(8,128)(2,1)S(1)} %fusion.3, bf16[128,512]{1,0:T(8,128)(2,1)S(1)} %copy-done), kind=kOutput, calls=%fused_computation.242 | convolution fusion | flops 1212668928 | bytes 19079680 | tf_op jit(solution)/shard_map/while/body/eval_jaxpr/dot_general | solution.py:226
  212.3 3.1 reduce_sum.560
  215.3 10.5 %fusion.162 = (bf16[128,9216]{0,1:T(8,128)(2,1)}, f32[128,9216]{0,1:T(8,128)S(1)}) fusion(f32[9216]{0:T(1024)S(1)} %fusion.144, f32[9216]{0:T(1024)S(1)} %get-tuple-element.289, f32[9216]{0:T(1024)S(1)} %get-tuple-element.290, f32[9216,128]{1,0:T(8,128)} %get-tuple-element.288, f32[9216]{0:T(1024)S(1)} %rsqrt.13, f32[9216]{0:T(1024)S(1)} %div.135, ...), kind=kLoop, calls=%fused_computation.405 | loop fusion | flops 10616832 | bytes 16699392 | tf_op jit(solution)/shard_map/while/body/eval_jaxpr/convert_element_type | solution.py:235
  225.8 2.7 pad.70
  228.5 6.2 %reshape.912 = f32[128,9792]{0,1:T(8,128)} reshape(f32[128,96,102]{0,2,1:T(8,128)} %pad.70) | data formatting | bytes 10027008 | tf_op jit(solution)/shard_map/while/body/eval_jaxpr/reshape | solution.py:167
  234.8 13.3 %fusion.92 = (f32[128]{0:T(128)S(1)}, f32[128]{0:T(128)S(1)}, f32[128]{0:T(128)S(1)}, f32[128]{0:T(128)S(1)}, f32[128]{0:T(128)S(1)}, /*index=5*/f32[128]{0:T(12...) fusion(f32[128,9792]{0,1:T(8,128)} %reshape.912, ...), kind=kLoop, calls=%fused_computation.210 | loop fusion | flops 67680000 | bytes 50144256 | tf_op jit(solution)/shard_map/while/body/eval_jaxpr/reduce_sum | solution.py:173
  248.1 13.2 %fusion.110 = (f32[128]{0:T(128)S(1)}, f32[128]{0:T(128)S(1)}, f32[128]{0:T(128)S(1)}, f32[128]{0:T(128)S(1)}, f32[128]{0:T(128)S(1)}, /*index=5*/f32[128]{0:T(1...) fusion(f32[128,9792]{0,1:T(8,128)S(1)} %copy-done.3, ...), kind=kLoop, calls=%fused_computation.228 | loop fusion | flops 67680000 | bytes 37768192 | tf_op jit(solution)/shard_map/while/body/eval_jaxpr/reduce_sum | solution.py:173
  263.2 4.9 reshape.909
  268.2 82.5 %multiply_add_fusion.2 = f32[128,10404]{0,1:T(8,128)} fusion(f32[128]{0:T(128)S(1)} %copy-done.25, f32[128]{0:T(128)S(1)} %copy-done.26, f32[128]{0:T(128)S(1)} %copy-done.28, f32[128]{0:T(128)S(1)} %copy-done.29, f32[128]{0:T(128)S(1)} %copy-done.30, f32[128]{0:T(128)S(1)} %copy-done.31, f32[128]{0:T(128)S(1)} %copy-done.32, f32[128]{0:T(128)S(1)} %copy-done.33, ...), kind=kLoop, calls=%fused_computation.131 | loop fusion | flops 194429952 | bytes 7858688 | tf_op jit(solution)/shard_map/while/body/eval_jaxpr/add | solution.py:190
  350.7 6.6 %broadcast_in_dim.154 = f32[1,128,102,102]{1,3,2,0:T(8,128)} reshape(f32[128,10404]{0,1:T(8,128)} %multiply_add_fusion.2) | data formatting | bytes 10653696 | tf_op jit(solution)/shard_map/while/body/jit(dynamic_update_index_in_dim)/broadcast_in_dim | solution.py:328
  357.3 2.9 convert.30
  360.5 4.9 concatenate.51
  365.5 9.6 %all_gather.15 = bf16[4,128,288]{1,2,0:T(8,128)(2,1)S(1)} all-gather(bf16[1,128,288]{1,2,0:T(8,128)(2,1)S(1)} %bitcast.400), channel_id=1, replica_groups=mesh['node'=4,'wide'=32] {'node'}, dimensions={0}, use_global_device_ids=true | all-gather | bytes 368640 | tf_op jit(solution)/shard_map/all_gather | solution.py:242
  375.1 17.6 %collective-permute-start.9 = (bf16[4,128,288]{1,2,0:T(8,128)(2,1)S(1)}, bf16[4,128,288]{1,2,0:T(8,128)(2,1)S(1)}, u32[]{:S(2)}, u32[]{:S(2)}) collective-permute-start(bf16[4,128,288]{1,2,0:T(8,128)(2,1)S(1)} %all_gather.15), channel_id=1, source_target_pairs={{0,1},{1,0},{2,3},{3,2},{4,5},{5,4},{6,7},{7,6},{8,9},{9,8},{10,11... | collective-permute-start | bytes 884744 | tf_op jit(solution)/shard_map/ppermute | solution.py:20
  392.7 10.0 %fusion.51 = (f32[128]{0:T(128)S(1)}, f32[128]{0:T(128)S(1)}, f32[128]{0:T(128)S(1)}, f32[128]{0:T(128)S(1)}, f32[128]{0:T(128)S(1)}, /*index=5*/f32[128]{0:T(12...) fusion(f32[128,9792]{0,1:T(8,128)} %reshape.912, ...), kind=kLoop, calls=%fused_computation.169 | loop fusion | flops 48880000 | bytes 37607936 | tf_op jit(solution)/shard_map/while/body/eval_jaxpr/reduce_sum | solution.py:173
  403.0 5.0 fusion.123
  408.0 3.1 collective-permute-done.10
  411.1 7.1 %fusion.160 = f32[128,512]{1,0:T(8,128)} fusion(bf16[512,9216]{0,1:T(8,128)(2,1)} %copy-done.2, f32[128,9216]{0,1:T(8,128)S(1)} %bitcast.370, f32[128]{0:T(128)S(1)} %copy-done.15, f32[9216]{0:T(1024)S(1)} %rsqrt.13), kind=kOutput, calls=%fused_computation.403 | convolution fusion | flops 1211498496 | bytes 14455296 | tf_op jit(solution)/shard_map/while/body/eval_jaxpr/dot_general | solution.py:224
  419.9 6.3 %copy.197 = bf16[4,128,1188]{1,0,2:T(4,128)(2,1)} copy(bf16[4,128,1188]{1,2,0:T(8,128)(2,1)} %all-gather.5.cloned.1.call-done) | data formatting | bytes 2433024 | tf_op jit(solution)/shard_map/all_gather | solution.py:241
  428.8 7.5 %fusion.13 = bf16[1,128,9216]{1,2,0:T(8,128)(2,1)} fusion(bf16[512,9216]{0,1:T(8,128)(2,1)} %get-tuple-element.285, bf16[512,128]{1,0:T(8,128)(2,1)S(1)} %copy-done.69, bf16[1,128,9216]{1,2,0:T(8,128)(2,1)S(1)} %copy-done.5, f32[128]{0:T(128)S(1)} %copy-done.73, f32[9216]{0:T(1024)S(1)} %bitcast.407), kind=kOutput, calls=%fused_computation.27 | convolution fusion | flops 1213857792 | bytes 14324224 | tf_op jit(solution)/shard_map/while/body/eval_jaxpr/dot_general | solution.py:217
  436.2 4.4 copy.210
  440.8 68.8 %psum.23 = f32[49,128]{1,0:T(8,128)S(1)} all-reduce(f32[49,128]{1,0:T(8,128)S(1)} %stack.249), channel_id=1, replica_groups=mesh['node'=4,'wide'=32] {'node','wide'}, use_global_device_ids=true, to_apply=%region_56.57 | all-reduce | flops 6272 | bytes 50176 | tf_op jit(solution)/shard_map/psum | solution.py:347
  511.4 56.4 %all-reduce.15.cloned.1.call-done = (f32[128,512]{1,0:T(8,128)}, f32[512,128]{1,0:T(8,128)}) async-done(((f32[128,512]{1,0:T(8,128)}, f32[512,128]{1,0:T(8,128)}), (f32[128,512]{1,0:T(8,128)}, f32[512,128]{1,0:T(8,128)})) %all-reduce.15.cloned.1.call-update) | async-done | bytes 524304 | tf_op jit(solution)/shard_map/psum | solution.py:347
  574.2 2.5 pad_maximum_fusion
  576.8 3.2 gather_fusion.1
  580.0 4.5 bitcast_select_fusion
  (279 shorter events, 51.3 us)
Async XLA Ops:
  7.2 165.8 %copy-start = (bf16[128,512]{1,0:T(8,128)(2,1)S(1)}, bf16[128,512]{1,0:T(8,128)(2,1)}, u32[]{:S(2)}) copy-start(bf16[128,512]{1,0:T(8,128)(2,1)} %param.18) | copy-start | bytes 393220
  7.2 40.1 %all-gather.3.cloned.1.call-start = ((), (), s32[]{:S(2)}) async-start(), calls=%async_computation | async-start | bytes 1474560 | tf_op jit(solution)/shard_map/all_gather | solution.py:241
  13.4 20.7 %copy-start.67 = (s32[256,8]{0,1:T(8,128)S(1)}, s32[256,8]{0,1:T(8,128)}, u32[]{:S(2)}) copy-start(s32[256,8]{0,1:T(8,128)} %param.15) | copy-start | bytes 24580
  13.4 20.9 %copy-start.71 = (s32[128]{0:T(128)S(1)}, s32[128]{0:T(128)}, u32[]{:S(2)}) copy-start(s32[128]{0:T(128)} %param.14) | copy-start | bytes 1540
  13.4 23.6 %copy-start.14 = (f32[49,128]{1,0:T(8,128)S(1)}, f32[49,128]{1,0:T(8,128)}, u32[]{:S(2)}) copy-start(f32[49,128]{1,0:T(8,128)} %param.16) | copy-start | bytes 75268
  19.7 400.2 %all-gather.5.cloned.1.call-start = ((), (), s32[]{:S(2)}) async-start(), calls=%async_computation.1 | async-start | bytes 1525760 | tf_op jit(solution)/shard_map/all_gather | solution.py:241
  31.4 4.0 collective-permute-start.2
  34.5 44.5 %copy-start.65 = (pred[8]{0:T(512)(128)(4,1)}, pred[8]{0:T(512)(128)(4,1)S(1)}, u32[]{:S(2)}) copy-start(pred[8]{0:T(512)(128)(4,1)S(1)} %compare_bitcast_fusion) | copy-start | bytes 28
  35.3 8.7 %collective-permute-start.3 = (bf16[4,128,288]{1,2,0:T(8,128)(2,1)S(1)}, bf16[4,128,288]{1,2,0:T(8,128)(2,1)S(1)}, u32[]{:S(2)}, u32[]{:S(2)}) collective-permute-start(bf16[4,128,288]{1,2,0:T(8,128)(2,1)S(1)} %collective-permute-done.2), channel_id=1, source_target_pairs={{0,2},{1,3},{2,0},{3,1},{4,6},{5,7},{6,4},{7,5},{8,10},{9,11},{10,... | collective-permute-start | bytes 884744 | tf_op jit(solution)/shard_map/ppermute | solution.py:20
  44.0 10.4 %collective-permute-start.4 = (bf16[4,128,288]{1,2,0:T(8,128)(2,1)S(1)}, bf16[4,128,288]{1,2,0:T(8,128)(2,1)}, u32[]{:S(2)}, u32[]{:S(2)}) collective-permute-start(bf16[4,128,288]{1,2,0:T(8,128)(2,1)S(1)} %collective-permute-done.3), channel_id=1, source_target_pairs={{0,4},{1,5},{2,6},{3,7},{4,0},{5,1},{6,2},{7,3},{8,12},{9,13},{10,... | collective-permute-start | bytes 884744 | tf_op jit(solution)/shard_map/ppermute | solution.py:20
  47.3 24.1 %collective-permute-start.1 = (bf16[4,128,1152]{2,1,0:T(8,128)(2,1)}, bf16[4,128,1152]{2,1,0:T(8,128)(2,1)}, u32[]{:S(2)}, u32[]{:S(2)}) collective-permute-start(bf16[4,128,1152]{2,1,0:T(8,128)(2,1)} %all-gather.3.cloned.1.call-done), channel_id=1, source_target_pairs={{1,0},{2,1},{3,2},{4,3},{5,4},{6,5},{7,6},{8,7},{9,8},{10,9},{11,1... | collective-permute-start | bytes 3538952 | tf_op jit(solution)/shard_map/ppermute | solution.py:26
  48.6 22.7 %collective-permute-start = (bf16[4,128,1152]{2,1,0:T(8,128)(2,1)}, bf16[4,128,1152]{2,1,0:T(8,128)(2,1)}, u32[]{:S(2)}, u32[]{:S(2)}) collective-permute-start(bf16[4,128,1152]{2,1,0:T(8,128)(2,1)} %all-gather.3.cloned.1.call-done), channel_id=1, source_target_pairs={{31,0},{0,1},{1,2},{2,3},{3,4},{4,5},{5,6},{6,7},{7,8},{8,9},{9,10... | collective-permute-start | bytes 3538952 | tf_op jit(solution)/shard_map/ppermute | solution.py:26
  54.5 9.6 %collective-permute-start.5 = (bf16[4,128,288]{1,2,0:T(8,128)(2,1)}, bf16[4,128,288]{1,2,0:T(8,128)(2,1)S(1)}, u32[]{:S(2)}, u32[]{:S(2)}) collective-permute-start(bf16[4,128,288]{1,2,0:T(8,128)(2,1)} %collective-permute-done.4), channel_id=1, source_target_pairs={{0,8},{1,9},{2,10},{3,11},{4,12},{5,13},{6,14},{7,15},{8,0},{9,1},... | collective-permute-start | bytes 884744 | tf_op jit(solution)/shard_map/ppermute | solution.py:20
  64.0 7.2 %collective-permute-start.6 = (bf16[4,128,288]{1,2,0:T(8,128)(2,1)S(1)}, bf16[4,128,288]{1,2,0:T(8,128)(2,1)S(1)}, u32[]{:S(2)}, u32[]{:S(2)}) collective-permute-start(bf16[4,128,288]{1,2,0:T(8,128)(2,1)S(1)} %collective-permute-done.5), channel_id=1, source_target_pairs={{0,16},{1,17},{2,18},{3,19},{4,20},{5,21},{6,22},{7,23},{8,24},{9,... | collective-permute-start | bytes 884744 | tf_op jit(solution)/shard_map/ppermute | solution.py:20
  66.9 12.2 %copy-start.16 = (s32[1024]{0:T(1024)}, s32[1024]{0:T(1024)S(1)}, u32[]{:S(2)}) copy-start(s32[1024]{0:T(1024)S(1)} %pad_clamp_fusion) | copy-start | bytes 12292
  97.8 11.4 %copy-start.17 = (f32[128]{0:T(128)S(1)}, f32[128]{0:T(128)}, u32[]{:S(2)}) copy-start(f32[128]{0:T(128)} %get-tuple-element.275) | copy-start | bytes 1540
  97.8 11.4 %copy-start.18 = (f32[128]{0:T(128)S(1)}, f32[128]{0:T(128)}, u32[]{:S(2)}) copy-start(f32[128]{0:T(128)} %get-tuple-element.276) | copy-start | bytes 1540
  97.8 11.4 %copy-start.19 = (f32[128]{0:T(128)S(1)}, f32[128]{0:T(128)}, u32[]{:S(2)}) copy-start(f32[128]{0:T(128)} %get-tuple-element.277) | copy-start | bytes 1540
  97.8 11.4 %copy-start.20 = (f32[128]{0:T(128)S(1)}, f32[128]{0:T(128)}, u32[]{:S(2)}) copy-start(f32[128]{0:T(128)} %get-tuple-element.278) | copy-start | bytes 1540
  97.8 11.4 %copy-start.21 = (f32[128]{0:T(128)S(1)}, f32[128]{0:T(128)}, u32[]{:S(2)}) copy-start(f32[128]{0:T(128)} %get-tuple-element.279) | copy-start | bytes 1540
  97.8 11.4 %copy-start.22 = (f32[128]{0:T(128)S(1)}, f32[128]{0:T(128)}, u32[]{:S(2)}) copy-start(f32[128]{0:T(128)} %get-tuple-element.280) | copy-start | bytes 1540
  97.8 11.4 %copy-start.23 = (f32[128]{0:T(128)S(1)}, f32[128]{0:T(128)}, u32[]{:S(2)}) copy-start(f32[128]{0:T(128)} %get-tuple-element.281) | copy-start | bytes 1540
  97.8 11.4 %copy-start.24 = (f32[128]{0:T(128)S(1)}, f32[128]{0:T(128)}, u32[]{:S(2)}) copy-start(f32[128]{0:T(128)} %get-tuple-element.282) | copy-start | bytes 1540
  97.8 11.4 %copy-start.25 = (f32[128]{0:T(128)S(1)}, f32[128]{0:T(128)}, u32[]{:S(2)}) copy-start(f32[128]{0:T(128)} %get-tuple-element.283) | copy-start | bytes 1540
  97.9 11.4 %copy-start.26 = (f32[128]{0:T(128)S(1)}, f32[128]{0:T(128)}, u32[]{:S(2)}) copy-start(f32[128]{0:T(128)} %get-tuple-element.284) | copy-start | bytes 1540
  173.0 32.0 %copy-start.4 = (f32[128,9216]{0,1:T(8,128)}, f32[128,9216]{0,1:T(8,128)S(1)}, u32[]{:S(2)}) copy-start(f32[128,9216]{0,1:T(8,128)S(1)} %fusion.121) | copy-start | bytes 14155780
  173.0 12.3 %copy-start.7 = (bf16[1,128,9216]{1,2,0:T(8,128)(2,1)S(1)}, bf16[1,128,9216]{1,2,0:T(8,128)(2,1)}, u32[]{:S(2)}) copy-start(bf16[1,128,9216]{1,2,0:T(8,128)(2,1)} %copy.196) | copy-start | bytes 7077892
  173.1 12.3 %copy-start.13 = (f32[1,9216]{1,0:T(1,128)S(1)}, f32[1,9216]{1,0:T(1,128)}, u32[]{:S(2)}) copy-start(f32[1,9216]{1,0:T(1,128)} %param.13) | copy-start | bytes 110596
  173.1 12.2 %copy-start.68 = (bf16[512,128]{1,0:T(8,128)(2,1)S(1)}, bf16[512,128]{1,0:T(8,128)(2,1)}, u32[]{:S(2)}) copy-start(bf16[512,128]{1,0:T(8,128)(2,1)} %param.20) | copy-start | bytes 393220
  173.1 12.2 %copy-start.72 = (f32[128]{0:T(128)S(1)}, f32[128]{0:T(128)}, u32[]{:S(2)}) copy-start(f32[128]{0:T(128)} %param.21) | copy-start | bytes 1540
  234.8 13.3 %copy-start.3 = (f32[128,9792]{0,1:T(8,128)S(1)}, f32[128,9792]{0,1:T(8,128)}, u32[]{:S(2)}) copy-start(f32[128,9792]{0,1:T(8,128)} %reshape.912) | copy-start | bytes 15040516
  248.1 13.4 %copy-start.6 = (bf16[128,9216]{0,1:T(8,128)(2,1)S(1)}, bf16[128,9216]{0,1:T(8,128)(2,1)}, u32[]{:S(2)}) copy-start(bf16[128,9216]{0,1:T(8,128)(2,1)} %get-tuple-element.203) | copy-start | bytes 7077892
  365.5 202.3 %all-reduce.15.cloned.1.call-start = ((), (), s32[]{:S(2)}) async-start(), calls=%async_computation.2 | async-start | bytes 1048576 | tf_op jit(solution)/shard_map/psum | solution.py:347
  365.5 37.5 %slice-start.4 = ((s8[9437184]{0:T(1024)(128)(4,1)}), s8[4194304]{0:T(1024)(128)(4,1)S(1)}, s32[]{:S(2)}) async-start(s8[9437184]{0:T(1024)(128)(4,1)} %bitcast.461), calls=%async_computation.7 | async-start | bytes 8388608
  375.1 27.9 %copy-start.8 = (bf16[1,128,9216]{1,2,0:T(8,128)(2,1)S(1)}, bf16[1,128,9216]{1,2,0:T(8,128)(2,1)}, u32[]{:S(2)}) copy-start(bf16[1,128,9216]{1,2,0:T(8,128)(2,1)} %copy.196) | copy-start | bytes 7077892
  375.1 27.9 %slice-start.5 = ((s8[9437184]{0:T(1024)(128)(4,1)}), s8[4194304]{0:T(1024)(128)(4,1)S(1)}, s32[]{:S(2)}) async-start(s8[9437184]{0:T(1024)(128)(4,1)} %bitcast.461), calls=%async_computation.8 | async-start | bytes 8388608
  375.1 27.9 %slice-start.6 = ((s8[9437184]{0:T(1024)(128)(4,1)}), s8[1048576]{0:T(1024)(128)(4,1)S(1)}, s32[]{:S(2)}) async-start(s8[9437184]{0:T(1024)(128)(4,1)} %bitcast.461), calls=%async_computation.9 | async-start | bytes 2097152
  375.1 27.6 %collective-permute-start.9 = (bf16[4,128,288]{1,2,0:T(8,128)(2,1)S(1)}, bf16[4,128,288]{1,2,0:T(8,128)(2,1)S(1)}, u32[]{:S(2)}, u32[]{:S(2)}) collective-permute-start(bf16[4,128,288]{1,2,0:T(8,128)(2,1)S(1)} %all_gather.15), channel_id=1, source_target_pairs={{0,1},{1,0},{2,3},{3,2},{4,5},{5,4},{6,7},{7,6},{8,9},{9,8},{10,11... | collective-permute-start | bytes 884744 | tf_op jit(solution)/shard_map/ppermute | solution.py:20
  402.7 8.4 %collective-permute-start.10 = (bf16[4,128,288]{1,2,0:T(8,128)(2,1)S(1)}, bf16[4,128,288]{1,2,0:T(8,128)(2,1)}, u32[]{:S(2)}, u32[]{:S(2)}) collective-permute-start(bf16[4,128,288]{1,2,0:T(8,128)(2,1)S(1)} %collective-permute-done.9), channel_id=1, source_target_pairs={{0,2},{1,3},{2,0},{3,1},{4,6},{5,7},{6,4},{7,5},{8,10},{9,11},{10,... | collective-permute-start | bytes 884744 | tf_op jit(solution)/shard_map/ppermute | solution.py:20
  408.0 20.8 %copy-start.5 = (bf16[1,128,9216]{1,2,0:T(8,128)(2,1)S(1)}, bf16[1,128,9216]{1,2,0:T(8,128)(2,1)}, u32[]{:S(2)}) copy-start(bf16[1,128,9216]{1,2,0:T(8,128)(2,1)} %copy.185) | copy-start | bytes 7077892
  408.0 20.8 %copy-start.69 = (bf16[512,128]{1,0:T(8,128)(2,1)S(1)}, bf16[512,128]{1,0:T(8,128)(2,1)}, u32[]{:S(2)}) copy-start(bf16[512,128]{1,0:T(8,128)(2,1)} %param.20) | copy-start | bytes 393220
  408.0 20.8 %copy-start.73 = (f32[128]{0:T(128)S(1)}, f32[128]{0:T(128)}, u32[]{:S(2)}) copy-start(f32[128]{0:T(128)} %param.21) | copy-start | bytes 1540
  411.1 8.8 %collective-permute-start.11 = (bf16[4,128,288]{1,2,0:T(8,128)(2,1)}, bf16[4,128,288]{1,2,0:T(8,128)(2,1)S(1)}, u32[]{:S(2)}, u32[]{:S(2)}) collective-permute-start(bf16[4,128,288]{1,2,0:T(8,128)(2,1)} %collective-permute-done.10), channel_id=1, source_target_pairs={{0,4},{1,5},{2,6},{3,7},{4,0},{5,1},{6,2},{7,3},{8,12},{9,13},{10,... | collective-permute-start | bytes 884744 | tf_op jit(solution)/shard_map/ppermute | solution.py:20
  419.9 90.2 %collective-permute-start.12 = (bf16[4,128,288]{1,2,0:T(8,128)(2,1)S(1)}, bf16[4,128,288]{1,2,0:T(8,128)(2,1)S(1)}, u32[]{:S(2)}, u32[]{:S(2)}) collective-permute-start(bf16[4,128,288]{1,2,0:T(8,128)(2,1)S(1)} %collective-permute-done.11), channel_id=1, source_target_pairs={{0,8},{1,9},{2,10},{3,11},{4,12},{5,13},{6,14},{7,15},{8,0},{9,1},... | collective-permute-start | bytes 884744 | tf_op jit(solution)/shard_map/ppermute | solution.py:20
  426.2 145.1 %collective-permute-start.8 = (bf16[4,128,1188]{1,0,2:T(4,128)(2,1)}, bf16[4,128,1188]{1,0,2:T(4,128)(2,1)}, u32[]{:S(2)}, u32[]{:S(2)}) collective-permute-start(bf16[4,128,1188]{1,0,2:T(4,128)(2,1)} %copy.197), channel_id=1, source_target_pairs={{1,0},{2,1},{3,2},{4,3},{5,4},{6,5},{7,6},{8,7},{9,8},{10,9},{11,1... | collective-permute-start | bytes 3649544 | tf_op jit(solution)/shard_map/ppermute | solution.py:26
  428.6 144.2 %collective-permute-start.7 = (bf16[4,128,1188]{1,0,2:T(4,128)(2,1)}, bf16[4,128,1188]{1,0,2:T(4,128)(2,1)}, u32[]{:S(2)}, u32[]{:S(2)}) collective-permute-start(bf16[4,128,1188]{1,0,2:T(4,128)(2,1)} %copy.197), channel_id=1, source_target_pairs={{31,0},{0,1},{1,2},{2,3},{3,4},{4,5},{5,6},{6,7},{7,8},{8,9},{9,10... | collective-permute-start | bytes 3649544 | tf_op jit(solution)/shard_map/ppermute | solution.py:26
  436.2 138.0 %copy-start.10 = (bf16[4,128,1188]{1,2,0:T(8,128)(2,1)S(1)}, bf16[4,128,1188]{1,2,0:T(8,128)(2,1)}, u32[]{:S(2)}) copy-start(bf16[4,128,1188]{1,2,0:T(8,128)(2,1)} %all-gather.5.cloned.1.call-done) | copy-start | bytes 3649540
  510.2 61.0 %collective-permute-start.13 = (bf16[4,128,288]{1,2,0:T(8,128)(2,1)S(1)}, bf16[4,128,288]{1,2,0:T(8,128)(2,1)S(1)}, u32[]{:S(2)}, u32[]{:S(2)}) collective-permute-start(bf16[4,128,288]{1,2,0:T(8,128)(2,1)S(1)} %collective-permute-done.12), channel_id=1, source_target_pairs={{0,16},{1,17},{2,18},{3,19},{4,20},{5,21},{6,22},{7,23},{8,24},{9,... | collective-permute-start | bytes 884744 | tf_op jit(solution)/shard_map/ppermute | solution.py:20
  (50 other events, 454.1 us)
Sparse Core Ops, SparseCore 0:
  19.9 26.6 all-gather.2
  365.6 35.4 all-gather.4
  418.4 149.3 all-reduce.14
where the time goes:
time: 605 us; the launch traced here: 598 us
  other arithmetic  226 us (37%)
  local copies, waits for them, and re-layouts  91.7 us (15%)
  blocking collectives  89.9 us (15%)
  waiting for transfers between devices  80.1 us (13%)
  matrix products  58.7 us (10%)
  starting transfers between devices  35.5 us (6%)
  between operations  16.4 us (3%)
    add x1, other arithmetic, spread_back(): total + kernel[7 * row_off + col_off][:, None] * long_flat[:, start:start...  82.5 us
    psum x1, blocking collectives, local(): lax.psum((jnp.sum(grad_w_in, axis=0), jnp.sum(grad_w_out, axis=0), jnp.su...  68.8 us
    psum x1, waiting for transfers between devices, local(): lax.psum((jnp.sum(grad_w_in, axis=0), jnp.sum(grad_w_out, axis=0), jnp.su...  56.4 us
    add x1, other arithmetic, depthwise(): total + kernel[7 * row_off + col_off][:, None] * flat[:, start:start + le...  37.2 us
    reduce_sum x3, other arithmetic, kernel_grad(): jnp.sum(grad_wide * flat[:, start:start + length].astype(jnp.float32), ax...  36.6 us
    ppermute x10, starting transfers between devices, swapped(): return lax.ppermute(value, axis, pairs)  30.8 us
    ppermute x10, waiting for transfers between devices, swapped(): return lax.ppermute(value, axis, pairs)  23.6 us
    all_gather x2, blocking collectives, neighbour_packs(): lax.all_gather(north_packs, 'node', axis=0, tiled=True)  21.2 us
  transfers between devices with their start and end apart: 17, of which 7 were waited for; matrix products, arithmetic and copies ran while one was open for 9% of the time, Pallas kernels for 0%

commit v1 on v0

v1 whole, which is shorter than its diff:
```python
import math

import jax
import jax.numpy as jnp
from jax import lax
from jax.experimental import pallas as pl
from jax.experimental.pallas import tpu as pltpu
from jax.sharding import PartitionSpec as P

C = 128
HID = 512
TS = 96
CELLS = TS * TS
NODE = 4
WIDE = 32
PITCH = 112
PADROWS = TS + 6
STRIP = 3 * TS
BAND = 3 * PITCH
BLOCK = 768
CHUNK = 256
EPS = 1e-06
GELU_COEF = 0.7978845608028654
CUBIC = 0.044715
GRAD_SCALE = 1.0 / math.sqrt(NODE * WIDE * CELLS)
MESH = pl.DeviceIdType.MESH
F32 = jnp.float32
BF16 = jnp.bfloat16
VMEM_LIMIT = 60 * 2**20


def border_peers(n, w):
    out = []
    for k in range(1, 4):
        out.append((k - 1, k - 1, (lax.rem(n + k, 4), w)))
    sides = ((3, 3, lax.rem(w + 31, 32)), (7, 4, lax.rem(w + 1, 32)), (11, 5, 31 - w))
    for base, source, column in sides:
        for k in range(4):
            out.append((base + k, source, (lax.rem(n + k, 4), column)))
    return out


def broadcast_taps(k49, kb):
    for t in range(49):
        kb[t] = jnp.broadcast_to(k49[t : t + 1, :], (8, C))


def taps_loop(src, kb, out, flip):
    def body(it, carry):
        i0 = (it // 6) * 4
        j0 = lax.rem(it, 6) * 16
        acc = [[None, None] for _ in range(4)]
        for b in range(7):
            for r in range(10):
                for h in range(2):
                    v = src[pl.ds((i0 + r) * PITCH + j0 + 5 + b + 8 * h, 8), :]
                    for a in range(7):
                        d = r - a
                        if 0 <= d < 4:
                            t = 48 - (7 * a + b) if flip else 7 * a + b
                            p = kb[t] * v
                            acc[d][h] = p if acc[d][h] is None else acc[d][h] + p
        for d in range(4):
            for h in range(2):
                o = pl.multiple_of((i0 + d) * TS + j0 + 8 * h, 8)
                out[pl.ds(o, 8), :] = acc[d][h]
        return carry

    lax.fori_loop(0, 144, body, 0)


def clear_margins(pad):
    zero8 = jnp.zeros((8, C), F32)
    zero_row = jnp.zeros((PITCH, C), F32)
    for r in (0, 1, 2, 99, 100, 101):
        pad[r * PITCH : (r + 1) * PITCH, :] = zero_row

    def body(i, carry):
        o = pl.multiple_of((i + 3) * PITCH, 8)
        pad[pl.ds(o, 8), :] = zero8
        pad[pl.ds(o + 104, 8), :] = zero8
        return carry

    lax.fori_loop(0, TS, body, 0)


def halo_kernel(feat, wc, k49, north_of, conv0, pad, got, strips, kb, send_sem, recv_sem):
    n = lax.axis_index("node")
    w = lax.axis_index("wide")
    peers = border_peers(n, w)
    barrier = pltpu.get_barrier_semaphore()
    for _, _, device in peers:
        pl.semaphore_signal(barrier, inc=1, device_id=device, device_id_type=MESH)

    broadcast_taps(k49, kb)
    clear_margins(pad)

    def prep(g, carry):
        o = pl.multiple_of(g * 384, 128)
        x = feat[:, pl.ds(o, 384)].astype(F32) * wc[:, pl.ds(o, 384)]
        t = x.astype(BF16).astype(F32).T
        for r in range(4):
            row = pl.multiple_of((g * 4 + r + 3) * PITCH + 8, 8)
            pad[pl.ds(row, TS), :] = t[r * TS : (r + 1) * TS]
        return carry

    lax.fori_loop(0, 24, prep, 0)
    for q in range(3):
        here = pl.ds(q * TS, TS)
        strips[3, here, :] = pad[pl.ds(3 * PITCH + 8 + q, TS, stride=PITCH), :].astype(BF16)
        strips[4, here, :] = pad[pl.ds(3 * PITCH + 101 + q, TS, stride=PITCH), :].astype(BF16)
        south = pad[pl.ds((3 + q) * PITCH + 8, TS), :]
        north = pad[pl.ds((96 + q) * PITCH + 8, TS), :]
        strips[5, here, :] = north.astype(BF16)
        for k in range(3):
            mine = jnp.where(north_of[k : k + 1, :] > 0.0, south, north)
            strips[k, here, :] = mine.astype(BF16)

    pl.semaphore_wait(barrier, len(peers))
    copies = []
    for slot, source, device in peers:
        copy = pltpu.make_async_remote_copy(
            src_ref=strips.at[source],
            dst_ref=got.at[slot],
            send_sem=send_sem.at[slot],
            recv_sem=recv_sem.at[slot],
            device_id=device,
            device_id_type=MESH,
        )
        copy.start()
        copies.append(copy)

    taps_loop(pad, kb, conv0, False)
    for copy in copies:
        copy.wait()


def halo_call(feat, wc, k49, north_of):
    vmem = pl.BlockSpec(memory_space=pltpu.VMEM)
    return pl.pallas_call(
        halo_kernel,
        out_shape=(
            jax.ShapeDtypeStruct((CELLS, C), F32),
            jax.ShapeDtypeStruct((PADROWS * PITCH, C), F32),
            jax.ShapeDtypeStruct((15, STRIP, C), BF16),
        ),
        in_specs=[vmem] * 4,
        out_specs=(vmem, vmem, vmem),
        scratch_shapes=[
            pltpu.VMEM((6, STRIP, C), BF16),
            pltpu.VMEM((49, 8, C), F32),
            pltpu.SemaphoreType.DMA((15,)),
            pltpu.SemaphoreType.DMA((15,)),
        ],
        compiler_params=pltpu.CompilerParams(
            collective_id=0, has_side_effects=True, vmem_limit_bytes=VMEM_LIMIT
        ),
        name="halo",
    )(feat, wc, k49, north_of)


def nt(a, b):
    return lax.dot_general(a, b, (((1,), (1,)), ((), ())), preferred_element_type=F32)


def mm(a, b):
    return jnp.dot(a, b, preferred_element_type=F32)


def wide2(column):
    return jnp.concatenate([column, column], axis=1)


def mlp_kernel(
    pick, got, conv0, feat, cot, wet, rmet, k49, gain, w_in_t, w_in, bias, w_out_t, w_out, scale,
    updated, gsrc, gwi, gwo, hw, he, hs, hn,
    cv, kb, strip,
):
    step = pl.program_id(0)

    @pl.when(step == 0)
    def _():
        broadcast_taps(k49, kb)
        gwi[...] = jnp.zeros_like(gwi)
        gwo[...] = jnp.zeros_like(gwo)
        hw[...] = jnp.zeros_like(hw)
        he[...] = jnp.zeros_like(he)

        def chosen(direction, q):
            v = got[pick[direction], pl.ds(q * TS, TS), :].astype(F32)
            return jnp.where(pick[8 + direction] > 0, v, 0.0)

        for side, (mid, top, low), col in ((hw, (2, 4, 6), 5), (he, (3, 5, 7), 8)):
            for q in range(3):
                strip[0:TS, :] = chosen(low, q)
                strip[0:3, :] = strip[TS - 3 : TS, :]
                strip[3 : TS + 3, :] = chosen(mid, q)
                strip[112 : 112 + TS, :] = chosen(top, q)
                strip[TS + 3 : TS + 6, :] = strip[112:115, :]
                side[pl.ds(col + q, PADROWS, stride=16), :] = strip[0:PADROWS, :]
        i0 = lax.broadcasted_iota(jnp.int32, (TS, TS), 0)
        i1 = lax.broadcasted_iota(jnp.int32, (TS, TS), 1)
        turn = (i0 + i1 == TS - 1).astype(BF16)
        for q in range(3):
            o = q * PITCH
            hs[o + 8 : o + 104, :] = chosen(1, q)
            hs[o : o + 8, :] = hw[q * 16 : q * 16 + 8, :]
            hs[o + 104 : o + 112, :] = he[q * 16 + 8 : q * 16 + 16, :]
            flipped = mm(turn, got[pick[16], (2 - q) * TS : (3 - q) * TS, :])
            north = jnp.where(pick[17] > 0, flipped, chosen(0, q))
            hn[o + 8 : o + 104, :] = jnp.where(pick[8] > 0, north, 0.0)
            r = (TS + 3 + q) * 16
            hn[o : o + 8, :] = hw[r : r + 8, :]
            hn[o + 104 : o + 112, :] = he[r + 8 : r + 16, :]

    cv[...] = conv0[...]

    for r in range(8):
        for side, taps, shift, col in ((hw, (0, 1, 2), 5, 0), (he, (4, 5, 6), -3, 88)):
            total = cv[r * TS + col : r * TS + col + 8, :]
            for a in range(7):
                row = step * 8 + r + a
                inside = jnp.logical_and(row >= 3, row < TS + 3).astype(F32)
                part = None
                for b in taps:
                    v = kb[7 * a + b] * side[pl.ds(row * 16 + b + shift, 8), :]
                    part = v if part is None else part + v
                total = total + part * inside
            cv[r * TS + col : r * TS + col + 8, :] = total

    def rim(rows, pairs):
        def body(jb, carry):
            j0 = pl.multiple_of(jb * 8, 8)
            for d, terms in pairs:
                o = pl.ds(pl.multiple_of(d * TS + j0, 8), 8)
                total = cv[o, :]
                for a, r in terms:
                    for b in range(7):
                        total = total + kb[7 * a + b] * rows[pl.ds(r * PITCH + j0 + 5 + b, 8), :]
                cv[o, :] = total
            return carry

        lax.fori_loop(0, 12, body, 0)

    @pl.when(step == 0)
    def _():
        rim(hs, [(i, [(a, i + a) for a in range(3 - i)]) for i in range(3)])

    @pl.when(step == 11)
    def _():
        rim(hn, [(5 + i, [(a, i + a - 6) for a in range(6 - i, 7)]) for i in range(3)])

    def chunk(c, carry):
        here = pl.ds(pl.multiple_of(c * CHUNK, CHUNK), CHUNK)
        rm = rmet[:, here]
        conv = cv[here, :].T * rm
        centred = conv - jnp.mean(conv, axis=0, keepdims=True)
        inv_std = lax.rsqrt(jnp.mean(centred * centred, axis=0, keepdims=True) + EPS)
        normed = centred * inv_std
        g2 = wide2(gain[...])
        normed_bf = (normed * g2).astype(BF16)
        hidden = mm(w_in_t[...], normed_bf) + wide2(bias[...])
        sq = hidden * hidden
        t = jnp.tanh(hidden * (GELU_COEF + (GELU_COEF * CUBIC) * sq))
        p = 0.5 + 0.5 * t
        active = hidden * p
        active_bf = active.astype(BF16)
        mixed = mm(w_out_t[...], active_bf)
        ms = wet[:, here] * wide2(scale[...])
        updated[:, here] = (feat[:, here].astype(F32) + ms * mixed).astype(BF16)
        gm = (ms * cot[:, here].astype(F32)).astype(BF16)
        slope = p + active * (1.0 - p) * (2.0 * GELU_COEF + (6.0 * GELU_COEF * CUBIC) * sq)
        gh = (mm(w_out[...], gm) * slope).astype(BF16)
        gn = mm(w_in[...], gh) * g2
        gwo[...] += nt(gm, active_bf)
        gwi[...] += nt(normed_bf, gh)
        gc = inv_std * (
            gn
            - jnp.mean(gn, axis=0, keepdims=True)
            - normed * jnp.mean(gn * normed, axis=0, keepdims=True)
        )
        gsrc[here, :] = (gc * rm).T.astype(BF16)
        return carry

    lax.fori_loop(0, BLOCK // CHUNK, chunk, 0)


def mlp_call(pick, got, conv0, feat, cot, wet, rmet, k49, gain, w_in, bias, w_out, scale):
    def whole(*shape):
        return pl.BlockSpec(shape, lambda i, p: (0,) * len(shape))

    rows = pl.BlockSpec((BLOCK, C), lambda i, p: (i, 0))
    cols = pl.BlockSpec((C, BLOCK), lambda i, p: (0, i))
    lane = pl.BlockSpec((1, BLOCK), lambda i, p: (0, i))
    return pl.pallas_call(
        mlp_kernel,
        out_shape=(
            jax.ShapeDtypeStruct((C, CELLS), BF16),
            jax.ShapeDtypeStruct((CELLS, C), BF16),
            jax.ShapeDtypeStruct((C, HID), F32),
            jax.ShapeDtypeStruct((C, HID), F32),
            jax.ShapeDtypeStruct((PADROWS * 16, C), F32),
            jax.ShapeDtypeStruct((PADROWS * 16, C), F32),
            jax.ShapeDtypeStruct((BAND, C), F32),
            jax.ShapeDtypeStruct((BAND, C), F32),
        ),
        grid_spec=pltpu.PrefetchScalarGridSpec(
            num_scalar_prefetch=1,
            grid=(CELLS // BLOCK,),
            in_specs=[
                whole(15, STRIP, C), rows, cols, cols, lane, lane, whole(49, C), whole(C, C),
                whole(HID, C), whole(C, HID), whole(HID, C), whole(C, HID), whole(HID, C),
                whole(C, C),
            ],
            out_specs=[
                cols, rows, whole(C, HID), whole(C, HID), whole(PADROWS * 16, C),
                whole(PADROWS * 16, C), whole(BAND, C), whole(BAND, C),
            ],
            scratch_shapes=[
                pltpu.VMEM((BLOCK, C), F32),
                pltpu.VMEM((49, 8, C), F32),
                pltpu.VMEM((208, C), F32),
            ],
        ),
        compiler_params=pltpu.CompilerParams(vmem_limit_bytes=VMEM_LIMIT),
        name="mlp",
    )(
        pick, got, conv0, feat, cot, wet, rmet, k49,
        jnp.broadcast_to(gain[:, None], (C, C)),
        w_in.T, w_in,
        jnp.broadcast_to(bias[:, None], (HID, C)),
        w_out.T, w_out,
        jnp.broadcast_to(scale[:, None], (C, C)),
    )


def back_kernel(
    gsrc, pad_hbm, hw, he, hs, hn, k49, north_of, gwi, gwo,
    inner, got, wsum, ksum,
    pad, gp, kb, frame, fw, fe, strips, wmine, wpart, wnode, wall, kacc, kmine, kpart, kwide, kall,
    pad_sem, bsend, brecv, s1, r1, s2, r2, s3, r3, s4, r4, s5, r5, s6, r6,
):
    n = lax.axis_index("node")
    w = lax.axis_index("wide")
    peers = border_peers(n, w)
    wide_peers = [(k, lax.rem(w + k, WIDE)) for k in range(1, WIDE)]
    node_peers = [(k, lax.rem(n + k, NODE)) for k in range(1, NODE)]
    greet = [(n, v) for _, v in wide_peers] + [(v, w) for _, v in node_peers]
    greet += [device for slot, _, device in peers if slot > 2 and slot not in (3, 7, 11)]
    barrier = pltpu.get_barrier_semaphore()
    for device in greet:
        pl.semaphore_signal(barrier, inc=1, device_id=device, device_id_type=MESH)
    fetch = pltpu.make_async_copy(pad_hbm, pad, pad_sem)
    fetch.start()

    def send(src, dst, send_sem, recv_sem, device):
        copy = pltpu.make_async_remote_copy(
            src_ref=src,
            dst_ref=dst,
            send_sem=send_sem,
            recv_sem=recv_sem,
            device_id=device,
            device_id_type=MESH,
        )
        copy.start()
        return copy

    for k in range(4):
        here = slice(k * C, (k + 1) * C)
        wmine[here, :] = (gwi[:, here] * GRAD_SCALE).astype(BF16)
        wmine[HID + k * C : HID + (k + 1) * C, :] = (gwo[:, here] * GRAD_SCALE).astype(BF16)
    pl.semaphore_wait(barrier, len(greet))
    first = []
    for k, v in wide_peers:
        src = wmine.at[pl.ds(pl.multiple_of(v * 32, 32), 32)]
        first.append(send(src, wpart.at[k], s1.at[k], r1.at[k], (n, v)))

    broadcast_taps(k49, kb)
    clear_margins(gp)

    def fill(i, carry):
        o = pl.multiple_of((i + 3) * PITCH + 8, 8)
        gp[pl.ds(o, TS), :] = gsrc[pl.ds(pl.multiple_of(i * TS, 32), TS), :].astype(F32)
        return carry

    lax.fori_loop(0, TS, fill, 0)

    def frame_rows(jb, carry):
        j0 = pl.multiple_of(jb * 8, 8)
        for f, p in enumerate((0, 1, 2, 99, 100, 101)):
            total = None
            for a in range(7):
                if 0 <= p - a < TS:
                    for b in range(7):
                        v = kb[7 * a + b] * gp[pl.ds((p - a + 3) * PITCH + j0 + 8 - b, 8), :]
                        total = v if total is None else total + v
            frame[f, pl.ds(j0, 8), :] = total
        return carry

    lax.fori_loop(0, 13, frame_rows, 0)

    def frame_cols(i, carry):
        p = i + 3
        for side, taps, q0 in ((fw, (0, 1, 2), 0), (fe, (4, 5, 6), 96)):
            total = None
            for a in range(7):
                for b in taps:
                    v = kb[7 * a + b] * gp[pl.ds((p - a + 3) * PITCH + q0 + 8 - b, 8), :]
                    total = v if total is None else total + v
            side[pl.ds(pl.multiple_of(p * 8, 8), 8), :] = total
        return carry

    lax.fori_loop(0, TS, frame_cols, 0)
    for f, p in enumerate((0, 1, 2, 99, 100, 101)):
        fw[p * 8 : p * 8 + 8, :] = frame[f, 0:8, :]
        fe[p * 8 : p * 8 + 8, :] = frame[f, 96:104, :]
    fw[PADROWS * 8 :, :] = jnp.zeros((80, C), F32)
    fe[PADROWS * 8 :, :] = jnp.zeros((80, C), F32)
    for q in range(3):
        here = pl.ds(q * PITCH, PITCH)
        strips[3, here, :] = fw[pl.ds(q, PITCH, stride=8), :].astype(BF16)
        strips[4, here, :] = fe[pl.ds(3 + q, PITCH, stride=8), :].astype(BF16)
        here = pl.ds(q * TS, TS)
        south = frame[q, 3 : 3 + TS, :]
        north = frame[3 + q, 3 : 3 + TS, :]
        strips[5, here, :] = north.astype(BF16)
        for k in range(3):
            mine = jnp.where(north_of[k : k + 1, :] > 0.0, south, north)
            strips[k, here, :] = mine.astype(BF16)
    borders = []
    for slot, source, device in peers:
        size = BAND if source in (3, 4) else STRIP
        borders.append(
            send(
                strips.at[source, pl.ds(0, size)],
                got.at[slot, pl.ds(0, size)],
                bsend.at[slot],
                brecv.at[slot],
                device,
            )
        )

    fetch.wait()
    pad[0:BAND, :] = hs[...]
    pad[99 * PITCH :, :] = hn[...]

    def sides(i, carry):
        o = pl.multiple_of((i + 3) * PITCH, 8)
        r = pl.multiple_of((i + 3) * 16, 8)
        pad[pl.ds(o, 8), :] = hw[pl.ds(r, 8), :]
        pad[pl.ds(o + 104, 8), :] = he[pl.ds(r + 8, 8), :]
        return carry

    lax.fori_loop(0, TS, sides, 0)
    kmine[48:64, :] = jnp.zeros((16, C), BF16)
    for b in range(7):

        def taps(it, acc, b=b):
            i0 = it * 4
            acc = list(acc)
            for jb in range(12):
                g = [gp[pl.ds((i0 + d + 3) * PITCH + 8 + 8 * jb, 8), :] for d in range(4)]
                for r in range(10):
                    v = pad[pl.ds((i0 + r) * PITCH + 8 * jb + 5 + b, 8), :]
                    for a in range(7):
                        if 0 <= r - a < 4:
                            acc[a] = acc[a] + g[r - a] * v
            return tuple(acc)

        zero = jnp.zeros((8, C), F32)
        acc = lax.fori_loop(0, 24, taps, (zero,) * 7)
        for a in range(7):
            kacc[7 * a + b : 7 * a + b + 1, :] = jnp.sum(acc[a], axis=0, keepdims=True)
    kacc[49:64, :] = jnp.zeros((15, C), F32)
    kmine[...] = (kacc[...] * GRAD_SCALE).astype(BF16)

    for copy in first:
        copy.wait()
    mine = pl.ds(pl.multiple_of(w * 32, 32), 32)
    total = wmine[mine, :].astype(F32)
    for k in range(1, WIDE):
        total = total + wpart[k].astype(F32)
    wnode[n] = total.astype(BF16)
    second = []
    for k, v in node_peers:
        second.append(send(wnode.at[n], wnode.at[n], s2.at[k], r2.at[k], (v, w)))
        src = kmine.at[pl.ds(pl.multiple_of(v * 16, 16), 16)]
        second.append(send(src, kpart.at[k], s4.at[k], r4.at[k], (v, w)))

    taps_loop(gp, kb, inner, True)

    for copy in second:
        copy.wait()
    total = wnode[0].astype(F32)
    for v in range(1, NODE):
        total = total + wnode[v].astype(F32)
    wall[w] = total.astype(BF16)
    total = kmine[pl.ds(pl.multiple_of(n * 16, 16), 16), :].astype(F32)
    for k in range(1, NODE):
        total = total + kpart[k].astype(F32)
    kwide[w] = total.astype(BF16)
    third = []
    for k, v in wide_peers:
        third.append(send(wall.at[w], wall.at[w], s3.at[k], r3.at[k], (n, v)))
        third.append(send(kwide.at[w], kwide.at[w], s5.at[k], r5.at[k], (n, v)))
    for copy in third:
        copy.wait()
    total = kwide[0].astype(F32)
    for v in range(1, WIDE):
        total = total + kwide[v].astype(F32)
    kall[n] = total.astype(BF16)
    fourth = []
    for k, v in node_peers:
        fourth.append(send(kall.at[n], kall.at[n], s6.at[k], r6.at[k], (v, w)))
    for v in range(WIDE):
        wsum[v * 32 : (v + 1) * 32, :] = wall[v].astype(F32)
    for copy in fourth:
        copy.wait()
    for v in range(NODE):
        ksum[v * 16 : (v + 1) * 16, :] = kall[v].astype(F32)
    for copy in borders:
        copy.wait()


def back_call(gsrc, pad, hw, he, hs, hn, k49, north_of, gwi, gwo):
    vmem = pl.BlockSpec(memory_space=pltpu.VMEM)
    dma = pltpu.SemaphoreType.DMA
    return pl.pallas_call(
        back_kernel,
        out_shape=(
            jax.ShapeDtypeStruct((CELLS, C), F32),
            jax.ShapeDtypeStruct((15, BAND, C), BF16),
            jax.ShapeDtypeStruct((8 * C, C), F32),
            jax.ShapeDtypeStruct((64, C), F32),
        ),
        in_specs=[vmem, pl.BlockSpec(memory_space=pl.ANY)] + [vmem] * 8,
        out_specs=(vmem,) * 4,
        scratch_shapes=[
            pltpu.VMEM((PADROWS * PITCH, C), F32),
            pltpu.VMEM((PADROWS * PITCH, C), F32),
            pltpu.VMEM((49, 8, C), F32),
            pltpu.VMEM((6, 104, C), F32),
            pltpu.VMEM((PITCH * 8, C), F32),
            pltpu.VMEM((PITCH * 8, C), F32),
            pltpu.VMEM((6, BAND, C), BF16),
            pltpu.VMEM((8 * C, C), BF16),
            pltpu.VMEM((WIDE, 32, C), BF16),
            pltpu.VMEM((NODE, 32, C), BF16),
            pltpu.VMEM((WIDE, 32, C), BF16),
            pltpu.VMEM((64, C), F32),
            pltpu.VMEM((64, C), BF16),
            pltpu.VMEM((NODE, 16, C), BF16),
            pltpu.VMEM((WIDE, 16, C), BF16),
            pltpu.VMEM((NODE, 16, C), BF16),
            dma,
            dma((15,)), dma((15,)),
            dma((WIDE,)), dma((WIDE,)),
            dma((NODE,)), dma((NODE,)),
            dma((WIDE,)), dma((WIDE,)),
            dma((NODE,)), dma((NODE,)),
            dma((WIDE,)), dma((WIDE,)),
            dma((NODE,)), dma((NODE,)),
        ],
        compiler_params=pltpu.CompilerParams(
            collective_id=1, has_side_effects=True, vmem_limit_bytes=VMEM_LIMIT
        ),
        name="back",
    )(gsrc, pad, hw, he, hs, hn, k49, north_of, gwi, gwo)


def final_kernel(pick, got, inner, cot, wc, out, cw, ce, low, top, strip, sb):
    step = pl.program_id(0)

    @pl.when(step == 0)
    def _():
        cw[...] = jnp.zeros_like(cw)
        ce[...] = jnp.zeros_like(ce)

        def chosen(direction, start, size):
            v = got[pick[direction], pl.ds(start, size), :].astype(F32)
            return jnp.where(pick[8 + direction] > 0, v, 0.0)

        for side, (mid, north, south), col in ((cw, (2, 4, 6), 0), (ce, (3, 5, 7), 5)):
            for q in range(3):
                strip[0] = chosen(mid, q * PITCH, PITCH)
                strip[1] = chosen(north, q * PITCH, PITCH)
                strip[2] = chosen(south, q * PITCH, PITCH)
                strip[0, TS : TS + 3, :] += strip[1, 0:3, :]
                strip[0, 3:6, :] += strip[2, TS + 3 : TS + 6, :]
                side[pl.ds(col + q, TS, stride=8), :] = strip[0, 3 : TS + 3, :]
        i0 = lax.broadcasted_iota(jnp.int32, (TS, TS), 0)
        i1 = lax.broadcasted_iota(jnp.int32, (TS, TS), 1)
        turn = (i0 + i1 == TS - 1).astype(BF16)
        for q in range(3):
            low[q * TS : (q + 1) * TS, :] = chosen(1, q * TS, TS)
            flipped = mm(turn, got[pick[16], (2 - q) * TS : (3 - q) * TS, :])
            north = jnp.where(pick[17] > 0, flipped, chosen(0, q * TS, TS))
            top[q * TS : (q + 1) * TS, :] = jnp.where(pick[8] > 0, north, 0.0)

    sb[...] = inner[...]
    for r in range(8):
        row = pl.multiple_of((step * 8 + r) * 8, 8)
        sb[r * TS : r * TS + 8, :] += cw[pl.ds(row, 8), :]
        sb[r * TS + 88 : r * TS + 96, :] += ce[pl.ds(row, 8), :]

    @pl.when(step == 0)
    def _():
        sb[0:STRIP, :] += low[...]

    @pl.when(step == 11)
    def _():
        sb[5 * TS :, :] += top[...]

    out[...] = (cot[...].astype(F32) + wc[...] * sb[...].T).astype(BF16)


def final_call(pick, got, inner, cot, wc):
    rows = pl.BlockSpec((BLOCK, C), lambda i, p: (i, 0))
    cols = pl.BlockSpec((C, BLOCK), lambda i, p: (0, i))
    lane = pl.BlockSpec((1, BLOCK), lambda i, p: (0, i))
    return pl.pallas_call(
        final_kernel,
        out_shape=jax.ShapeDtypeStruct((C, CELLS), BF16),
        grid_spec=pltpu.PrefetchScalarGridSpec(
            num_scalar_prefetch=1,
            grid=(CELLS // BLOCK,),
            in_specs=[pl.BlockSpec((15, BAND, C), lambda i, p: (0, 0, 0)), rows, cols, lane],
            out_specs=cols,
            scratch_shapes=[
                pltpu.VMEM((TS * 8, C), F32),
                pltpu.VMEM((TS * 8, C), F32),
                pltpu.VMEM((STRIP, C), F32),
                pltpu.VMEM((STRIP, C), F32),
                pltpu.VMEM((3, PITCH, C), F32),
                pltpu.VMEM((BLOCK, C), F32),
            ],
        ),
        compiler_params=pltpu.CompilerParams(vmem_limit_bytes=VMEM_LIMIT),
        name="final",
    )(pick, got, inner, cot, wc)


def local(
    features,
    cotangent,
    wet_fraction,
    slot_tile,
    neighbours,
    kernel,
    norm_gain,
    weight_in,
    bias_in,
    weight_out,
    layer_scale,
):
    n = lax.axis_index("node")
    w = lax.axis_index("wide")
    tile = slot_tile[n * WIDE + w]
    row = jnp.maximum(tile, 0) // WIDE
    cell_row = jnp.arange(CELLS, dtype=jnp.int32) // TS
    global_row = row * TS + cell_row
    latitude = -80.0 + 160.0 * (global_row.astype(F32) + 0.5) / float(8 * TS)
    metric = jnp.cos(latitude * (math.pi / 180.0))[None, :]
    near = jnp.where(tile >= 0, neighbours[jnp.maximum(tile, 0)], -1)
    present = near >= 0
    target = jnp.maximum(near, 0) // 2
    slot_ids = jnp.arange(NODE * WIDE, dtype=jnp.int32)
    owner = jnp.sum(
        jnp.where(slot_tile[None, :] == target[:, None], slot_ids[None, :], 0), axis=-1
    )
    turn = (n - owner // WIDE + NODE) % NODE
    base = jnp.array([-1, -1, 7, 3, 7, 3, 7, 3], jnp.int32)
    slot = jnp.where(present, jnp.maximum(base + turn, 0), 0)
    flip = jnp.where(present[0], near[0] % 2, 0)
    pick = jnp.concatenate(
        [
            slot.at[0].set(jnp.where(flip > 0, 0, slot[0])),
            present.astype(jnp.int32),
            jnp.stack([11 + turn[0], flip]),
        ]
    )
    column = slot_tile[((n + jnp.arange(1, 4)) % NODE) * WIDE + w]
    is_north = (column == target[1]) & present[1]
    north_of = jnp.broadcast_to(
        jnp.pad(is_north.astype(F32), (0, 5))[:, None], (8, C)
    )
    wc = wet_fraction * metric
    feat = features.reshape(C, CELLS)
    cot = cotangent.reshape(C, CELLS)
    conv0, pad, got = halo_call(feat, wc, kernel, north_of)
    updated, gsrc, gwi, gwo, hw, he, hs, hn = mlp_call(
        pick, got, conv0, feat, cot, wet_fraction, 1.0 / metric, kernel, norm_gain, weight_in,
        bias_in, weight_out, layer_scale,
    )
    inner, back_got, wsum, ksum = back_call(gsrc, pad, hw, he, hs, hn, kernel, north_of, gwi, gwo)
    grad_features = final_call(pick, back_got, inner, cot, wc)
    halves = wsum.reshape(2, 4, C, C)
    grad_in = jnp.transpose(halves[0], (1, 0, 2)).reshape(C, HID)
    grad_out = jnp.transpose(halves[1], (0, 2, 1)).reshape(HID, C)
    return (
        updated.reshape(1, C, CELLS),
        grad_features.reshape(1, C, CELLS),
        grad_in,
        grad_out,
        ksum[:49],
    )


def solution(mesh):
    shards = P(("node", "wide"), None, None)
    in_specs = (shards, shards, P(("node", "wide"), None)) + (P(),) * 8
    out_specs = (shards, shards, P(), P(), P())
    return jax.shard_map(local, mesh=mesh, in_specs=in_specs, out_specs=out_specs, check_vma=False)
```

time: 605 us -> 194 us (0.32); the launches traced: 598 us -> 194 us
  other arithmetic: 226 us -> 7.08 us
  Pallas kernels: 0 us -> 167 us
  blocking collectives: 89.9 us -> 0 us
  waiting for transfers between devices: 80.1 us -> 0 us
  local copies, waits for them, and re-layouts: 91.7 us -> 14.6 us
  matrix products: 58.7 us -> 0 us
  starting transfers between devices: 35.5 us -> 0 us
  between operations: 16.4 us -> 4.73 us
    pallas_call x0 -> x4, Pallas kernels: none -> 167 us  [the longest x1 68.2 us: back_call(): pl.pallas_call(back_kernel, out_shape=(jax.ShapeDtypeStruct((CELLS, C), F...]
    add x5 -> x0, other arithmetic: 121 us -> none  [the longest x1 82.5 us: spread_back(): total + kernel[7 * row_off + col_off][:, None] * long_flat[:, start:start...]
    psum x1 -> x0, blocking collectives: 68.8 us -> none  [local(): lax.psum((jnp.sum(grad_w_in, axis=0), jnp.sum(grad_w_out, axis=0), jnp.su...]
    dot_general x6 -> x0, matrix products: 58.7 us -> none  [the longest x1 19.7 us: block_tile(): jnp.dot(weight_out, grad_mixed, preferred_element_type=jnp.float32)]
    psum x1 -> x0, waiting for transfers between devices: 56.4 us -> none  [local(): lax.psum((jnp.sum(grad_w_in, axis=0), jnp.sum(grad_w_out, axis=0), jnp.su...]
    reduce_sum x7 -> x1, other arithmetic: 52.7 us -> 0.84 us  [local(): jnp.sum(jnp.where(slot_tile[None, :] == target[:, None], slot_ids[None, :...]
    ppermute x14 -> x0, starting transfers between devices: 35.4 us -> none  [the longest x10 30.8 us: swapped(): return lax.ppermute(value, axis, pairs)]
    ppermute x14 -> x0, waiting for transfers between devices: 23.6 us -> none  [the longest x10 23.6 us: swapped(): return lax.ppermute(value, axis, pairs)]
  transfers between devices with their start and end apart: 17 -> 0, of which waited for: 7 -> 0; matrix products, arithmetic and copies ran while one was open for 9% -> 0% of each run, Pallas kernels for 0% -> 0%
where the time goes in v1:
time: 194 us
  Pallas kernels  167 us (86%)
  local copies, waits for them, and re-layouts  14.6 us (8%)
  other arithmetic  7.08 us (4%)
  between operations  4.73 us (2%)
    pallas_call x1, Pallas kernels, back_call(): pl.pallas_call(back_kernel, out_shape=(jax.ShapeDtypeStruct((CELLS, C), F...  68.2 us
    pallas_call x1, Pallas kernels, mlp_call(): pl.pallas_call(mlp_kernel, out_shape=(jax.ShapeDtypeStruct((C, CELLS), BF...  45.7 us
    pallas_call x1, Pallas kernels, halo_call(): pl.pallas_call(halo_kernel, out_shape=(jax.ShapeDtypeStruct((CELLS, C), F...  42.1 us
    pallas_call x1, Pallas kernels, final_call(): pl.pallas_call(final_kernel, out_shape=jax.ShapeDtypeStruct((C, CELLS), B...  11.2 us

profile of v1, /device:TPU:1, one launch (start us, length us, event | category | flops | bytes accessed | tf_op | source)
XLA Modules:
  0.0 193.7 jit_solution(17537035453333587056)
XLA Ops:
  0.6 1.2 dynamic_slice.6
  3.2 1.3 gather_fusion
  4.5 0.9 fusion.16
  5.4 0.5 slice.43
  7.9 0.5 fusion.18
  9.1 0.1 fusion.9
  9.2 0.1 shift-right-logical_reduce_fusion
  9.3 0.6 slice.46
  9.9 1.3 compare_and_fusion
  11.2 0.8 select_reduce_fusion
  12.0 0.7 fusion.15
  12.8 0.7 pad_add_fusion.pick
  13.5 0.7 broadcast_in_dim.32.north_of
  14.1 1.4 broadcast_in_dim.54.gain
  15.5 1.4 broadcast_in_dim.56.scale
  16.8 2.5 %broadcast_divide_fusion = (f32[1,9216]{1,0:T(1,128)}, f32[1,9216]{1,0:T(1,128)}) fusion(s32[]{:T(128)S(6)} %mul.41, f32[1,9216]{1,0:T(1,128)} %wet.1), kind=kLoop, calls=%fused_computation.13 | loop fusion | flops 147456 | bytes 110596 | tf_op jit(solution)/shard_map/div | solution.py:692
  19.3 1.7 copy.25
  21.0 1.7 copy.26
  22.6 1.5 broadcast_in_dim.55.bias
  24.1 42.1 %halo.1 = (f32[9216,128]{1,0:T(8,128)}, f32[11424,128]{1,0:T(8,128)}, bf16[15,288,128]{2,1,0:T(8,128)(2,1)}) custom-call(bf16[128,9216]{1,0:T(8,128)(2,1)} %bitcast.30, f32[1,9216]{1,0:T(1,128)} %get-tuple-element.57.wc, f32[49,128]{1,0:T(8,128)} %k49.5, f32[8,128]{1,0:T(8,128)} %broadcast_in_dim.32.north_of), custom_call_target="tpu_custom_call" | custom-call | tf_op jit(solution)/shard_map/halo/pallas_call | solution.py:140
  66.3 45.7 %mlp.1 = (bf16[128,9216]{1,0:T(8,128)(2,1)}, bf16[9216,128]{1,0:T(8,128)(2,1)}, f32[128,512]{1,0:T(8,128)}, f32[128,512]{1,0:T(8,128)}, f32[1632,128]{1,0:T(8,12...) custom-call(s32[18]{0:T(128)} %pad_add_fusion.pick, ...), custom_call_target="tpu_custom_call" | custom-call | tf_op jit(solution)/shard_map/mlp/pallas_call | solution.py:295
  112.0 68.2 %back.1 = (f32[9216,128]{1,0:T(8,128)}, bf16[15,336,128]{2,1,0:T(8,128)(2,1)}, f32[1024,128]{1,0:T(8,128)}, f32[64,128]{1,0:T(8,128)}) custom-call(bf16[9216,128]{1,0:T(8,128)(2,1)} %get-tuple-element.35.gsrc, f32[11424,128]{1,0:T(8,128)} %get-tuple-element.36.pad_hbm, f32[1632,128]{1,0:T(8,128)} %get-tuple-element.37.hw, f32[1632,128]{1,0:T(8,128)} %get-tuple-element.38.he, ...), custom_call_target="tpu_custom_call" | custom-call | tf_op jit(solution)/shard_map/back/pallas_call | solution.py:528
  180.3 0.0 copy-start.1
  180.3 0.0 copy-start
  180.3 11.2 %final.1 = bf16[128,9216]{1,0:T(8,128)(2,1)} custom-call(s32[18]{0:T(128)} %pad_add_fusion.pick, bf16[15,336,128]{2,1,0:T(8,128)(2,1)} %get-tuple-element.43.got, f32[9216,128]{1,0:T(8,128)} %get-tuple-element.44.inner, bf16[128,9216]{1,0:T(8,128)(2,1)} %bitcast.33, f32[1,9216]{1,0:T(1,128)} %get-tuple-element.57.wc), custom_call_target="tpu_custom_call" | custom-call | tf_op jit(solution)/shard_map/final/pallas_call | solution.py:621
  191.5 0.0 copy-done.1
  191.5 0.6 slice.50
  192.1 0.0 copy-done
  192.1 0.8 copy.28
  193.0 0.7 copy.31
  (7 shorter events, 0.1 us)
Async XLA Ops:
  180.3 11.2 %copy-start.1 = (f32[64,128]{1,0:T(8,128)S(1)}, f32[64,128]{1,0:T(8,128)}, u32[]{:S(2)}) copy-start(f32[64,128]{1,0:T(8,128)} %get-tuple-element.46) | copy-start | bytes 98308
  180.3 11.8 %copy-start = (f32[1024,128]{1,0:T(8,128)S(1)}, f32[1024,128]{1,0:T(8,128)}, u32[]{:S(2)}) copy-start(f32[1024,128]{1,0:T(8,128)} %get-tuple-element.45) | copy-start | bytes 1572868

commit v2 on v1

--- a/solution.py
+++ b/solution.py
@@ -46,27 +46,30 @@
 
 
 def taps_loop(src, kb, out, flip):
+    zero = jnp.zeros((TS, C), F32)
+
+    def clear(i, carry):
+        out[pl.ds(pl.multiple_of(i * TS, 8), TS), :] = zero
+        return carry
+
+    lax.fori_loop(0, TS, clear, 0)
+
     def body(it, carry):
-        i0 = (it // 6) * 4
-        j0 = lax.rem(it, 6) * 16
-        acc = [[None, None] for _ in range(4)]
-        for b in range(7):
-            for r in range(10):
-                for h in range(2):
-                    v = src[pl.ds((i0 + r) * PITCH + j0 + 5 + b + 8 * h, 8), :]
-                    for a in range(7):
-                        d = r - a
-                        if 0 <= d < 4:
-                            t = 48 - (7 * a + b) if flip else 7 * a + b
-                            p = kb[t] * v
-                            acc[d][h] = p if acc[d][h] is None else acc[d][h] + p
-        for d in range(4):
-            for h in range(2):
-                o = pl.multiple_of((i0 + d) * TS + j0 + 8 * h, 8)
-                out[pl.ds(o, 8), :] = acc[d][h]
-        return carry
-
-    lax.fori_loop(0, 144, body, 0)
+        b = it // 12
+        i0 = lax.rem(it, 12) * 8
+        taps = [kb[48 - 7 * a - b] if flip else kb[7 * a + b] for a in range(7)]
+        for jb in range(12):
+            base = i0 * PITCH + 8 * jb + 5 + b
+            v = [src[pl.ds(base + r * PITCH, 8), :] for r in range(14)]
+            for d in range(8):
+                total = taps[0] * v[d]
+                for a in range(1, 7):
+                    total = total + taps[a] * v[d + a]
+                o = pl.ds(pl.multiple_of((i0 + d) * TS + 8 * jb, 8), 8)
+                out[o, :] = out[o, :] + total
+        return carry
+
+    lax.fori_loop(0, 84, body, 0)
 
 
 def clear_margins(pad):
@@ -84,7 +87,19 @@
     lax.fori_loop(0, TS, body, 0)
 
 
-def halo_kernel(feat, wc, k49, north_of, conv0, pad, got, strips, kb, send_sem, recv_sem):
+def cosine(x):
+    x2 = x * x
+    total = jnp.full_like(x, 1.0 / math.factorial(16))
+    for k in range(7, -1, -1):
+        total = total * x2 + (-1.0) ** k / math.factorial(2 * k)
+    return total
+
+
+def halo_kernel(
+    feat, wet, k49, slot_tile, neighbours,
+    conv0, field, got, wc, rmet, pick,
+    pad, strips, kb, send_sem, recv_sem,
+):
     n = lax.axis_index("node")
     w = lax.axis_index("wide")
     peers = border_peers(n, w)
@@ -92,16 +107,60 @@
     for _, _, device in peers:
         pl.semaphore_signal(barrier, inc=1, device_id=device, device_id_type=MESH)
 
+    tile = slot_tile[n * WIDE + w]
+    known = jnp.maximum(tile, 0)
+    lane = lax.broadcasted_iota(jnp.int32, (1, 8), 1)
+    near = jnp.where(tile >= 0, neighbours[pl.ds(known, 1), :], -1)
+    present = near >= 0
+    target = jnp.maximum(near, 0) >> 1
+    flip = jnp.where(present, near & 1, 0)
+    is_west = (lane == 2) | (lane == 4) | (lane == 6)
+    is_east = (lane == 3) | (lane == 5) | (lane == 7)
+    turn = jnp.zeros((1, 8), jnp.int32)
+    mirror_turn = jnp.zeros((1, 8), jnp.int32)
+    for k in range(4):
+        m = lax.rem(n + 4 - k, 4) * WIDE
+        held = jnp.where(
+            is_west,
+            slot_tile[m + lax.rem(w + 31, 32)],
+            jnp.where(is_east, slot_tile[m + lax.rem(w + 1, 32)], slot_tile[m + w]),
+        )
+        turn = jnp.where(held == target, k, turn)
+        mirror_turn = jnp.where(slot_tile[m + 31 - w] == target, k, mirror_turn)
+    slot = jnp.where(is_west, 7 + turn, jnp.where(is_east, 3 + turn, turn - 1))
+    slot = jnp.where(present & (flip == 0), jnp.maximum(slot, 0), 0)
+    pick[...] = jnp.zeros((8, 128), jnp.int32)
+    pick[0:1, 0:8] = slot
+    pick[1:2, 0:8] = present.astype(jnp.int32)
+    pick[2:3, 0:8] = 11 + mirror_turn
+    pick[3:4, 0:8] = flip
+    north_of = []
+    for k in range(1, 4):
+        held = slot_tile[lax.rem(n + k, 4) * WIDE + w]
+        same = jnp.where((lane == 1) & present & (held == target), 1.0, 0.0)
+        same = jnp.broadcast_to(jnp.sum(same, axis=1, keepdims=True), (1, C))
+        north_of.append(same > 0.0)
+        pick[3 + k : 4 + k, :] = same.astype(jnp.int32)
+
     broadcast_taps(k49, kb)
     clear_margins(pad)
+    cell = lax.broadcasted_iota(jnp.int32, (1, 384), 1)
+    sub_row = jnp.where(cell >= 96, 1.0, 0.0) + jnp.where(cell >= 192, 1.0, 0.0)
+    sub_row = sub_row + jnp.where(cell >= 288, 1.0, 0.0)
+    first_row = ((known >> 5) * TS).astype(F32) + 0.5
 
     def prep(g, carry):
-        o = pl.multiple_of(g * 384, 128)
-        x = feat[:, pl.ds(o, 384)].astype(F32) * wc[:, pl.ds(o, 384)]
-        t = x.astype(BF16).astype(F32).T
+        here = pl.ds(pl.multiple_of(g * 384, 128), 384)
+        latitude = -80.0 + 160.0 * (sub_row + ((g * 4).astype(F32) + first_row)) / float(8 * TS)
+        metric = cosine(latitude * (math.pi / 180.0))
+        weight = wet[:, here] * metric
+        wc[:, here] = weight
+        rmet[:, here] = 1.0 / metric
+        t = (feat[:, here].astype(F32) * weight).astype(BF16).astype(F32).T
         for r in range(4):
             row = pl.multiple_of((g * 4 + r + 3) * PITCH + 8, 8)
             pad[pl.ds(row, TS), :] = t[r * TS : (r + 1) * TS]
+        field[pl.ds(pl.multiple_of(g * 384, 128), 384), :] = t.astype(BF16)
         return carry
 
     lax.fori_loop(0, 24, prep, 0)
@@ -113,8 +172,7 @@
         north = pad[pl.ds((96 + q) * PITCH + 8, TS), :]
         strips[5, here, :] = north.astype(BF16)
         for k in range(3):
-            mine = jnp.where(north_of[k : k + 1, :] > 0.0, south, north)
-            strips[k, here, :] = mine.astype(BF16)
+            strips[k, here, :] = jnp.where(north_of[k], south, north).astype(BF16)
 
     pl.semaphore_wait(barrier, len(peers))
     copies = []
@@ -135,18 +193,23 @@
         copy.wait()
 
 
-def halo_call(feat, wc, k49, north_of):
+def halo_call(feat, wet, k49, slot_tile, neighbours):
     vmem = pl.BlockSpec(memory_space=pltpu.VMEM)
+    smem = pl.BlockSpec(memory_space=pltpu.SMEM)
     return pl.pallas_call(
         halo_kernel,
         out_shape=(
             jax.ShapeDtypeStruct((CELLS, C), F32),
-            jax.ShapeDtypeStruct((PADROWS * PITCH, C), F32),
+            jax.ShapeDtypeStruct((CELLS, C), BF16),
             jax.ShapeDtypeStruct((15, STRIP, C), BF16),
+            jax.ShapeDtypeStruct((1, CELLS), F32),
+            jax.ShapeDtypeStruct((1, CELLS), F32),
+            jax.ShapeDtypeStruct((8, 128), jnp.int32),
         ),
-        in_specs=[vmem] * 4,
-        out_specs=(vmem, vmem, vmem),
+        in_specs=[vmem, vmem, vmem, smem, vmem],
+        out_specs=(vmem,) * 6,
         scratch_shapes=[
+            pltpu.VMEM((PADROWS * PITCH, C), F32),
             pltpu.VMEM((6, STRIP, C), BF16),
             pltpu.VMEM((49, 8, C), F32),
             pltpu.SemaphoreType.DMA((15,)),
@@ -156,7 +219,7 @@
             collective_id=0, has_side_effects=True, vmem_limit_bytes=VMEM_LIMIT
         ),
         name="halo",
-    )(feat, wc, k49, north_of)
+    )(feat, wet, k49, slot_tile, neighbours)
 
 
 def nt(a, b):
@@ -172,23 +235,30 @@
 
 
 def mlp_kernel(
-    pick, got, conv0, feat, cot, wet, rmet, k49, gain, w_in_t, w_in, bias, w_out_t, w_out, scale,
+    pick, got, conv0, feat, cot, wet, rmet, k49, gain_row, w_in, bias_row, w_out, scale_row,
     updated, gsrc, gwi, gwo, hw, he, hs, hn,
-    cv, kb, strip,
+    cv, kb, strip, gain, scale, bias, w_in_t, w_out_t,
 ):
     step = pl.program_id(0)
 
     @pl.when(step == 0)
     def _():
         broadcast_taps(k49, kb)
+        gain[...] = jnp.broadcast_to(gain_row[...], (C, C)).T
+        scale[...] = jnp.broadcast_to(scale_row[...], (C, C)).T
+        for k in range(4):
+            here = slice(k * C, (k + 1) * C)
+            bias[here, :] = jnp.broadcast_to(bias_row[:, here], (C, C)).T
+            w_in_t[here, :] = w_in[:, here].astype(F32).T.astype(BF16)
+            w_out_t[:, here] = w_out[here, :].astype(F32).T.astype(BF16)
         gwi[...] = jnp.zeros_like(gwi)
         gwo[...] = jnp.zeros_like(gwo)
         hw[...] = jnp.zeros_like(hw)
         he[...] = jnp.zeros_like(he)
 
         def chosen(direction, q):
-            v = got[pick[direction], pl.ds(q * TS, TS), :].astype(F32)
-            return jnp.where(pick[8 + direction] > 0, v, 0.0)
+            v = got[pick[0, direction], pl.ds(q * TS, TS), :].astype(F32)
+            return jnp.where(pick[1, direction] > 0, v, 0.0)
 
         for side, (mid, top, low), col in ((hw, (2, 4, 6), 5), (he, (3, 5, 7), 8)):
             for q in range(3):
@@ -206,9 +276,9 @@
             hs[o + 8 : o + 104, :] = chosen(1, q)
             hs[o : o + 8, :] = hw[q * 16 : q * 16 + 8, :]
             hs[o + 104 : o + 112, :] = he[q * 16 + 8 : q * 16 + 16, :]
-            flipped = mm(turn, got[pick[16], (2 - q) * TS : (3 - q) * TS, :])
-            north = jnp.where(pick[17] > 0, flipped, chosen(0, q))
-            hn[o + 8 : o + 104, :] = jnp.where(pick[8] > 0, north, 0.0)
+            flipped = mm(turn, got[pick[2, 0], (2 - q) * TS : (3 - q) * TS, :])
+            north = jnp.where(pick[3, 0] > 0, flipped, chosen(0, q))
+            hn[o + 8 : o + 104, :] = jnp.where(pick[1, 0] > 0, north, 0.0)
             r = (TS + 3 + q) * 16
             hn[o : o + 8, :] = hw[r : r + 8, :]
             hn[o + 104 : o + 112, :] = he[r + 8 : r + 16, :]
@@ -250,8 +320,8 @@
     def _():
         rim(hn, [(5 + i, [(a, i + a - 6) for a in range(6 - i, 7)]) for i in range(3)])
 
-    def chunk(c, carry):
-        here = pl.ds(pl.multiple_of(c * CHUNK, CHUNK), CHUNK)
+    for c in range(BLOCK // CHUNK):
+        here = pl.ds(c * CHUNK, CHUNK)
         rm = rmet[:, here]
         conv = cv[here, :].T * rm
         centred = conv - jnp.mean(conv, axis=0, keepdims=True)
@@ -280,9 +350,6 @@
             - normed * jnp.mean(gn * normed, axis=0, keepdims=True)
         )
         gsrc[here, :] = (gc * rm).T.astype(BF16)
-        return carry
-
-    lax.fori_loop(0, BLOCK // CHUNK, chunk, 0)
 
 
 def mlp_call(pick, got, conv0, feat, cot, wet, rmet, k49, gain, w_in, bias, w_out, scale):
@@ -308,9 +375,8 @@
             num_scalar_prefetch=1,
             grid=(CELLS // BLOCK,),
             in_specs=[
-                whole(15, STRIP, C), rows, cols, cols, lane, lane, whole(49, C), whole(C, C),
-                whole(HID, C), whole(C, HID), whole(HID, C), whole(C, HID), whole(HID, C),
-                whole(C, C),
+                whole(15, STRIP, C), rows, cols, cols, lane, lane, whole(49, C), whole(1, C),
+                whole(C, HID), whole(1, HID), whole(HID, C), whole(1, C),
             ],
             out_specs=[
                 cols, rows, whole(C, HID), whole(C, HID), whole(PADROWS * 16, C),
@@ -320,25 +386,26 @@
                 pltpu.VMEM((BLOCK, C), F32),
                 pltpu.VMEM((49, 8, C), F32),
                 pltpu.VMEM((208, C), F32),
+                pltpu.VMEM((C, C), F32),
+                pltpu.VMEM((C, C), F32),
+                pltpu.VMEM((HID, C), F32),
+                pltpu.VMEM((HID, C), BF16),
+                pltpu.VMEM((C, HID), BF16),
             ],
         ),
         compiler_params=pltpu.CompilerParams(vmem_limit_bytes=VMEM_LIMIT),
         name="mlp",
     )(
-        pick, got, conv0, feat, cot, wet, rmet, k49,
-        jnp.broadcast_to(gain[:, None], (C, C)),
-        w_in.T, w_in,
-        jnp.broadcast_to(bias[:, None], (HID, C)),
-        w_out.T, w_out,
-        jnp.broadcast_to(scale[:, None], (C, C)),
+        pick, got, conv0, feat, cot, wet, rmet, k49, gain[None, :], w_in, bias[None, :], w_out,
+        scale[None, :],
     )
 
 
 def back_kernel(
-    gsrc, pad_hbm, hw, he, hs, hn, k49, north_of, gwi, gwo,
-    inner, got, wsum, ksum,
+    gsrc, field, hw, he, hs, hn, k49, north_of, gwi, gwo,
+    inner, got, g_in, g_out, ksum,
     pad, gp, kb, frame, fw, fe, strips, wmine, wpart, wnode, wall, kacc, kmine, kpart, kwide, kall,
-    pad_sem, bsend, brecv, s1, r1, s2, r2, s3, r3, s4, r4, s5, r5, s6, r6,
+    bsend, brecv, s1, r1, s2, r2, s3, r3, s4, r4, s5, r5, s6, r6,
 ):
     n = lax.axis_index("node")
     w = lax.axis_index("wide")
@@ -350,8 +417,6 @@
     barrier = pltpu.get_barrier_semaphore()
     for device in greet:
         pl.semaphore_signal(barrier, inc=1, device_id=device, device_id_type=MESH)
-    fetch = pltpu.make_async_copy(pad_hbm, pad, pad_sem)
-    fetch.start()
 
     def send(src, dst, send_sem, recv_sem, device):
         copy = pltpu.make_async_remote_copy(
@@ -380,7 +445,9 @@
 
     def fill(i, carry):
         o = pl.multiple_of((i + 3) * PITCH + 8, 8)
-        gp[pl.ds(o, TS), :] = gsrc[pl.ds(pl.multiple_of(i * TS, 32), TS), :].astype(F32)
+        here = pl.ds(pl.multiple_of(i * TS, 32), TS)
+        gp[pl.ds(o, TS), :] = gsrc[here, :].astype(F32)
+        pad[pl.ds(o, TS), :] = field[here, :].astype(F32)
         return carry
 
     lax.fori_loop(0, TS, fill, 0)
@@ -425,8 +492,7 @@
         north = frame[3 + q, 3 : 3 + TS, :]
         strips[5, here, :] = north.astype(BF16)
         for k in range(3):
-            mine = jnp.where(north_of[k : k + 1, :] > 0.0, south, north)
-            strips[k, here, :] = mine.astype(BF16)
+            strips[k, here, :] = jnp.where(north_of[4 + k : 5 + k, :] > 0, south, north).astype(BF16)
     borders = []
     for slot, source, device in peers:
         size = BAND if source in (3, 4) else STRIP
@@ -440,7 +506,6 @@
             )
         )
 
-    fetch.wait()
     pad[0:BAND, :] = hs[...]
     pad[99 * PITCH :, :] = hn[...]
 
@@ -453,24 +518,26 @@
 
     lax.fori_loop(0, TS, sides, 0)
     kmine[48:64, :] = jnp.zeros((16, C), BF16)
-    for b in range(7):
-
-        def taps(it, acc, b=b):
+    zero = jnp.zeros((8, C), F32)
+
+    def tap_column(b, carry):
+        def taps(it, acc):
             i0 = it * 4
             acc = list(acc)
             for jb in range(12):
                 g = [gp[pl.ds((i0 + d + 3) * PITCH + 8 + 8 * jb, 8), :] for d in range(4)]
-                for r in range(10):
-                    v = pad[pl.ds((i0 + r) * PITCH + 8 * jb + 5 + b, 8), :]
-                    for a in range(7):
-                        if 0 <= r - a < 4:
-                            acc[a] = acc[a] + g[r - a] * v
+                v = [pad[pl.ds((i0 + r) * PITCH + 8 * jb + 5 + b, 8), :] for r in range(10)]
+                for a in range(7):
+                    near = (g[0] * v[a] + g[1] * v[a + 1]) + (g[2] * v[a + 2] + g[3] * v[a + 3])
+                    acc[a] = acc[a] + near
             return tuple(acc)
 
-        zero = jnp.zeros((8, C), F32)
         acc = lax.fori_loop(0, 24, taps, (zero,) * 7)
         for a in range(7):
-            kacc[7 * a + b : 7 * a + b + 1, :] = jnp.sum(acc[a], axis=0, keepdims=True)
+            kacc[pl.ds(7 * a + b, 1), :] = jnp.sum(acc[a], axis=0, keepdims=True)
+        return carry
+
+    lax.fori_loop(0, 7, tap_column, 0)
     kacc[49:64, :] = jnp.zeros((15, C), F32)
     kmine[...] = (kacc[...] * GRAD_SCALE).astype(BF16)
 
@@ -512,17 +579,21 @@
     fourth = []
     for k, v in node_peers:
         fourth.append(send(kall.at[n], kall.at[n], s6.at[k], r6.at[k], (v, w)))
-    for v in range(WIDE):
-        wsum[v * 32 : (v + 1) * 32, :] = wall[v].astype(F32)
+    for v in range(16):
+        g_in[(v % 4) * 32 : (v % 4 + 1) * 32, (v // 4) * C : (v // 4 + 1) * C] = wall[v].astype(F32)
+    for k in range(4):
+        block = jnp.concatenate([wall[16 + 4 * k + v] for v in range(4)], axis=0)
+        g_out[k * C : (k + 1) * C, :] = block.astype(F32).T
     for copy in fourth:
         copy.wait()
-    for v in range(NODE):
+    for v in range(3):
         ksum[v * 16 : (v + 1) * 16, :] = kall[v].astype(F32)
+    ksum[48:49, :] = kall[3].astype(F32)[0:1, :]
     for copy in borders:
         copy.wait()
 
 
-def back_call(gsrc, pad, hw, he, hs, hn, k49, north_of, gwi, gwo):
+def back_call(gsrc, field, hw, he, hs, hn, k49, north_of, gwi, gwo):
     vmem = pl.BlockSpec(memory_space=pltpu.VMEM)
     dma = pltpu.SemaphoreType.DMA
     return pl.pallas_call(
@@ -530,11 +601,12 @@
         out_shape=(
             jax.ShapeDtypeStruct((CELLS, C), F32),
             jax.ShapeDtypeStruct((15, BAND, C), BF16),
-            jax.ShapeDtypeStruct((8 * C, C), F32),
-            jax.ShapeDtypeStruct((64, C), F32),
+            jax.ShapeDtypeStruct((C, HID), F32),
+            jax.ShapeDtypeStruct((HID, C), F32),
+            jax.ShapeDtypeStruct((49, C), F32),
         ),
-        in_specs=[vmem, pl.BlockSpec(memory_space=pl.ANY)] + [vmem] * 8,
-        out_specs=(vmem,) * 4,
+        in_specs=[vmem] * 10,
+        out_specs=(vmem,) * 5,
         scratch_shapes=[
             pltpu.VMEM((PADROWS * PITCH, C), F32),
             pltpu.VMEM((PADROWS * PITCH, C), F32),
@@ -552,7 +624,6 @@
             pltpu.VMEM((NODE, 16, C), BF16),
             pltpu.VMEM((WIDE, 16, C), BF16),
             pltpu.VMEM((NODE, 16, C), BF16),
-            dma,
             dma((15,)), dma((15,)),
             dma((WIDE,)), dma((WIDE,)),
             dma((NODE,)), dma((NODE,)),
@@ -565,7 +636,7 @@
             collective_id=1, has_side_effects=True, vmem_limit_bytes=VMEM_LIMIT
         ),
         name="back",
-    )(gsrc, pad, hw, he, hs, hn, k49, north_of, gwi, gwo)
+    )(gsrc, field, hw, he, hs, hn, k49, north_of, gwi, gwo)
 
 
 def final_kernel(pick, got, inner, cot, wc, out, cw, ce, low, top, strip, sb):
@@ -577,8 +648,8 @@
         ce[...] = jnp.zeros_like(ce)
 
         def chosen(direction, start, size):
-            v = got[pick[direction], pl.ds(start, size), :].astype(F32)
-            return jnp.where(pick[8 + direction] > 0, v, 0.0)
+            v = got[pick[0, direction], pl.ds(start, size), :].astype(F32)
+            return jnp.where(pick[1, direction] > 0, v, 0.0)
 
         for side, (mid, north, south), col in ((cw, (2, 4, 6), 0), (ce, (3, 5, 7), 5)):
             for q in range(3):
@@ -593,9 +664,9 @@
         turn = (i0 + i1 == TS - 1).astype(BF16)
         for q in range(3):
             low[q * TS : (q + 1) * TS, :] = chosen(1, q * TS, TS)
-            flipped = mm(turn, got[pick[16], (2 - q) * TS : (3 - q) * TS, :])
-            north = jnp.where(pick[17] > 0, flipped, chosen(0, q * TS, TS))
-            top[q * TS : (q + 1) * TS, :] = jnp.where(pick[8] > 0, north, 0.0)
+            flipped = mm(turn, got[pick[2, 0], (2 - q) * TS : (3 - q) * TS, :])
+            north = jnp.where(pick[3, 0] > 0, flipped, chosen(0, q * TS, TS))
+            top[q * TS : (q + 1) * TS, :] = jnp.where(pick[1, 0] > 0, north, 0.0)
 
     sb[...] = inner[...]
     for r in range(8):
@@ -653,56 +724,25 @@
     weight_out,
     layer_scale,
 ):
-    n = lax.axis_index("node")
-    w = lax.axis_index("wide")
-    tile = slot_tile[n * WIDE + w]
-    row = jnp.maximum(tile, 0) // WIDE
-    cell_row = jnp.arange(CELLS, dtype=jnp.int32) // TS
-    global_row = row * TS + cell_row
-    latitude = -80.0 + 160.0 * (global_row.astype(F32) + 0.5) / float(8 * TS)
-    metric = jnp.cos(latitude * (math.pi / 180.0))[None, :]
-    near = jnp.where(tile >= 0, neighbours[jnp.maximum(tile, 0)], -1)
-    present = near >= 0
-    target = jnp.maximum(near, 0) // 2
-    slot_ids = jnp.arange(NODE * WIDE, dtype=jnp.int32)
-    owner = jnp.sum(
-        jnp.where(slot_tile[None, :] == target[:, None], slot_ids[None, :], 0), axis=-1
-    )
-    turn = (n - owner // WIDE + NODE) % NODE
-    base = jnp.array([-1, -1, 7, 3, 7, 3, 7, 3], jnp.int32)
-    slot = jnp.where(present, jnp.maximum(base + turn, 0), 0)
-    flip = jnp.where(present[0], near[0] % 2, 0)
-    pick = jnp.concatenate(
-        [
-            slot.at[0].set(jnp.where(flip > 0, 0, slot[0])),
-            present.astype(jnp.int32),
-            jnp.stack([11 + turn[0], flip]),
-        ]
-    )
-    column = slot_tile[((n + jnp.arange(1, 4)) % NODE) * WIDE + w]
-    is_north = (column == target[1]) & present[1]
-    north_of = jnp.broadcast_to(
-        jnp.pad(is_north.astype(F32), (0, 5))[:, None], (8, C)
-    )
-    wc = wet_fraction * metric
     feat = features.reshape(C, CELLS)
     cot = cotangent.reshape(C, CELLS)
-    conv0, pad, got = halo_call(feat, wc, kernel, north_of)
+    conv0, field, got, wc, rmet, pick = halo_call(
+        feat, wet_fraction, kernel, slot_tile, neighbours
+    )
     updated, gsrc, gwi, gwo, hw, he, hs, hn = mlp_call(
-        pick, got, conv0, feat, cot, wet_fraction, 1.0 / metric, kernel, norm_gain, weight_in,
-        bias_in, weight_out, layer_scale,
+        pick, got, conv0, feat, cot, wet_fraction, rmet, kernel, norm_gain, weight_in, bias_in,
+        weight_out, layer_scale,
     )
-    inner, back_got, wsum, ksum = back_call(gsrc, pad, hw, he, hs, hn, kernel, north_of, gwi, gwo)
+    inner, back_got, grad_in, grad_out, ksum = back_call(
+        gsrc, field, hw, he, hs, hn, kernel, pick, gwi, gwo
+    )
     grad_features = final_call(pick, back_got, inner, cot, wc)
-    halves = wsum.reshape(2, 4, C, C)
-    grad_in = jnp.transpose(halves[0], (1, 0, 2)).reshape(C, HID)
-    grad_out = jnp.transpose(halves[1], (0, 2, 1)).reshape(HID, C)
     return (
         updated.reshape(1, C, CELLS),
         grad_features.reshape(1, C, CELLS),
         grad_in,
         grad_out,
-        ksum[:49],
+        ksum,
     )
 
 

time: 194 us -> 145 us (0.75)
  Pallas kernels: 167 us -> 140 us
  local copies, waits for them, and re-layouts: 14.6 us -> 3.51 us
  other arithmetic: 7.08 us -> 0 us
  between operations: 4.73 us -> 0.68 us
    pallas_call x1, Pallas kernels: 45.7 us -> 35.9 us  [mlp_call(): pl.pallas_call(mlp_kernel, out_shape=(jax.ShapeDtypeStruct((C, CELLS), BF...]
    pallas_call x1, Pallas kernels: 42.1 us -> 32.3 us  [halo_call(): pl.pallas_call(halo_kernel, out_shape=(jax.ShapeDtypeStruct((CELLS, C), F...]
    pallas_call x1, Pallas kernels: 68.2 us -> 60.4 us  [back_call(): pl.pallas_call(back_kernel, out_shape=(jax.ShapeDtypeStruct((CELLS, C), F...]
    broadcast_in_dim x4 -> x0, local copies, waits for them, and re-layouts: 4.89 us -> none  [the longest x1 1.52 us: mlp_call(): jnp.broadcast_to(bias[:, None], (HID, C))]
    div x2 -> x0, other arithmetic: 2.57 us -> none  [the longest x1 2.46 us: local(): 1.0 / metric]
    slice x5 -> x0, local copies, waits for them, and re-layouts: 2.27 us -> none  [the longest x2 1.11 us: local(): is_north = (column == target[1]) & present[1]]
where the time goes in v2:
time: 145 us; the launch traced here: 144 us
  Pallas kernels  140 us (97%)
  local copies, waits for them, and re-layouts  3.51 us (2%)
    pallas_call x1, Pallas kernels, back_call(): pl.pallas_call(back_kernel, out_shape=(jax.ShapeDtypeStruct((CELLS, C), F...  60.4 us
    pallas_call x1, Pallas kernels, mlp_call(): pl.pallas_call(mlp_kernel, out_shape=(jax.ShapeDtypeStruct((C, CELLS), BF...  35.9 us
    pallas_call x1, Pallas kernels, halo_call(): pl.pallas_call(halo_kernel, out_shape=(jax.ShapeDtypeStruct((CELLS, C), F...  32.3 us
    pallas_call x1, Pallas kernels, final_call(): pl.pallas_call(final_kernel, out_shape=jax.ShapeDtypeStruct((C, CELLS), B...  11.3 us
    unnamed x10, local copies, waits for them, and re-layouts  3.51 us

profile of v2, /device:TPU:1, one launch (start us, length us, event | category | flops | bytes accessed | tf_op | source)
XLA Modules:
  0.0 144.0 jit_solution(8708525483120729233)
XLA Ops:
  0.6 1.5 %copy.16.neighbours = s32[256,8]{1,0:T(8,128)} copy(s32[256,8]{0,1:T(8,128)} %param.15) | data formatting | bytes 16384 | tf_op args[4]
  2.1 32.3 %halo.1 = (f32[9216,128]{1,0:T(8,128)}, bf16[9216,128]{1,0:T(8,128)(2,1)}, bf16[15,288,128]{2,1,0:T(8,128)(2,1)}, f32[1,9216]{1,0:T(1,128)}, f32[1,9216]{1,0:T(1,128)}, /*index=5*/s32[8,128]{1,0:T(8,128)}) custom-call(bf16[128,9216]{1,0:T(8,128)(2,1)} %bitcast.9, f32[1,9216]{1,0:T(1,128)} %wet.3, f32[49,128]{1,0:T(8,128)} %k49.5, s32[128]{0:T(128)} %slot_tile.1, ...), custom_call_target="tpu_custom_call" | custom-call | tf_op jit(solution)/shard_map/halo/pallas_call | solution.py:199
  34.5 35.9 %mlp.1 = (bf16[128,9216]{1,0:T(8,128)(2,1)}, bf16[9216,128]{1,0:T(8,128)(2,1)}, f32[128,512]{1,0:T(8,128)}, f32[128,512]{1,0:T(8,128)}, f32[1632,128]{1,0:T(8,12...) custom-call(s32[8,128]{1,0:T(8,128)} %get-tuple-element.24.pick.north_of, ...), custom_call_target="tpu_custom_call" | custom-call | tf_op jit(solution)/shard_map/mlp/pallas_call | solution.py:362
  70.3 60.4 %back.1 = (f32[9216,128]{1,0:T(8,128)}, bf16[15,336,128]{2,1,0:T(8,128)(2,1)}, f32[128,512]{1,0:T(8,128)}, f32[512,128]{1,0:T(8,128)}, f32[49,128]{1,0:T(8,128)}) custom-call(bf16[9216,128]{1,0:T(8,128)(2,1)} %get-tuple-element.29.gsrc, bf16[9216,128]{1,0:T(8,128)(2,1)} %get-tuple-element.30.field, f32[1632,128]{1,0:T(8,128)} %get-tuple-element.31.hw, ...), custom_call_target="tpu_custom_call" | custom-call | tf_op jit(solution)/shard_map/back/pallas_call | solution.py:599
  130.7 0.0 copy-start.1
  130.7 0.0 copy-start
  130.7 0.0 copy-start.2
  130.7 11.3 %final.1 = bf16[128,9216]{1,0:T(8,128)(2,1)} custom-call(s32[8,128]{1,0:T(8,128)} %get-tuple-element.24.pick.north_of, bf16[15,336,128]{2,1,0:T(8,128)(2,1)} %get-tuple-element.37.got, f32[9216,128]{1,0:T(8,128)} %get-tuple-element.38.inner, bf16[128,9216]{1,0:T(8,128)(2,1)} %bitcast.8, f32[1,9216]{1,0:T(1,128)} %get-tuple-element.39.wc), custom_call_target="tpu_custom_call" | custom-call | tf_op jit(solution)/shard_map/final/pallas_call | solution.py:692
  142.0 0.0 copy-done.1
  142.0 0.7 copy.20
  142.7 0.0 copy-done
  142.7 0.7 copy.21
  143.4 0.0 copy-done.2
  143.4 0.6 copy.22
Async XLA Ops:
  130.7 11.3 %copy-start.1 = (f32[128,512]{1,0:T(8,128)S(1)}, f32[128,512]{1,0:T(8,128)}, u32[]{:S(2)}) copy-start(f32[128,512]{1,0:T(8,128)} %get-tuple-element.50) | copy-start | bytes 786436
  130.7 12.0 %copy-start = (f32[512,128]{1,0:T(8,128)S(1)}, f32[512,128]{1,0:T(8,128)}, u32[]{:S(2)}) copy-start(f32[512,128]{1,0:T(8,128)} %get-tuple-element.51) | copy-start | bytes 786436
  130.7 12.7 %copy-start.2 = (f32[49,128]{1,0:T(8,128)S(1)}, f32[49,128]{1,0:T(8,128)}, u32[]{:S(2)}) copy-start(f32[49,128]{1,0:T(8,128)} %get-tuple-element.52) | copy-start | bytes 75268

commit v3 on v2

v3 whole, which is shorter than its diff:
```python
import math

import jax
import jax.numpy as jnp
from jax import lax
from jax.experimental import pallas as pl
from jax.experimental.pallas import tpu as pltpu
from jax.sharding import PartitionSpec as P

C = 128
HID = 512
TS = 96
CELLS = TS * TS
NODE = 4
WIDE = 32
PITCH = 112
PADROWS = TS + 6
STRIP = 3 * TS
BAND = 3 * PITCH
BLOCK = 768
CHUNK = 256
EPS = 1e-06
GELU_COEF = 0.7978845608028654
CUBIC = 0.044715
GRAD_SCALE = 1.0 / math.sqrt(NODE * WIDE * CELLS)
MESH = pl.DeviceIdType.MESH
F32 = jnp.float32
BF16 = jnp.bfloat16
VMEM_LIMIT = 60 * 2**20


def border_peers(n, w):
    out = []
    for k in range(1, 4):
        out.append((k - 1, k - 1, (lax.rem(n + k, 4), w)))
    sides = ((3, 3, lax.rem(w + 31, 32)), (7, 4, lax.rem(w + 1, 32)), (11, 5, 31 - w))
    for base, source, column in sides:
        for k in range(4):
            out.append((base + k, source, (lax.rem(n + k, 4), column)))
    return out


def broadcast_taps(k49, kb):
    for t in range(49):
        kb[t] = jnp.broadcast_to(k49[t : t + 1, :], (8, C))


def taps_columns(src, kb, out, flip, low, high):
    def body(it, carry):
        b = it // 12
        i0 = lax.rem(it, 12) * 8
        taps = [kb[48 - 7 * a - b] if flip else kb[7 * a + b] for a in range(7)]
        for jb in range(12):
            base = i0 * PITCH + 8 * jb + 5 + b
            v = [src[pl.ds(base + r * PITCH, 8), :] for r in range(14)]
            for d in range(8):
                total = taps[0] * v[d]
                for a in range(1, 7):
                    total = total + taps[a] * v[d + a]
                o = pl.ds(pl.multiple_of((i0 + d) * TS + 8 * jb, 8), 8)
                out[o, :] = out[o, :] + total
        return carry

    lax.fori_loop(low * 12, high * 12, body, 0)


def clear_rows(out):
    zero = jnp.zeros((TS, C), F32)

    def body(i, carry):
        out[pl.ds(pl.multiple_of(i * TS, 8), TS), :] = zero
        return carry

    lax.fori_loop(0, TS, body, 0)


def clear_margins(pad):
    zero8 = jnp.zeros((8, C), F32)
    zero_row = jnp.zeros((PITCH, C), F32)
    for r in (0, 1, 2, 99, 100, 101):
        pad[r * PITCH : (r + 1) * PITCH, :] = zero_row

    def body(i, carry):
        o = pl.multiple_of((i + 3) * PITCH, 8)
        pad[pl.ds(o, 8), :] = zero8
        pad[pl.ds(o + 104, 8), :] = zero8
        return carry

    lax.fori_loop(0, TS, body, 0)


def cosine(x):
    x2 = x * x
    total = jnp.full_like(x, 1.0 / math.factorial(16))
    for k in range(7, -1, -1):
        total = total * x2 + (-1.0) ** k / math.factorial(2 * k)
    return total


def nt(a, b):
    return lax.dot_general(a, b, (((1,), (1,)), ((), ())), preferred_element_type=F32)


def mm(a, b):
    return jnp.dot(a, b, preferred_element_type=F32)


def wide2(column):
    return jnp.concatenate([column, column], axis=1)


def find_neighbours(n, w, slot_tile, neighbours):
    tile = slot_tile[n * WIDE + w]
    known = jnp.maximum(tile, 0)
    columns = {0: w, 3: lax.rem(w + 1, 32), 7: lax.rem(w + 31, 32), 11: 31 - w}
    held = {key: [slot_tile[k * WIDE + col] for k in range(4)] for key, col in columns.items()}
    bases = (0, 0, 7, 3, 7, 3, 7, 3)
    slots, present, targets = [], [], []

    def find(base, target):
        slot = jnp.int32(0)
        for k in range(4):
            away = lax.rem(n + 4 - k, 4)
            here = jnp.maximum(away - 1, 0) if base == 0 else base + away
            slot = jnp.where(held[base][k] == target, here, slot)
        return slot

    for d in range(8):
        near = jnp.where(tile >= 0, neighbours[known * 8 + d], -1)
        present.append(near >= 0)
        targets.append(jnp.maximum(near, 0) >> 1)
        slots.append(find(bases[d], targets[d]))
        if d == 0:
            flip = near & 1
    mirror = find(11, targets[0])
    north_of = []
    for k in range(1, 4):
        other = slot_tile[lax.rem(n + k, 4) * WIDE + w]
        north_of.append(present[1] & (other == targets[1]))
    return known, slots, present, mirror, present[0] & (flip == 1), north_of


def block_kernel(
    feat_hbm, cot_hbm, wet, k49, slot_tile, neighbours, gain_row, w_in, bias_row, w_out, scale_row,
    updated_hbm, grad_hbm, g_in, g_out, ksum,
    feat, cot, updated, grad, wc, rmet, pad, gp, cells, kb, strips, got, hw, he, hs, hn, strip,
    gain, scale, bias, w_in_t, w_out_t, gwi, gwo, frame, fw, fe, back_strips, back_got, cw, ce,
    kx, wmine, part8, mine4, part4, nodes, all4, wall,
    in_sem, up_sem, gr_sem, fsend, frecv, bsend, brecv, s1, r1, s2, r2, s3, r3, s4, r4, s5, r5,
):
    n = lax.axis_index("node")
    w = lax.axis_index("wide")
    x = w // 8
    z = lax.rem(w, 8)
    peers = border_peers(n, w)
    z_peers = [(k, lax.rem(z + k, 8)) for k in range(1, 8)]
    x_peers = [(k, lax.rem(x + k, 4)) for k in range(1, 4)]
    n_peers = [(k, lax.rem(n + k, 4)) for k in range(1, 4)]
    greet = [device for _, _, device in peers]
    greet += [(n, x * 8 + v) for _, v in z_peers] + [(n, v * 8 + z) for _, v in x_peers]
    barrier = pltpu.get_barrier_semaphore()
    for device in greet:
        pl.semaphore_signal(barrier, inc=1, device_id=device, device_id_type=MESH)
    fetch = [
        pltpu.make_async_copy(feat_hbm, feat, in_sem.at[0]),
        pltpu.make_async_copy(cot_hbm, cot, in_sem.at[1]),
    ]
    for copy in fetch:
        copy.start()

    def send(src, dst, send_sem, recv_sem, device):
        copy = pltpu.make_async_remote_copy(
            src_ref=src,
            dst_ref=dst,
            send_sem=send_sem,
            recv_sem=recv_sem,
            device_id=device,
            device_id_type=MESH,
        )
        copy.start()
        return copy

    known, slots, present, mirror, folded, north_of = find_neighbours(n, w, slot_tile, neighbours)
    broadcast_taps(k49, kb)
    clear_margins(pad)
    clear_margins(gp)
    clear_rows(cells)
    cell = lax.broadcasted_iota(jnp.int32, (1, 384), 1)
    sub_row = jnp.where(cell >= 96, 1.0, 0.0) + jnp.where(cell >= 192, 1.0, 0.0)
    sub_row = sub_row + jnp.where(cell >= 288, 1.0, 0.0)
    first_row = ((known >> 5) * TS).astype(F32) + 0.5
    fetch[0].wait()

    def prep(g, carry):
        here = pl.ds(pl.multiple_of(g * 384, 128), 384)
        latitude = -80.0 + 160.0 * (sub_row + ((g * 4).astype(F32) + first_row)) / float(8 * TS)
        metric = cosine(latitude * (math.pi / 180.0))
        weight = wet[:, here] * metric
        wc[:, here] = weight
        rmet[:, here] = 1.0 / metric
        t = (feat[:, here].astype(F32) * weight).astype(BF16).astype(F32).T
        for r in range(4):
            row = pl.multiple_of((g * 4 + r + 3) * PITCH + 8, 8)
            pad[pl.ds(row, TS), :] = t[r * TS : (r + 1) * TS]
        return carry

    lax.fori_loop(0, 2, lambda g, carry: prep(g * 23, carry), 0)
    for q in range(3):
        here = pl.ds(q * TS, TS)
        south = pad[pl.ds((3 + q) * PITCH + 8, TS), :]
        north = pad[pl.ds((96 + q) * PITCH + 8, TS), :]
        strips[5, here, :] = north.astype(BF16)
        for k in range(3):
            strips[k, here, :] = jnp.where(north_of[k], south, north).astype(BF16)
    pl.semaphore_wait(barrier, len(greet))
    copies = []

    def send_strips(sources):
        for slot, source, device in peers:
            if source in sources:
                copies.append(
                    send(strips.at[source], got.at[slot], fsend.at[slot], frecv.at[slot], device)
                )

    send_strips((0, 1, 2, 5))
    lax.fori_loop(1, 23, prep, 0)
    for q in range(3):
        here = pl.ds(q * TS, TS)
        strips[3, here, :] = pad[pl.ds(3 * PITCH + 8 + q, TS, stride=PITCH), :].astype(BF16)
        strips[4, here, :] = pad[pl.ds(3 * PITCH + 101 + q, TS, stride=PITCH), :].astype(BF16)
    send_strips((3, 4))

    taps_columns(pad, kb, cells, False, 0, 7)
    gain[...] = jnp.broadcast_to(gain_row[...], (C, C)).T
    scale[...] = jnp.broadcast_to(scale_row[...], (C, C)).T
    for k in range(4):
        here = slice(k * C, (k + 1) * C)
        bias[here, :] = jnp.broadcast_to(bias_row[:, here], (C, C)).T
        w_in_t[here, :] = w_in[:, here].astype(F32).T.astype(BF16)
        w_out_t[:, here] = w_out[here, :].astype(F32).T.astype(BF16)
    gwi[...] = jnp.zeros_like(gwi)
    gwo[...] = jnp.zeros_like(gwo)
    hw[...] = jnp.zeros_like(hw)
    he[...] = jnp.zeros_like(he)
    i0 = lax.broadcasted_iota(jnp.int32, (TS, TS), 0)
    i1 = lax.broadcasted_iota(jnp.int32, (TS, TS), 1)
    turn = (i0 + i1 == TS - 1).astype(BF16)
    for copy in copies:
        copy.wait()

    def chosen(direction, q):
        v = got[slots[direction], pl.ds(q * TS, TS), :].astype(F32)
        return jnp.where(present[direction], v, 0.0)

    for side, (mid, top, low), col in ((hw, (2, 4, 6), 5), (he, (3, 5, 7), 8)):
        for q in range(3):
            strip[0:TS, :] = chosen(low, q)
            strip[0:3, :] = strip[TS - 3 : TS, :]
            strip[3 : TS + 3, :] = chosen(mid, q)
            strip[112 : 112 + TS, :] = chosen(top, q)
            strip[TS + 3 : TS + 6, :] = strip[112:115, :]
            side[pl.ds(col + q, PADROWS, stride=16), :] = strip[0:PADROWS, :]
    for q in range(3):
        o = q * PITCH
        hs[o + 8 : o + 104, :] = chosen(1, q)
        hs[o : o + 8, :] = hw[q * 16 : q * 16 + 8, :]
        hs[o + 104 : o + 112, :] = he[q * 16 + 8 : q * 16 + 16, :]
        flipped = mm(turn, got[mirror, pl.ds((2 - q) * TS, TS), :])
        north = jnp.where(folded, flipped, chosen(0, q))
        hn[o + 8 : o + 104, :] = jnp.where(present[0], north, 0.0)
        r = (TS + 3 + q) * 16
        hn[o : o + 8, :] = hw[r : r + 8, :]
        hn[o + 104 : o + 112, :] = he[r + 8 : r + 16, :]
    pad[0:BAND, :] = hs[...]
    pad[99 * PITCH :, :] = hn[...]

    def rim(rows, pairs):
        def body(jb, carry):
            j0 = pl.multiple_of(jb * 8, 8)
            for d, terms in pairs:
                o = pl.ds(pl.multiple_of(d * TS + j0, 8), 8)
                total = cells[o, :]
                for a, r in terms:
                    part = None
                    for b in range(7):
                        v = kb[7 * a + b] * rows[pl.ds(r * PITCH + j0 + 5 + b, 8), :]
                        part = v if part is None else part + v
                    total = total + part
                cells[o, :] = total
            return carry

        lax.fori_loop(0, 12, body, 0)

    rim(hs, [(i, [(a, i + a) for a in range(3 - i)]) for i in range(3)])
    rim(hn, [(93 + i, [(a, i + a - 6) for a in range(6 - i, 7)]) for i in range(3)])

    def sides(i, carry):
        p = pl.multiple_of((i + 3) * PITCH, 8)
        r = pl.multiple_of((i + 3) * 16, 8)
        pad[pl.ds(p, 8), :] = hw[pl.ds(r, 8), :]
        pad[pl.ds(p + 104, 8), :] = he[pl.ds(r + 8, 8), :]
        for side, taps, shift, col in ((hw, (0, 1, 2), 5, 0), (he, (4, 5, 6), -3, 88)):
            o = pl.ds(pl.multiple_of(i * TS + col, 8), 8)
            total = cells[o, :]
            for a in range(7):
                row = i + a
                inside = jnp.logical_and(row >= 3, row < TS + 3).astype(F32)
                part = None
                for b in taps:
                    v = kb[7 * a + b] * side[pl.ds(row * 16 + b + shift, 8), :]
                    part = v if part is None else part + v
                total = total + part * inside
            cells[o, :] = total
        return carry

    lax.fori_loop(0, TS, sides, 0)
    fetch[1].wait()

    def mlp_block(step, carry):
        for c in range(BLOCK // CHUNK):
            here = pl.ds(pl.multiple_of(step * BLOCK + c * CHUNK, CHUNK), CHUNK)
            rm = rmet[:, here]
            conv = cells[here, :].T * rm
            centred = conv - jnp.mean(conv, axis=0, keepdims=True)
            inv_std = lax.rsqrt(jnp.mean(centred * centred, axis=0, keepdims=True) + EPS)
            normed = centred * inv_std
            g2 = wide2(gain[...])
            normed_bf = (normed * g2).astype(BF16)
            hidden = mm(w_in_t[...], normed_bf) + wide2(bias[...])
            sq = hidden * hidden
            t = jnp.tanh(hidden * (GELU_COEF + (GELU_COEF * CUBIC) * sq))
            p = 0.5 + 0.5 * t
            active = hidden * p
            active_bf = active.astype(BF16)
            mixed = mm(w_out_t[...], active_bf)
            ms = wet[:, here] * wide2(scale[...])
            updated[:, here] = (feat[:, here].astype(F32) + ms * mixed).astype(BF16)
            gm = (ms * cot[:, here].astype(F32)).astype(BF16)
            slope = p + active * (1.0 - p) * (2.0 * GELU_COEF + (6.0 * GELU_COEF * CUBIC) * sq)
            gh = (mm(w_out[...], gm) * slope).astype(BF16)
            gn = mm(w_in[...], gh) * g2
            gwo[...] += nt(gm, active_bf)
            gwi[...] += nt(normed_bf, gh)
            gc = inv_std * (
                gn
                - jnp.mean(gn, axis=0, keepdims=True)
                - normed * jnp.mean(gn * normed, axis=0, keepdims=True)
            )
            gs = (gc * rm).T.astype(BF16).astype(F32)
            for r in range(8):
                low, high = max(c * CHUNK, r * TS), min((c + 1) * CHUNK, (r + 1) * TS)
                if low < high:
                    o = pl.multiple_of((step * 8 + r + 3) * PITCH + 8 + low - r * TS, 8)
                    gp[pl.ds(o, high - low), :] = gs[low - c * CHUNK : high - c * CHUNK]
        return carry

    lax.fori_loop(0, CELLS // BLOCK, mlp_block, 0)
    out_updated = pltpu.make_async_copy(updated, updated_hbm, up_sem)
    out_updated.start()

    def frame_rows(jb, carry):
        j0 = pl.multiple_of(jb * 8, 8)
        for f, p in enumerate((0, 1, 2, 99, 100, 101)):
            total = None
            for a in range(7):
                if 0 <= p - a < TS:
                    for b in range(7):
                        v = kb[7 * a + b] * gp[pl.ds((p - a + 3) * PITCH + j0 + 8 - b, 8), :]
                        total = v if total is None else total + v
            frame[f, pl.ds(j0, 8), :] = total
        return carry

    lax.fori_loop(0, 13, frame_rows, 0)

    def frame_cols(i, carry):
        p = i + 3
        for side, taps, q0 in ((fw, (0, 1, 2), 0), (fe, (4, 5, 6), 96)):
            total = None
            for a in range(7):
                for b in taps:
                    v = kb[7 * a + b] * gp[pl.ds((p - a + 3) * PITCH + q0 + 8 - b, 8), :]
                    total = v if total is None else total + v
            side[pl.ds(pl.multiple_of(p * 8, 8), 8), :] = total
        return carry

    lax.fori_loop(0, TS, frame_cols, 0)
    for f, p in enumerate((0, 1, 2, 99, 100, 101)):
        fw[p * 8 : p * 8 + 8, :] = frame[f, 0:8, :]
        fe[p * 8 : p * 8 + 8, :] = frame[f, 96:104, :]
    fw[PADROWS * 8 :, :] = jnp.zeros((80, C), F32)
    fe[PADROWS * 8 :, :] = jnp.zeros((80, C), F32)
    for q in range(3):
        here = pl.ds(q * PITCH, PITCH)
        back_strips[3, here, :] = fw[pl.ds(q, PITCH, stride=8), :].astype(BF16)
        back_strips[4, here, :] = fe[pl.ds(3 + q, PITCH, stride=8), :].astype(BF16)
        here = pl.ds(q * TS, TS)
        south = frame[q, 3 : 3 + TS, :]
        north = frame[3 + q, 3 : 3 + TS, :]
        back_strips[5, here, :] = north.astype(BF16)
        for k in range(3):
            back_strips[k, here, :] = jnp.where(north_of[k], south, north).astype(BF16)
    borders = []
    for slot, source, device in peers:
        size = BAND if source in (3, 4) else STRIP
        borders.append(
            send(
                back_strips.at[source, pl.ds(0, size)],
                back_got.at[slot, pl.ds(0, size)],
                bsend.at[slot],
                brecv.at[slot],
                device,
            )
        )

    kx[...] = jnp.zeros_like(kx)
    zero = jnp.zeros((8, C), F32)

    def tap_column(b, carry):
        def taps(it, acc):
            i0 = it * 4
            acc = list(acc)
            for jb in range(12):
                g = [gp[pl.ds((i0 + d + 3) * PITCH + 8 + 8 * jb, 8), :] for d in range(4)]
                v = [pad[pl.ds((i0 + r) * PITCH + 8 * jb + 5 + b, 8), :] for r in range(10)]
                for a in range(7):
                    near = (g[0] * v[a] + g[1] * v[a + 1]) + (g[2] * v[a + 2] + g[3] * v[a + 3])
                    acc[a] = acc[a] + near
            return tuple(acc)

        acc = lax.fori_loop(0, 24, taps, (zero,) * 7)
        for a in range(7):
            t = 7 * a + b
            row = (t // 2) * 16 + lax.rem(t, 2)
            kx[pl.ds(row, 1), :] = jnp.sum(acc[a], axis=0, keepdims=True)
        return carry

    lax.fori_loop(0, 7, tap_column, 0)

    for c in range(32):
        acc = gwi if c < 16 else gwo
        part = acc[(c % 4) * 32 : (c % 4 + 1) * 32, (c // 4 % 4) * C : (c // 4 % 4 + 1) * C]
        wmine[c * 48 : c * 48 + 32, :] = (part * GRAD_SCALE).astype(BF16)
        wmine[c * 48 + 32 : c * 48 + 48, :] = (kx[c * 16 : c * 16 + 16, :] * GRAD_SCALE).astype(BF16)
    stage = []
    for k, v in z_peers:
        src = wmine.at[pl.ds(pl.multiple_of(v * 192, 64), 192)]
        stage.append(send(src, part8.at[k], s1.at[k], r1.at[k], (n, x * 8 + v)))
    clear_rows(cells)
    taps_columns(gp, kb, cells, True, 0, 2)
    for copy in stage:
        copy.wait()
    total = wmine[pl.ds(pl.multiple_of(z * 192, 64), 192), :].astype(F32)
    for k in range(1, 8):
        total = total + part8[k].astype(F32)
    mine4[...] = total
    stage = []
    for k, v in x_peers:
        src = mine4.at[pl.ds(pl.multiple_of(v * 48, 16), 48)]
        stage.append(send(src, part4.at[k], s2.at[k], r2.at[k], (n, v * 8 + z)))
    taps_columns(gp, kb, cells, True, 2, 3)
    for copy in stage:
        copy.wait()
    total = mine4[pl.ds(pl.multiple_of(x * 48, 16), 48), :]
    for k in range(1, 4):
        total = total + part4[k]
    nodes[n] = total
    stage = []
    for k, v in n_peers:
        stage.append(send(nodes.at[n], nodes.at[n], s3.at[k], r3.at[k], (v, w)))
    taps_columns(gp, kb, cells, True, 3, 4)
    for copy in stage:
        copy.wait()
    all4[x] = ((nodes[0] + nodes[1]) + (nodes[2] + nodes[3])).astype(BF16)
    stage = []
    for k, v in x_peers:
        stage.append(send(all4.at[x], all4.at[x], s4.at[k], r4.at[k], (n, v * 8 + z)))
    taps_columns(gp, kb, cells, True, 4, 5)
    for copy in stage:
        copy.wait()
    for v in range(4):
        wall[z, v * 48 : (v + 1) * 48, :] = all4[v]
    stage = []
    for k, v in z_peers:
        stage.append(send(wall.at[z], wall.at[z], s5.at[k], r5.at[k], (n, x * 8 + v)))
    taps_columns(gp, kb, cells, True, 5, 7)
    for copy in borders:
        copy.wait()

    cw[...] = jnp.zeros_like(cw)
    ce[...] = jnp.zeros_like(ce)

    def received(direction, start, size):
        v = back_got[slots[direction], pl.ds(start, size), :].astype(F32)
        return jnp.where(present[direction], v, 0.0)

    for side, (mid, north, south), col in ((cw, (2, 4, 6), 0), (ce, (3, 5, 7), 5)):
        for q in range(3):
            strip[0:PITCH, :] = received(mid, q * PITCH, PITCH)
            strip[PITCH : 2 * PITCH, :] = received(north, q * PITCH, PITCH)
            strip[2 * PITCH :, :] = received(south, q * PITCH, PITCH)
            strip[TS : TS + 3, :] += strip[PITCH : PITCH + 3, :]
            strip[3:6, :] += strip[2 * PITCH + TS + 3 : 2 * PITCH + TS + 6, :]
            side[pl.ds(col + q, TS, stride=8), :] = strip[3 : TS + 3, :]
    for q in range(3):
        cells[q * TS : (q + 1) * TS, :] += received(1, q * TS, TS)
        flipped = mm(turn, back_got[mirror, pl.ds((2 - q) * TS, TS), :])
        north = jnp.where(folded, flipped, received(0, q * TS, TS))
        cells[(93 + q) * TS : (94 + q) * TS, :] += jnp.where(present[0], north, 0.0)

    def finish(step, carry):
        for r in range(8):
            i = step * 8 + r
            o = pl.multiple_of(i * TS, 8)
            row = pl.multiple_of(i * 8, 8)
            cells[pl.ds(o, 8), :] += cw[pl.ds(row, 8), :]
            cells[pl.ds(o + 88, 8), :] += ce[pl.ds(row, 8), :]
        here = pl.ds(pl.multiple_of(step * BLOCK, BLOCK), BLOCK)
        whole = cot[:, here].astype(F32) + wc[:, here] * cells[here, :].T
        grad[:, here] = whole.astype(BF16)
        return carry

    lax.fori_loop(0, CELLS // BLOCK, finish, 0)
    out_grad = pltpu.make_async_copy(grad, grad_hbm, gr_sem)
    out_grad.start()
    for copy in stage:
        copy.wait()
    for c in range(32):
        rows = slice((c % 4) * 48, (c % 4) * 48 + 32)
        if c < 16:
            g_in[(c % 4) * 32 : (c % 4 + 1) * 32, (c // 4) * C : (c // 4 + 1) * C] = wall[
                c // 4, rows, :
            ].astype(F32)
        elif c % 4 == 0:
            block = jnp.concatenate(
                [wall[c // 4, v * 48 : v * 48 + 32, :] for v in range(4)], axis=0
            )
            g_out[(c // 4 - 4) * C : (c // 4 - 3) * C, :] = block.astype(F32).T
        if c < 25:
            size = min(2, 49 - 2 * c)
            pair = wall[c // 4, (c % 4) * 48 + 32 : (c % 4) * 48 + 48, :].astype(F32)
            ksum[2 * c : 2 * c + size, :] = pair[0:size]
    out_updated.wait()
    out_grad.wait()


def block_call(*args):
    vmem = pl.BlockSpec(memory_space=pltpu.VMEM)
    smem = pl.BlockSpec(memory_space=pltpu.SMEM)
    hbm = pl.BlockSpec(memory_space=pl.ANY)
    dma = pltpu.SemaphoreType.DMA
    shapes = [
        ((C, CELLS), BF16), ((C, CELLS), BF16), ((C, CELLS), BF16), ((C, CELLS), BF16),
        ((1, CELLS), F32), ((1, CELLS), F32),
        ((PADROWS * PITCH, C), F32), ((PADROWS * PITCH, C), F32), ((CELLS, C), F32),
        ((49, 8, C), F32), ((6, STRIP, C), BF16), ((15, STRIP, C), BF16),
        ((PADROWS * 16, C), F32), ((PADROWS * 16, C), F32), ((BAND, C), F32), ((BAND, C), F32),
        ((3 * PITCH, C), F32),
        ((C, C), F32), ((C, C), F32), ((HID, C), F32), ((HID, C), BF16), ((C, HID), BF16),
        ((C, HID), F32), ((C, HID), F32),
        ((6, 104, C), F32), ((PITCH * 8, C), F32), ((PITCH * 8, C), F32),
        ((6, BAND, C), BF16), ((15, BAND, C), BF16), ((TS * 8, C), F32), ((TS * 8, C), F32),
        ((512, C), F32), ((1536, C), BF16), ((8, 192, C), BF16), ((192, C), F32),
        ((4, 48, C), F32), ((4, 48, C), F32), ((4, 48, C), BF16), ((8, 192, C), BF16),
    ]
    sems = [dma((2,)), dma, dma, dma((15,)), dma((15,)), dma((15,)), dma((15,))]
    sems += [dma((8,)), dma((8,))] + [dma((4,))] * 6 + [dma((8,)), dma((8,))]
    return pl.pallas_call(
        block_kernel,
        out_shape=(
            jax.ShapeDtypeStruct((C, CELLS), BF16),
            jax.ShapeDtypeStruct((C, CELLS), BF16),
            jax.ShapeDtypeStruct((C, HID), F32),
            jax.ShapeDtypeStruct((HID, C), F32),
            jax.ShapeDtypeStruct((49, C), F32),
        ),
        in_specs=[hbm, hbm, vmem, vmem, smem, smem] + [vmem] * 5,
        out_specs=(hbm, hbm, vmem, vmem, vmem),
        scratch_shapes=[pltpu.VMEM(shape, dtype) for shape, dtype in shapes] + sems,
        compiler_params=pltpu.CompilerParams(
            collective_id=0, has_side_effects=True, vmem_limit_bytes=VMEM_LIMIT
        ),
        name="block",
    )(*args)


def local(
    features,
    cotangent,
    wet_fraction,
    slot_tile,
    neighbours,
    kernel,
    norm_gain,
    weight_in,
    bias_in,
    weight_out,
    layer_scale,
):
    updated, grad_features, grad_in, grad_out, grad_kernel = block_call(
        features.reshape(C, CELLS),
        cotangent.reshape(C, CELLS),
        wet_fraction,
        kernel,
        slot_tile,
        neighbours.reshape(-1),
        norm_gain[None, :],
        weight_in,
        bias_in[None, :],
        weight_out,
        layer_scale[None, :],
    )
    return (
        updated.reshape(1, C, CELLS),
        grad_features.reshape(1, C, CELLS),
        grad_in,
        grad_out,
        grad_kernel,
    )


def solution(mesh):
    shards = P(("node", "wide"), None, None)
    in_specs = (shards, shards, P(("node", "wide"), None)) + (P(),) * 8
    out_specs = (shards, shards, P(), P(), P())
    return jax.shard_map(local, mesh=mesh, in_specs=in_specs, out_specs=out_specs, check_vma=False)
```

time: 145 us -> 119 us (0.82)
  Pallas kernels: 140 us -> 109 us
  local copies, waits for them, and re-layouts: 3.51 us -> 8.34 us
    pallas_call x4 -> x1, Pallas kernels: 140 us -> 109 us  [block_call(): pl.pallas_call(block_kernel, out_shape=(jax.ShapeDtypeStruct((C, CELLS),...]
    unnamed x10 -> x14, local copies, waits for them, and re-layouts: 3.51 us -> 7.63 us
where the time goes in v3:
time: 119 us; the launch traced here: 118 us
  Pallas kernels  109 us (92%)
  local copies, waits for them, and re-layouts  8.34 us (7%)
    pallas_call x1, Pallas kernels, block_call(): pl.pallas_call(block_kernel, out_shape=(jax.ShapeDtypeStruct((C, CELLS),...  109 us
    unnamed x14, local copies, waits for them, and re-layouts  7.63 us

profile of v3, /device:TPU:1, one launch (start us, length us, event | category | flops | bytes accessed | tf_op | source)
XLA Modules:
  0.0 117.7 jit_solution(6934751640839465397)
XLA Ops:
  0.6 0.8 copy.16
  1.5 0.7 reshape.27.neighbours
  2.2 108.7 %block.1 = (bf16[128,9216]{1,0:T(8,128)(2,1)}, bf16[128,9216]{1,0:T(8,128)(2,1)}, f32[128,512]{1,0:T(8,128)}, f32[512,128]{1,0:T(8,128)}, f32[49,128]{1,0:T(8,128)}) custom-call(bf16[128,9216]{1,0:T(8,128)(2,1)} %bitcast.9, bf16[128,9216]{1,0:T(8,128)(2,1)} %bitcast.10, f32[1,9216]{1,0:T(1,128)} %wet.1, f32[49,128]{1,0:T(8,128)} %k49.1, s32[128]{0:T(128)} %slot_tile.1, ...), custom_call_target="tpu_custom_call" | custom-call | tf_op jit(solution)/shard_map/block/pallas_call | solution.py:567
  110.9 0.0 copy-start
  110.9 3.4 %copy.22 = bf16[1,128,9216]{2,1,0:T(8,128)(2,1)} copy(bf16[1,128,9216]{2,1,0:T(8,128)(2,1)} %bitcast.8) | data formatting | bytes 4718592
  114.3 0.0 copy-done
  114.3 0.0 copy-start.2
  114.3 0.0 copy-start.1
  114.3 0.0 copy-start.3
  114.3 1.4 %copy.23 = bf16[1,128,9216]{2,1,0:T(8,128)(2,1)} copy(bf16[1,128,9216]{2,1,0:T(8,128)(2,1)S(1)} %bitcast.7) | data formatting | bytes 4718592
  115.7 0.0 copy-done.2
  115.7 0.7 copy.24
  116.4 0.0 copy-done.1
  116.4 0.7 copy.25
  117.1 0.0 copy-done.3
  117.1 0.6 copy.26
Async XLA Ops:
  110.9 3.4 %copy-start = (bf16[128,9216]{1,0:T(8,128)(2,1)S(1)}, bf16[128,9216]{1,0:T(8,128)(2,1)}, u32[]{:S(2)}) copy-start(bf16[128,9216]{1,0:T(8,128)(2,1)} %get-tuple-element.11) | copy-start | bytes 7077892
  114.3 1.4 %copy-start.2 = (f32[128,512]{1,0:T(8,128)S(1)}, f32[128,512]{1,0:T(8,128)}, u32[]{:S(2)}) copy-start(f32[128,512]{1,0:T(8,128)} %get-tuple-element.22) | copy-start | bytes 786436
  114.3 2.1 %copy-start.1 = (f32[512,128]{1,0:T(8,128)S(1)}, f32[512,128]{1,0:T(8,128)}, u32[]{:S(2)}) copy-start(f32[512,128]{1,0:T(8,128)} %get-tuple-element.23) | copy-start | bytes 786436
  114.3 2.8 %copy-start.3 = (f32[49,128]{1,0:T(8,128)S(1)}, f32[49,128]{1,0:T(8,128)}, u32[]{:S(2)}) copy-start(f32[49,128]{1,0:T(8,128)} %get-tuple-element.24) | copy-start | bytes 75268

commit v4 on v3

--- a/solution.py
+++ b/solution.py
@@ -17,7 +17,7 @@
 PADROWS = TS + 6
 STRIP = 3 * TS
 BAND = 3 * PITCH
-BLOCK = 768
+BLOCK = 1536
 CHUNK = 256
 EPS = 1e-06
 GELU_COEF = 0.7978845608028654
@@ -105,6 +105,13 @@
     return jnp.dot(a, b, preferred_element_type=F32)
 
 
+def tree(parts):
+    while len(parts) > 1:
+        pairs = [parts[k] + parts[k + 1] for k in range(0, len(parts) - 1, 2)]
+        parts = pairs + parts[len(pairs) * 2 :]
+    return parts[0]
+
+
 def wide2(column):
     return jnp.concatenate([column, column], axis=1)
 
@@ -145,8 +152,9 @@
     updated_hbm, grad_hbm, g_in, g_out, ksum,
     feat, cot, updated, grad, wc, rmet, pad, gp, cells, kb, strips, got, hw, he, hs, hn, strip,
     gain, scale, bias, w_in_t, w_out_t, gwi, gwo, frame, fw, fe, back_strips, back_got, cw, ce,
-    kx, wmine, part8, mine4, part4, nodes, all4, wall,
+    wmine, part8, mine4, part4, nodes, all4, wall, kx, kmine, kz, kq, kn,
     in_sem, up_sem, gr_sem, fsend, frecv, bsend, brecv, s1, r1, s2, r2, s3, r3, s4, r4, s5, r5,
+    s6, r6, s7, r7, s8, r8,
 ):
     n = lax.axis_index("node")
     w = lax.axis_index("wide")
@@ -162,8 +170,8 @@
     for device in greet:
         pl.semaphore_signal(barrier, inc=1, device_id=device, device_id_type=MESH)
     fetch = [
-        pltpu.make_async_copy(feat_hbm, feat, in_sem.at[0]),
-        pltpu.make_async_copy(cot_hbm, cot, in_sem.at[1]),
+        pltpu.make_async_copy(feat_hbm.at[0], feat, in_sem.at[0]),
+        pltpu.make_async_copy(cot_hbm.at[0], cot, in_sem.at[1]),
     ]
     for copy in fetch:
         copy.start()
@@ -204,7 +212,12 @@
             pad[pl.ds(row, TS), :] = t[r * TS : (r + 1) * TS]
         return carry
 
-    lax.fori_loop(0, 2, lambda g, carry: prep(g * 23, carry), 0)
+    def prep_pair(g, carry):
+        prep(2 * g - 1, carry)
+        return prep(2 * g, carry)
+
+    prep(jnp.int32(0), 0)
+    prep(jnp.int32(23), 0)
     for q in range(3):
         here = pl.ds(q * TS, TS)
         south = pad[pl.ds((3 + q) * PITCH + 8, TS), :]
@@ -223,7 +236,7 @@
                 )
 
     send_strips((0, 1, 2, 5))
-    lax.fori_loop(1, 23, prep, 0)
+    lax.fori_loop(1, 12, prep_pair, 0)
     for q in range(3):
         here = pl.ds(q * TS, TS)
         strips[3, here, :] = pad[pl.ds(3 * PITCH + 8 + q, TS, stride=PITCH), :].astype(BF16)
@@ -294,96 +307,122 @@
     rim(hs, [(i, [(a, i + a) for a in range(3 - i)]) for i in range(3)])
     rim(hn, [(93 + i, [(a, i + a - 6) for a in range(6 - i, 7)]) for i in range(3)])
 
-    def sides(i, carry):
-        p = pl.multiple_of((i + 3) * PITCH, 8)
-        r = pl.multiple_of((i + 3) * 16, 8)
-        pad[pl.ds(p, 8), :] = hw[pl.ds(r, 8), :]
-        pad[pl.ds(p + 104, 8), :] = he[pl.ds(r + 8, 8), :]
-        for side, taps, shift, col in ((hw, (0, 1, 2), 5, 0), (he, (4, 5, 6), -3, 88)):
-            o = pl.ds(pl.multiple_of(i * TS + col, 8), 8)
-            total = cells[o, :]
-            for a in range(7):
-                row = i + a
-                inside = jnp.logical_and(row >= 3, row < TS + 3).astype(F32)
-                part = None
-                for b in taps:
-                    v = kb[7 * a + b] * side[pl.ds(row * 16 + b + shift, 8), :]
-                    part = v if part is None else part + v
-                total = total + part * inside
-            cells[o, :] = total
-        return carry
-
-    lax.fori_loop(0, TS, sides, 0)
+    def sides(g, carry):
+        for e in range(4):
+            i = g * 4 + e
+            p = pl.multiple_of((i + 3) * PITCH, 8)
+            r = pl.multiple_of((i + 3) * 16, 8)
+            pad[pl.ds(p, 8), :] = hw[pl.ds(r, 8), :]
+            pad[pl.ds(p + 104, 8), :] = he[pl.ds(r + 8, 8), :]
+            for side, taps, shift, col in ((hw, (0, 1, 2), 5, 0), (he, (4, 5, 6), -3, 88)):
+                parts = []
+                for a in range(7):
+                    row = i + a
+                    inside = jnp.logical_and(row >= 3, row < TS + 3).astype(F32)
+                    v = [
+                        kb[7 * a + b] * side[pl.ds(row * 16 + b + shift, 8), :] for b in taps
+                    ]
+                    parts.append(((v[0] + v[1]) + v[2]) * inside)
+                o = pl.ds(pl.multiple_of(i * TS + col, 8), 8)
+                cells[o, :] = cells[o, :] + tree(parts)
+        return carry
+
+    lax.fori_loop(0, TS // 4, sides, 0)
     fetch[1].wait()
 
+    def first_half(here):
+        rm = rmet[:, here]
+        conv = cells[here, :].T * rm
+        centred = conv - jnp.mean(conv, axis=0, keepdims=True)
+        inv_std = lax.rsqrt(jnp.mean(centred * centred, axis=0, keepdims=True) + EPS)
+        normed = centred * inv_std
+        normed_bf = (normed * wide2(gain[...])).astype(BF16)
+        ms = wet[:, here] * wide2(scale[...])
+        gm = (ms * cot[:, here].astype(F32)).astype(BF16)
+        hidden = mm(w_in_t[...], normed_bf) + wide2(bias[...])
+        grad_active = mm(w_out[...], gm)
+        return rm, inv_std, normed, normed_bf, ms, gm, hidden, grad_active
+
+    def second_half(here, rm, inv_std, normed, normed_bf, ms, gm, hidden, grad_active):
+        sq = hidden * hidden
+        t = jnp.tanh(hidden * (GELU_COEF + (GELU_COEF * CUBIC) * sq))
+        p = 0.5 + 0.5 * t
+        active = hidden * p
+        slope = p + active * (1.0 - p) * (2.0 * GELU_COEF + (6.0 * GELU_COEF * CUBIC) * sq)
+        active_bf = active.astype(BF16)
+        gh = (grad_active * slope).astype(BF16)
+        mixed = mm(w_out_t[...], active_bf)
+        updated[:, here] = (feat[:, here].astype(F32) + ms * mixed).astype(BF16)
+        gn = mm(w_in[...], gh) * wide2(gain[...])
+        gc = inv_std * (
+            gn
+            - jnp.mean(gn, axis=0, keepdims=True)
+            - normed * jnp.mean(gn * normed, axis=0, keepdims=True)
+        )
+        gwo[...] += nt(gm, active_bf)
+        gwi[...] += nt(normed_bf, gh)
+        return (gc * rm).T.astype(BF16).astype(F32)
+
     def mlp_block(step, carry):
+        at = [
+            pl.ds(pl.multiple_of(step * BLOCK + c * CHUNK, CHUNK), CHUNK)
+            for c in range(BLOCK // CHUNK)
+        ]
+        ahead = first_half(at[0])
         for c in range(BLOCK // CHUNK):
-            here = pl.ds(pl.multiple_of(step * BLOCK + c * CHUNK, CHUNK), CHUNK)
-            rm = rmet[:, here]
-            conv = cells[here, :].T * rm
-            centred = conv - jnp.mean(conv, axis=0, keepdims=True)
-            inv_std = lax.rsqrt(jnp.mean(centred * centred, axis=0, keepdims=True) + EPS)
-            normed = centred * inv_std
-            g2 = wide2(gain[...])
-            normed_bf = (normed * g2).astype(BF16)
-            hidden = mm(w_in_t[...], normed_bf) + wide2(bias[...])
-            sq = hidden * hidden
-            t = jnp.tanh(hidden * (GELU_COEF + (GELU_COEF * CUBIC) * sq))
-            p = 0.5 + 0.5 * t
-            active = hidden * p
-            active_bf = active.astype(BF16)
-            mixed = mm(w_out_t[...], active_bf)
-            ms = wet[:, here] * wide2(scale[...])
-            updated[:, here] = (feat[:, here].astype(F32) + ms * mixed).astype(BF16)
-            gm = (ms * cot[:, here].astype(F32)).astype(BF16)
-            slope = p + active * (1.0 - p) * (2.0 * GELU_COEF + (6.0 * GELU_COEF * CUBIC) * sq)
-            gh = (mm(w_out[...], gm) * slope).astype(BF16)
-            gn = mm(w_in[...], gh) * g2
-            gwo[...] += nt(gm, active_bf)
-            gwi[...] += nt(normed_bf, gh)
-            gc = inv_std * (
-                gn
-                - jnp.mean(gn, axis=0, keepdims=True)
-                - normed * jnp.mean(gn * normed, axis=0, keepdims=True)
-            )
-            gs = (gc * rm).T.astype(BF16).astype(F32)
-            for r in range(8):
+            now = ahead
+            if c + 1 < BLOCK // CHUNK:
+                ahead = first_half(at[c + 1])
+            gs = second_half(at[c], *now)
+            for r in range(BLOCK // TS):
                 low, high = max(c * CHUNK, r * TS), min((c + 1) * CHUNK, (r + 1) * TS)
                 if low < high:
-                    o = pl.multiple_of((step * 8 + r + 3) * PITCH + 8 + low - r * TS, 8)
+                    row = step * (BLOCK // TS) + r + 3
+                    o = pl.multiple_of(row * PITCH + 8 + low - r * TS, 8)
                     gp[pl.ds(o, high - low), :] = gs[low - c * CHUNK : high - c * CHUNK]
         return carry
 
     lax.fori_loop(0, CELLS // BLOCK, mlp_block, 0)
-    out_updated = pltpu.make_async_copy(updated, updated_hbm, up_sem)
+    out_updated = pltpu.make_async_copy(updated, updated_hbm.at[0], up_sem)
     out_updated.start()
+
+    for k in range(4):
+        here = slice(k * C, (k + 1) * C)
+        wmine[here, :] = (gwi[:, here] * GRAD_SCALE).astype(BF16)
+        wmine[HID + k * C : HID + (k + 1) * C, :] = (gwo[:, here] * GRAD_SCALE).astype(BF16)
+    stage1 = []
+    for k, v in z_peers:
+        src = wmine.at[pl.ds(pl.multiple_of(v * C, C), C)]
+        stage1.append(send(src, part8.at[k], s1.at[k], r1.at[k], (n, x * 8 + v)))
 
     def frame_rows(jb, carry):
         j0 = pl.multiple_of(jb * 8, 8)
         for f, p in enumerate((0, 1, 2, 99, 100, 101)):
-            total = None
+            parts = []
             for a in range(7):
                 if 0 <= p - a < TS:
-                    for b in range(7):
-                        v = kb[7 * a + b] * gp[pl.ds((p - a + 3) * PITCH + j0 + 8 - b, 8), :]
-                        total = v if total is None else total + v
-            frame[f, pl.ds(j0, 8), :] = total
+                    parts += [
+                        kb[7 * a + b] * gp[pl.ds((p - a + 3) * PITCH + j0 + 8 - b, 8), :]
+                        for b in range(7)
+                    ]
+            frame[f, pl.ds(j0, 8), :] = tree(parts)
         return carry
 
     lax.fori_loop(0, 13, frame_rows, 0)
 
-    def frame_cols(i, carry):
-        p = i + 3
-        for side, taps, q0 in ((fw, (0, 1, 2), 0), (fe, (4, 5, 6), 96)):
-            total = None
-            for a in range(7):
-                for b in taps:
-                    v = kb[7 * a + b] * gp[pl.ds((p - a + 3) * PITCH + q0 + 8 - b, 8), :]
-                    total = v if total is None else total + v
-            side[pl.ds(pl.multiple_of(p * 8, 8), 8), :] = total
-        return carry
-
-    lax.fori_loop(0, TS, frame_cols, 0)
+    def frame_cols(g, carry):
+        for e in range(4):
+            p = g * 4 + e + 3
+            for side, taps, q0 in ((fw, (0, 1, 2), 0), (fe, (4, 5, 6), 96)):
+                parts = [
+                    kb[7 * a + b] * gp[pl.ds((p - a + 3) * PITCH + q0 + 8 - b, 8), :]
+                    for a in range(7)
+                    for b in taps
+                ]
+                side[pl.ds(pl.multiple_of(p * 8, 8), 8), :] = tree(parts)
+        return carry
+
+    lax.fori_loop(0, TS // 4, frame_cols, 0)
     for f, p in enumerate((0, 1, 2, 99, 100, 101)):
         fw[p * 8 : p * 8 + 8, :] = frame[f, 0:8, :]
         fe[p * 8 : p * 8 + 8, :] = frame[f, 96:104, :]
@@ -430,59 +469,64 @@
         acc = lax.fori_loop(0, 24, taps, (zero,) * 7)
         for a in range(7):
             t = 7 * a + b
-            row = (t // 2) * 16 + lax.rem(t, 2)
-            kx[pl.ds(row, 1), :] = jnp.sum(acc[a], axis=0, keepdims=True)
+            kx[pl.ds(t, 1), :] = jnp.sum(acc[a], axis=0, keepdims=True)
         return carry
 
     lax.fori_loop(0, 7, tap_column, 0)
 
-    for c in range(32):
-        acc = gwi if c < 16 else gwo
-        part = acc[(c % 4) * 32 : (c % 4 + 1) * 32, (c // 4 % 4) * C : (c // 4 % 4 + 1) * C]
-        wmine[c * 48 : c * 48 + 32, :] = (part * GRAD_SCALE).astype(BF16)
-        wmine[c * 48 + 32 : c * 48 + 48, :] = (kx[c * 16 : c * 16 + 16, :] * GRAD_SCALE).astype(BF16)
-    stage = []
+    kmine[...] = (kx[...] * GRAD_SCALE).astype(BF16)
+    kz[z] = kmine[...]
+    kstage = []
     for k, v in z_peers:
-        src = wmine.at[pl.ds(pl.multiple_of(v * 192, 64), 192)]
-        stage.append(send(src, part8.at[k], s1.at[k], r1.at[k], (n, x * 8 + v)))
-    clear_rows(cells)
-    taps_columns(gp, kb, cells, True, 0, 2)
-    for copy in stage:
-        copy.wait()
-    total = wmine[pl.ds(pl.multiple_of(z * 192, 64), 192), :].astype(F32)
+        kstage.append(send(kmine, kz.at[z], s6.at[k], r6.at[k], (n, x * 8 + v)))
+    for copy in stage1:
+        copy.wait()
+    total = wmine[pl.ds(pl.multiple_of(z * C, C), C), :].astype(F32)
     for k in range(1, 8):
         total = total + part8[k].astype(F32)
     mine4[...] = total
-    stage = []
+    stage2 = []
     for k, v in x_peers:
-        src = mine4.at[pl.ds(pl.multiple_of(v * 48, 16), 48)]
-        stage.append(send(src, part4.at[k], s2.at[k], r2.at[k], (n, v * 8 + z)))
-    taps_columns(gp, kb, cells, True, 2, 3)
-    for copy in stage:
-        copy.wait()
-    total = mine4[pl.ds(pl.multiple_of(x * 48, 16), 48), :]
+        src = mine4.at[pl.ds(pl.multiple_of(v * 32, 32), 32)]
+        stage2.append(send(src, part4.at[k], s2.at[k], r2.at[k], (n, v * 8 + z)))
+    clear_rows(cells)
+    taps_columns(gp, kb, cells, True, 0, 2)
+    for copy in stage2 + kstage:
+        copy.wait()
+    total = mine4[pl.ds(pl.multiple_of(x * 32, 32), 32), :]
     for k in range(1, 4):
         total = total + part4[k]
     nodes[n] = total
-    stage = []
+    stage3 = []
     for k, v in n_peers:
-        stage.append(send(nodes.at[n], nodes.at[n], s3.at[k], r3.at[k], (v, w)))
-    taps_columns(gp, kb, cells, True, 3, 4)
-    for copy in stage:
+        stage3.append(send(nodes.at[n], nodes.at[n], s3.at[k], r3.at[k], (v, w)))
+    total = kz[0].astype(F32)
+    for v in range(1, 8):
+        total = total + kz[v].astype(F32)
+    kq[x] = total
+    kstage = []
+    for k, v in x_peers:
+        kstage.append(send(kq.at[x], kq.at[x], s7.at[k], r7.at[k], (n, v * 8 + z)))
+    taps_columns(gp, kb, cells, True, 2, 4)
+    for copy in stage3 + kstage:
         copy.wait()
     all4[x] = ((nodes[0] + nodes[1]) + (nodes[2] + nodes[3])).astype(BF16)
-    stage = []
+    stage4 = []
     for k, v in x_peers:
-        stage.append(send(all4.at[x], all4.at[x], s4.at[k], r4.at[k], (n, v * 8 + z)))
-    taps_columns(gp, kb, cells, True, 4, 5)
-    for copy in stage:
+        stage4.append(send(all4.at[x], all4.at[x], s4.at[k], r4.at[k], (n, v * 8 + z)))
+    kn[n] = (kq[0] + kq[1]) + (kq[2] + kq[3])
+    kstage = []
+    for k, v in n_peers:
+        kstage.append(send(kn.at[n], kn.at[n], s8.at[k], r8.at[k], (v, w)))
+    taps_columns(gp, kb, cells, True, 4, 6)
+    for copy in stage4:
         copy.wait()
     for v in range(4):
-        wall[z, v * 48 : (v + 1) * 48, :] = all4[v]
-    stage = []
+        wall[z, v * 32 : (v + 1) * 32, :] = all4[v]
+    stage5 = []
     for k, v in z_peers:
-        stage.append(send(wall.at[z], wall.at[z], s5.at[k], r5.at[k], (n, x * 8 + v)))
-    taps_columns(gp, kb, cells, True, 5, 7)
+        stage5.append(send(wall.at[z], wall.at[z], s5.at[k], r5.at[k], (n, x * 8 + v)))
+    taps_columns(gp, kb, cells, True, 6, 7)
     for copy in borders:
         copy.wait()
 
@@ -508,8 +552,8 @@
         cells[(93 + q) * TS : (94 + q) * TS, :] += jnp.where(present[0], north, 0.0)
 
     def finish(step, carry):
-        for r in range(8):
-            i = step * 8 + r
+        for r in range(BLOCK // TS):
+            i = step * (BLOCK // TS) + r
             o = pl.multiple_of(i * TS, 8)
             row = pl.multiple_of(i * 8, 8)
             cells[pl.ds(o, 8), :] += cw[pl.ds(row, 8), :]
@@ -520,25 +564,17 @@
         return carry
 
     lax.fori_loop(0, CELLS // BLOCK, finish, 0)
-    out_grad = pltpu.make_async_copy(grad, grad_hbm, gr_sem)
+    out_grad = pltpu.make_async_copy(grad, grad_hbm.at[0], gr_sem)
     out_grad.start()
-    for copy in stage:
-        copy.wait()
-    for c in range(32):
-        rows = slice((c % 4) * 48, (c % 4) * 48 + 32)
-        if c < 16:
-            g_in[(c % 4) * 32 : (c % 4 + 1) * 32, (c // 4) * C : (c // 4 + 1) * C] = wall[
-                c // 4, rows, :
-            ].astype(F32)
-        elif c % 4 == 0:
-            block = jnp.concatenate(
-                [wall[c // 4, v * 48 : v * 48 + 32, :] for v in range(4)], axis=0
-            )
-            g_out[(c // 4 - 4) * C : (c // 4 - 3) * C, :] = block.astype(F32).T
-        if c < 25:
-            size = min(2, 49 - 2 * c)
-            pair = wall[c // 4, (c % 4) * 48 + 32 : (c % 4) * 48 + 48, :].astype(F32)
-            ksum[2 * c : 2 * c + size, :] = pair[0:size]
+    for copy in kstage:
+        copy.wait()
+    ksum[...] = ((kn[0] + kn[1]) + (kn[2] + kn[3]))[0:49, :]
+    for copy in stage5:
+        copy.wait()
+    for k in range(4):
+        here = slice(k * C, (k + 1) * C)
+        g_in[:, here] = wall[k].astype(F32)
+        g_out[here, :] = wall[4 + k].astype(F32).T
     out_updated.wait()
     out_grad.wait()
 
@@ -559,16 +595,17 @@
         ((C, HID), F32), ((C, HID), F32),
         ((6, 104, C), F32), ((PITCH * 8, C), F32), ((PITCH * 8, C), F32),
         ((6, BAND, C), BF16), ((15, BAND, C), BF16), ((TS * 8, C), F32), ((TS * 8, C), F32),
-        ((512, C), F32), ((1536, C), BF16), ((8, 192, C), BF16), ((192, C), F32),
-        ((4, 48, C), F32), ((4, 48, C), F32), ((4, 48, C), BF16), ((8, 192, C), BF16),
+        ((8 * C, C), BF16), ((8, C, C), BF16), ((C, C), F32), ((4, 32, C), F32),
+        ((4, 32, C), F32), ((4, 32, C), BF16), ((8, C, C), BF16),
+        ((64, C), F32), ((64, C), BF16), ((8, 64, C), BF16), ((4, 64, C), F32), ((4, 64, C), F32),
     ]
     sems = [dma((2,)), dma, dma, dma((15,)), dma((15,)), dma((15,)), dma((15,))]
-    sems += [dma((8,)), dma((8,))] + [dma((4,))] * 6 + [dma((8,)), dma((8,))]
+    sems += [dma((8,)), dma((8,))] + [dma((4,))] * 6 + [dma((8,))] * 4 + [dma((4,))] * 4
     return pl.pallas_call(
         block_kernel,
         out_shape=(
-            jax.ShapeDtypeStruct((C, CELLS), BF16),
-            jax.ShapeDtypeStruct((C, CELLS), BF16),
+            jax.ShapeDtypeStruct((1, C, CELLS), BF16),
+            jax.ShapeDtypeStruct((1, C, CELLS), BF16),
             jax.ShapeDtypeStruct((C, HID), F32),
             jax.ShapeDtypeStruct((HID, C), F32),
             jax.ShapeDtypeStruct((49, C), F32),
@@ -596,9 +633,9 @@
     weight_out,
     layer_scale,
 ):
-    updated, grad_features, grad_in, grad_out, grad_kernel = block_call(
-        features.reshape(C, CELLS),
-        cotangent.reshape(C, CELLS),
+    return block_call(
+        features,
+        cotangent,
         wet_fraction,
         kernel,
         slot_tile,
@@ -609,13 +646,6 @@
         weight_out,
         layer_scale[None, :],
     )
-    return (
-        updated.reshape(1, C, CELLS),
-        grad_features.reshape(1, C, CELLS),
-        grad_in,
-        grad_out,
-        grad_kernel,
-    )
 
 
 def solution(mesh):

time: 119 us -> 105 us (0.88)
  Pallas kernels: 109 us -> 95.7 us
    pallas_call x1, Pallas kernels: 109 us -> 95.7 us  [block_call(): pl.pallas_call(block_kernel, out_shape=(jax.ShapeDtypeStruct((1, C, CELLS...]
where the time goes in v4:
time: 105 us
  Pallas kernels  95.7 us (91%)
  local copies, waits for them, and re-layouts  8.34 us (8%)
    pallas_call x1, Pallas kernels, block_call(): pl.pallas_call(block_kernel, out_shape=(jax.ShapeDtypeStruct((1, C, CELLS...  95.7 us
    unnamed x14, local copies, waits for them, and re-layouts  7.63 us

profile of v4, /device:TPU:1, one launch (start us, length us, event | category | flops | bytes accessed | tf_op | source)
XLA Modules:
  0.0 104.7 jit_solution(7954772459669955202)
XLA Ops:
  0.6 0.8 copy.16
  1.5 0.7 reshape.13.neighbours
  2.2 95.7 %block.1 = (bf16[1,128,9216]{2,1,0:T(8,128)(2,1)}, bf16[1,128,9216]{2,1,0:T(8,128)(2,1)}, f32[128,512]{1,0:T(8,128)}, f32[512,128]{1,0:T(8,128)}, f32[49,128]{1,0:T(8,128)}) custom-call(bf16[1,128,9216]{2,1,0:T(8,128)(2,1)} %feat_hbm.1, bf16[1,128,9216]{2,1,0:T(8,128)(2,1)} %cot_hbm.1, f32[1,9216]{1,0:T(1,128)} %wet.1, f32[49,128]{1,0:T(8,128)} %k49.1, ...), custom_call_target="tpu_custom_call" | custom-call | tf_op jit(solution)/shard_map/block/pallas_call | solution.py:604
  97.9 0.0 copy-start
  97.9 3.4 %copy.22 = bf16[1,128,9216]{2,1,0:T(8,128)(2,1)} copy(bf16[1,128,9216]{2,1,0:T(8,128)(2,1)} %get-tuple-element.10) | data formatting | bytes 4718592
  101.3 0.0 copy-done
  101.3 0.0 copy-start.2
  101.3 0.0 copy-start.1
  101.3 0.0 copy-start.3
  101.3 1.4 %copy.23 = bf16[1,128,9216]{2,1,0:T(8,128)(2,1)} copy(bf16[1,128,9216]{2,1,0:T(8,128)(2,1)S(1)} %copy-done) | data formatting | bytes 4718592
  102.7 0.0 copy-done.2
  102.7 0.7 copy.24
  103.4 0.0 copy-done.1
  103.4 0.7 copy.25
  104.1 0.0 copy-done.3
  104.1 0.6 copy.26
Async XLA Ops:
  97.9 3.4 %copy-start = (bf16[1,128,9216]{2,1,0:T(8,128)(2,1)S(1)}, bf16[1,128,9216]{2,1,0:T(8,128)(2,1)}, u32[]{:S(2)}) copy-start(bf16[1,128,9216]{2,1,0:T(8,128)(2,1)} %get-tuple-element.11) | copy-start | bytes 7077892
  101.3 1.4 %copy-start.2 = (f32[128,512]{1,0:T(8,128)S(1)}, f32[128,512]{1,0:T(8,128)}, u32[]{:S(2)}) copy-start(f32[128,512]{1,0:T(8,128)} %get-tuple-element.12) | copy-start | bytes 786436
  101.3 2.1 %copy-start.1 = (f32[512,128]{1,0:T(8,128)S(1)}, f32[512,128]{1,0:T(8,128)}, u32[]{:S(2)}) copy-start(f32[512,128]{1,0:T(8,128)} %get-tuple-element.13) | copy-start | bytes 786436
  101.3 2.8 %copy-start.3 = (f32[49,128]{1,0:T(8,128)S(1)}, f32[49,128]{1,0:T(8,128)}, u32[]{:S(2)}) copy-start(f32[49,128]{1,0:T(8,128)} %get-tuple-element.14) | copy-start | bytes 75268

commit v5 on v4

--- a/solution.py
+++ b/solution.py
@@ -133,7 +133,7 @@
         return slot
 
     for d in range(8):
-        near = jnp.where(tile >= 0, neighbours[known * 8 + d], -1)
+        near = jnp.where(tile >= 0, neighbours[d, known], -1)
         present.append(near >= 0)
         targets.append(jnp.maximum(near, 0) >> 1)
         slots.append(find(bases[d], targets[d]))
@@ -620,6 +620,41 @@
     )(*args)
 
 
+def hand_over_kernel(*refs):
+    sources, results, held = refs[:5], refs[5:10], refs[10:15]
+    in_sem, out_sem = refs[15:]
+    pieces = []
+    for source, result, stage in zip(sources[:2], results[:2], held[:2]):
+        for k in range(4):
+            here = pl.ds(k * 32, 32)
+            pieces.append((source.at[0, here], stage.at[here], result.at[0, here]))
+    pieces += [(a, b, c) for a, b, c in zip(sources[2:], held[2:], results[2:])]
+    loads = [pltpu.make_async_copy(a, b, in_sem.at[k]) for k, (a, b, _) in enumerate(pieces)]
+    stores = [pltpu.make_async_copy(b, c, out_sem.at[k]) for k, (_, b, c) in enumerate(pieces)]
+    for copy in loads:
+        copy.start()
+    for load, store in zip(loads, stores):
+        load.wait()
+        store.start()
+    for copy in stores:
+        copy.wait()
+
+
+def hand_over(*arrays):
+    hbm = pl.BlockSpec(memory_space=pl.ANY)
+    held = [pltpu.VMEM((C, CELLS), BF16)] * 2
+    held += [pltpu.VMEM(a.shape, a.dtype) for a in arrays[2:]]
+    return pl.pallas_call(
+        hand_over_kernel,
+        out_shape=tuple(jax.ShapeDtypeStruct(a.shape, a.dtype) for a in arrays),
+        in_specs=[hbm] * 5,
+        out_specs=(hbm,) * 5,
+        scratch_shapes=held + [pltpu.SemaphoreType.DMA((11,))] * 2,
+        compiler_params=pltpu.CompilerParams(vmem_limit_bytes=VMEM_LIMIT),
+        name="hand_over",
+    )(*arrays)
+
+
 def local(
     features,
     cotangent,
@@ -633,19 +668,20 @@
     weight_out,
     layer_scale,
 ):
-    return block_call(
+    results = block_call(
         features,
         cotangent,
         wet_fraction,
         kernel,
         slot_tile,
-        neighbours.reshape(-1),
+        neighbours.T,
         norm_gain[None, :],
         weight_in,
         bias_in[None, :],
         weight_out,
         layer_scale[None, :],
     )
+    return hand_over(*results)
 
 
 def solution(mesh):

time: 105 us -> 101 us (0.962)
  local copies, waits for them, and re-layouts: 8.34 us -> 0 us
  Pallas kernels: 95.7 us -> 100 us
    unnamed x14 -> x0, local copies, waits for them, and re-layouts: 7.63 us -> none
    pallas_call x0 -> x1, Pallas kernels: none -> 4.58 us  [hand_over(): pl.pallas_call(hand_over_kernel, out_shape=tuple((jax.ShapeDtypeStruct(a....]
where the time goes in v5:
time: 101 us
  Pallas kernels  100 us (99%)
    pallas_call x1, Pallas kernels, block_call(): pl.pallas_call(block_kernel, out_shape=(jax.ShapeDtypeStruct((1, C, CELLS...  95.8 us
    pallas_call x1, Pallas kernels, hand_over(): pl.pallas_call(hand_over_kernel, out_shape=tuple((jax.ShapeDtypeStruct(a....  4.58 us

profile of v5, /device:TPU:1, one launch (start us, length us, event | category | flops | bytes accessed | tf_op | source)
XLA Modules:
  0.0 101.0 jit_solution(4358726390328626243)
XLA Ops:
  0.6 95.8 %block.1 = (bf16[1,128,9216]{2,1,0:T(8,128)(2,1)}, bf16[1,128,9216]{2,1,0:T(8,128)(2,1)}, f32[128,512]{1,0:T(8,128)}, f32[512,128]{1,0:T(8,128)}, f32[49,128]{1,0:T(8,128)}) custom-call(bf16[1,128,9216]{2,1,0:T(8,128)(2,1)} %feat_hbm.1, bf16[1,128,9216]{2,1,0:T(8,128)(2,1)} %cot_hbm.1, f32[1,9216]{1,0:T(1,128)} %wet.1, f32[49,128]{1,0:T(8,128)} %k49.1, ...), custom_call_target="tpu_custom_call" | custom-call | tf_op jit(solution)/shard_map/block/pallas_call | solution.py:604
  96.4 4.6 %hand_over.1 = (bf16[1,128,9216]{2,1,0:T(8,128)(2,1)}, bf16[1,128,9216]{2,1,0:T(8,128)(2,1)}, f32[128,512]{1,0:T(8,128)}, f32[512,128]{1,0:T(8,128)}, f32[49,128]{1,0:T(8,128)}) custom-call(bf16[1,128,9216]{2,1,0:T(8,128)(2,1)} %get-tuple-element.10.refs_0_, bf16[1,128,9216]{2,1,0:T(8,128)(2,1)} %get-tuple-element.11.refs_1_, ...), custom_call_target="tpu_custom_call" | custom-call | tf_op jit(solution)/shard_map/hand_over/pallas_call | solution.py:647

commit v6 on v5

--- a/solution.py
+++ b/solution.py
@@ -17,7 +17,7 @@
 PADROWS = TS + 6
 STRIP = 3 * TS
 BAND = 3 * PITCH
-BLOCK = 1536
+BLOCK = 2304
 CHUNK = 256
 EPS = 1e-06
 GELU_COEF = 0.7978845608028654
@@ -46,22 +46,35 @@
 
 
 def taps_columns(src, kb, out, flip, low, high):
-    def body(it, carry):
-        b = it // 12
-        i0 = lax.rem(it, 12) * 8
-        taps = [kb[48 - 7 * a - b] if flip else kb[7 * a + b] for a in range(7)]
-        for jb in range(12):
-            base = i0 * PITCH + 8 * jb + 5 + b
-            v = [src[pl.ds(base + r * PITCH, 8), :] for r in range(14)]
-            for d in range(8):
-                total = taps[0] * v[d]
-                for a in range(1, 7):
-                    total = total + taps[a] * v[d + a]
-                o = pl.ds(pl.multiple_of((i0 + d) * TS + 8 * jb, 8), 8)
-                out[o, :] = out[o, :] + total
-        return carry
-
-    lax.fori_loop(low * 12, high * 12, body, 0)
+    def passes(columns):
+        def body(it, carry):
+            b0 = low + columns * (it // 12)
+            i0 = lax.rem(it, 12) * 8
+            taps = [
+                [kb[48 - 7 * a - b0 - e] if flip else kb[7 * a + b0 + e] for a in range(7)]
+                for e in range(columns)
+            ]
+            for jb in range(12):
+                base = i0 * PITCH + 8 * jb + 5 + b0
+                totals = [None] * 8
+                for e in range(columns):
+                    v = [src[pl.ds(base + e + r * PITCH, 8), :] for r in range(14)]
+                    for d in range(8):
+                        for a in range(7):
+                            p = taps[e][a] * v[d + a]
+                            totals[d] = p if totals[d] is None else totals[d] + p
+                for d in range(8):
+                    o = pl.ds(pl.multiple_of((i0 + d) * TS + 8 * jb, 8), 8)
+                    out[o, :] = out[o, :] + totals[d]
+            return carry
+
+        return body
+
+    if (high - low) % 2:
+        lax.fori_loop(0, 12, passes(1), 0)
+        low += 1
+    if high > low:
+        lax.fori_loop(0, (high - low) // 2 * 12, passes(2), 0)
 
 
 def clear_rows(out):
@@ -151,7 +164,7 @@
     feat_hbm, cot_hbm, wet, k49, slot_tile, neighbours, gain_row, w_in, bias_row, w_out, scale_row,
     updated_hbm, grad_hbm, g_in, g_out, ksum,
     feat, cot, updated, grad, wc, rmet, pad, gp, cells, kb, strips, got, hw, he, hs, hn, strip,
-    gain, scale, bias, w_in_t, w_out_t, gwi, gwo, frame, fw, fe, back_strips, back_got, cw, ce,
+    gain, scale, ones, w_in_t, w_out_t, w_out_half, gwi, gwo, frame, fw, fe, back_strips, back_got, cw, ce,
     wmine, part8, mine4, part4, nodes, all4, wall, kx, kmine, kz, kq, kn,
     in_sem, up_sem, gr_sem, fsend, frecv, bsend, brecv, s1, r1, s2, r2, s3, r3, s4, r4, s5, r5,
     s6, r6, s7, r7, s8, r8,
@@ -244,12 +257,21 @@
     send_strips((3, 4))
 
     taps_columns(pad, kb, cells, False, 0, 7)
+    ones[...] = jnp.ones((C, CHUNK), BF16)
+    column = lax.broadcasted_iota(jnp.int32, (C, C), 1)
     gain[...] = jnp.broadcast_to(gain_row[...], (C, C)).T
     scale[...] = jnp.broadcast_to(scale_row[...], (C, C)).T
     for k in range(4):
         here = slice(k * C, (k + 1) * C)
-        bias[here, :] = jnp.broadcast_to(bias_row[:, here], (C, C)).T
-        w_in_t[here, :] = w_in[:, here].astype(F32).T.astype(BF16)
+        w_in_t[here, 0:C] = (0.5 * w_in[:, here].astype(F32).T).astype(BF16)
+        w_out_half[here, :] = (0.5 * w_out[here, :].astype(F32)).astype(BF16)
+        rest = 0.5 * jnp.broadcast_to(bias_row[:, here], (C, C)).T
+        parts = jnp.zeros((C, C), F32)
+        for part in range(3):
+            now = rest.astype(BF16).astype(F32)
+            parts = jnp.where(column == part, now, parts)
+            rest = rest - now
+        w_in_t[here, C : 2 * C] = parts.astype(BF16)
         w_out_t[:, here] = w_out[here, :].astype(F32).T.astype(BF16)
     gwi[...] = jnp.zeros_like(gwi)
     gwo[...] = jnp.zeros_like(gwo)
@@ -339,29 +361,30 @@
         normed_bf = (normed * wide2(gain[...])).astype(BF16)
         ms = wet[:, here] * wide2(scale[...])
         gm = (ms * cot[:, here].astype(F32)).astype(BF16)
-        hidden = mm(w_in_t[...], normed_bf) + wide2(bias[...])
-        grad_active = mm(w_out[...], gm)
-        return rm, inv_std, normed, normed_bf, ms, gm, hidden, grad_active
-
-    def second_half(here, rm, inv_std, normed, normed_bf, ms, gm, hidden, grad_active):
-        sq = hidden * hidden
-        t = jnp.tanh(hidden * (GELU_COEF + (GELU_COEF * CUBIC) * sq))
-        p = 0.5 + 0.5 * t
-        active = hidden * p
-        slope = p + active * (1.0 - p) * (2.0 * GELU_COEF + (6.0 * GELU_COEF * CUBIC) * sq)
+        half = mm(w_in_t[...], jnp.concatenate([normed_bf, ones[...]], axis=0))
+        half_grad = mm(w_out_half[...], gm)
+        return rm, inv_std, normed, normed_bf, ms, gm, half, half_grad
+
+    def second_half(here, rm, inv_std, normed, normed_bf, ms, gm, half, half_grad):
+        sq = half * half
+        t = jnp.tanh(half * (2.0 * GELU_COEF + (8.0 * GELU_COEF * CUBIC) * sq))
+        one_more = 1.0 + t
+        active = half * one_more
+        slope = (2.0 * GELU_COEF) + (24.0 * GELU_COEF * CUBIC) * sq
+        slope = one_more + active * (1.0 - t) * slope
         active_bf = active.astype(BF16)
-        gh = (grad_active * slope).astype(BF16)
+        gh = (half_grad * slope).astype(BF16)
         mixed = mm(w_out_t[...], active_bf)
         updated[:, here] = (feat[:, here].astype(F32) + ms * mixed).astype(BF16)
         gn = mm(w_in[...], gh) * wide2(gain[...])
-        gc = inv_std * (
+        gc = (inv_std * rm) * (
             gn
             - jnp.mean(gn, axis=0, keepdims=True)
             - normed * jnp.mean(gn * normed, axis=0, keepdims=True)
         )
         gwo[...] += nt(gm, active_bf)
         gwi[...] += nt(normed_bf, gh)
-        return (gc * rm).T.astype(BF16).astype(F32)
+        return gc.T.astype(BF16).astype(F32)
 
     def mlp_block(step, carry):
         at = [
@@ -591,7 +614,8 @@
         ((49, 8, C), F32), ((6, STRIP, C), BF16), ((15, STRIP, C), BF16),
         ((PADROWS * 16, C), F32), ((PADROWS * 16, C), F32), ((BAND, C), F32), ((BAND, C), F32),
         ((3 * PITCH, C), F32),
-        ((C, C), F32), ((C, C), F32), ((HID, C), F32), ((HID, C), BF16), ((C, HID), BF16),
+        ((C, C), F32), ((C, C), F32), ((C, CHUNK), BF16), ((HID, 2 * C), BF16), ((C, HID), BF16),
+        ((HID, C), BF16),
         ((C, HID), F32), ((C, HID), F32),
         ((6, 104, C), F32), ((PITCH * 8, C), F32), ((PITCH * 8, C), F32),
         ((6, BAND, C), BF16), ((15, BAND, C), BF16), ((TS * 8, C), F32), ((TS * 8, C), F32),

time: 101 us -> 98 us (0.970)
  Pallas kernels: 100 us -> 97.2 us
    pallas_call x1, Pallas kernels: 95.8 us -> 92.6 us  [block_call(): pl.pallas_call(block_kernel, out_shape=(jax.ShapeDtypeStruct((1, C, CELLS...]
where the time goes in v6:
time: 98 us; the launch traced here: 97.8 us
  Pallas kernels  97.2 us (99%)
    pallas_call x1, Pallas kernels, block_call(): pl.pallas_call(block_kernel, out_shape=(jax.ShapeDtypeStruct((1, C, CELLS...  92.6 us
    pallas_call x1, Pallas kernels, hand_over(): pl.pallas_call(hand_over_kernel, out_shape=tuple((jax.ShapeDtypeStruct(a....  4.58 us

profile of v6, /device:TPU:1, one launch (start us, length us, event | category | flops | bytes accessed | tf_op | source)
XLA Modules:
  0.0 97.8 jit_solution(11988152321505197922)
XLA Ops:
  0.6 92.6 %block.1 = (bf16[1,128,9216]{2,1,0:T(8,128)(2,1)}, bf16[1,128,9216]{2,1,0:T(8,128)(2,1)}, f32[128,512]{1,0:T(8,128)}, f32[512,128]{1,0:T(8,128)}, f32[49,128]{1,0:T(8,128)}) custom-call(bf16[1,128,9216]{2,1,0:T(8,128)(2,1)} %feat_hbm.1, bf16[1,128,9216]{2,1,0:T(8,128)(2,1)} %cot_hbm.1, f32[1,9216]{1,0:T(1,128)} %wet.1, f32[49,128]{1,0:T(8,128)} %k49.1, ...), custom_call_target="tpu_custom_call" | custom-call | tf_op jit(solution)/shard_map/block/pallas_call | solution.py:628
  93.3 4.6 %hand_over.1 = (bf16[1,128,9216]{2,1,0:T(8,128)(2,1)}, bf16[1,128,9216]{2,1,0:T(8,128)(2,1)}, f32[128,512]{1,0:T(8,128)}, f32[512,128]{1,0:T(8,128)}, f32[49,128]{1,0:T(8,128)}) custom-call(bf16[1,128,9216]{2,1,0:T(8,128)(2,1)} %get-tuple-element.10.refs_0_, bf16[1,128,9216]{2,1,0:T(8,128)(2,1)} %get-tuple-element.11.refs_1_, ...), custom_call_target="tpu_custom_call" | custom-call | tf_op jit(solution)/shard_map/hand_over/pallas_call | solution.py:671

commit v7 on v6

--- a/solution.py
+++ b/solution.py
@@ -591,7 +591,7 @@
     out_grad.start()
     for copy in kstage:
         copy.wait()
-    ksum[...] = ((kn[0] + kn[1]) + (kn[2] + kn[3]))[0:49, :]
+    ksum[...] = ((kn[0] + kn[1]) + (kn[2] + kn[3]))[0:56, :]
     for copy in stage5:
         copy.wait()
     for k in range(4):
@@ -612,7 +612,7 @@
         ((1, CELLS), F32), ((1, CELLS), F32),
         ((PADROWS * PITCH, C), F32), ((PADROWS * PITCH, C), F32), ((CELLS, C), F32),
         ((49, 8, C), F32), ((6, STRIP, C), BF16), ((15, STRIP, C), BF16),
-        ((PADROWS * 16, C), F32), ((PADROWS * 16, C), F32), ((BAND, C), F32), ((BAND, C), F32),
+        ((1680, C), F32), ((1680, C), F32), ((BAND, C), F32), ((BAND, C), F32),
         ((3 * PITCH, C), F32),
         ((C, C), F32), ((C, C), F32), ((C, CHUNK), BF16), ((HID, 2 * C), BF16), ((C, HID), BF16),
         ((HID, C), BF16),
@@ -632,7 +632,7 @@
             jax.ShapeDtypeStruct((1, C, CELLS), BF16),
             jax.ShapeDtypeStruct((C, HID), F32),
             jax.ShapeDtypeStruct((HID, C), F32),
-            jax.ShapeDtypeStruct((49, C), F32),
+            jax.ShapeDtypeStruct((56, C), F32),
         ),
         in_specs=[hbm, hbm, vmem, vmem, smem, smem] + [vmem] * 5,
         out_specs=(hbm, hbm, vmem, vmem, vmem),
@@ -705,7 +705,8 @@
         weight_out,
         layer_scale[None, :],
     )
-    return hand_over(*results)
+    results = hand_over(*results)
+    return (*results[:4], results[4][:49])
 
 
 def solution(mesh):

time: 98 us -> 98 us (level)
  no operation moved by 1% of the time
where the time goes in v7:
time: 98 us; the launch traced here: 97.9 us
  Pallas kernels  97.2 us (99%)
    pallas_call x1, Pallas kernels, block_call(): pl.pallas_call(block_kernel, out_shape=(jax.ShapeDtypeStruct((1, C, CELLS...  92.6 us
    pallas_call x1, Pallas kernels, hand_over(): pl.pallas_call(hand_over_kernel, out_shape=tuple((jax.ShapeDtypeStruct(a....  4.58 us

profile of v7, /device:TPU:1, one launch (start us, length us, event | category | flops | bytes accessed | tf_op | source)
XLA Modules:
  0.0 97.9 jit_solution(11037610303184056441)
XLA Ops:
  0.6 92.6 %block.1 = (bf16[1,128,9216]{2,1,0:T(8,128)(2,1)}, bf16[1,128,9216]{2,1,0:T(8,128)(2,1)}, f32[128,512]{1,0:T(8,128)}, f32[512,128]{1,0:T(8,128)}, f32[56,128]{1,0:T(8,128)}) custom-call(bf16[1,128,9216]{2,1,0:T(8,128)(2,1)} %feat_hbm.1, bf16[1,128,9216]{2,1,0:T(8,128)(2,1)} %cot_hbm.1, f32[1,9216]{1,0:T(1,128)} %wet.1, f32[49,128]{1,0:T(8,128)} %k49.1, ...), custom_call_target="tpu_custom_call" | custom-call | tf_op jit(solution)/shard_map/block/pallas_call | solution.py:628
  93.3 4.6 %hand_over.1 = (bf16[1,128,9216]{2,1,0:T(8,128)(2,1)}, bf16[1,128,9216]{2,1,0:T(8,128)(2,1)}, f32[128,512]{1,0:T(8,128)}, f32[512,128]{1,0:T(8,128)}, f32[56,128]{1,0:T(8,128)}) custom-call(bf16[1,128,9216]{2,1,0:T(8,128)(2,1)} %get-tuple-element.15.refs_0_, bf16[1,128,9216]{2,1,0:T(8,128)(2,1)} %get-tuple-element.16.refs_1_, ...), custom_call_target="tpu_custom_call" | custom-call | tf_op jit(solution)/shard_map/hand_over/pallas_call | solution.py:671
